TPU v7x, 256 devices: a whole 4x4x8 slice. The times are simulated.
256 devices in a mesh: blk: 256 (over x, y, z, core).
Axes of the slice: x: 4, y: 4, z: 8, core: 2. Of those that a mesh axis runs over, the one named last changes fastest.
Arguments:
- points: bfloat16 [262144, 128], P('blk'), may hold values from -6 to 6
- w_input: bfloat16 [128, 128], replicated, may hold values from -0.5 to 0.5
- w_output: bfloat16 [128, 128], replicated, may hold values from -0.5 to 0.5
- vectors: bfloat16 [17, 262144], P(None, 'blk'), may hold values from -0.5 to 0.5
- adjoint: bfloat16 [17, 262144], P(None, 'blk'), may hold values from -0.5 to 0.5
Outputs:
- products: float32 [17, 262144], P(None, 'blk')
- grad_input: float32 [128, 128], replicated
- grad_output: float32 [128, 128], replicated
All inputs are finite; a program needn't handle non-finite values.
Results may differ from a plain program's by a relative error of at most 0.014.
Values may be sent and summed in bfloat16 or wider, within the bound.
No kernel may reach another device: no remote copies, remote signals or barrier semaphores. Data moves between devices by JAX's collectives and lax.ppermute only.
A program may use at most 64 MiB of HBM per device.

v0:
```python
import jax
import jax.numpy as jnp
from jax import lax
from jax.sharding import PartitionSpec as P

ROUNDS = 4


def from_partner(x, axis, distance):
    return lax.ppermute(x, axis, [(i, i ^ 1 << distance) for i in range(lax.axis_size(axis))])


def tile_terms(row_feats, row_adj, row_vec, col_feats, col_adj, col_vec):
    kernel_scale = row_feats.shape[1] / 4.0
    row_sq = jnp.sum(jnp.square(row_feats.astype(jnp.float32)), axis=1)
    col_sq = jnp.sum(jnp.square(col_feats.astype(jnp.float32)), axis=1)
    inner = lax.dot_general(
        row_feats, col_feats, (((1,), (1,)), ((), ())), preferred_element_type=jnp.float32
    )
    distance = row_sq[:, None] + col_sq[None, :] - 2.0 * inner
    kernel = jnp.exp(-distance / kernel_scale)
    kernel_b = kernel.astype(jnp.bfloat16)
    row_prod = lax.dot_general(
        col_vec, kernel_b, (((1,), (1,)), ((), ())), preferred_element_type=jnp.float32
    )
    left = jnp.concatenate([row_adj, row_vec], axis=0)
    right = jnp.concatenate([col_vec, col_adj], axis=0)
    pairing = lax.dot_general(
        left, right, (((0,), (0,)), ((), ())), preferred_element_type=jnp.float32
    )
    weight = pairing * kernel
    weight_b = weight.astype(jnp.bfloat16)
    factor = -2.0 / kernel_scale
    row_grad = factor * (
        jnp.sum(weight, axis=1)[:, None] * row_feats.astype(jnp.float32)
        - jnp.dot(weight_b, col_feats, preferred_element_type=jnp.float32)
    )
    return (row_prod, row_grad)


def local(points, w_input, w_output, vectors, adjoint):
    preact = jnp.dot(points, w_input, preferred_element_type=jnp.float32)
    hidden = jnp.tanh(preact).astype(jnp.bfloat16)
    feats = jnp.dot(hidden, w_output, preferred_element_type=jnp.float32).astype(jnp.bfloat16)
    prod_sum, grad_sum = tile_terms(feats, adjoint, vectors, feats, adjoint, vectors)
    for level in range(ROUNDS):
        other_feats, other_adj, other_vec = from_partner((feats, adjoint, vectors), "blk", level)
        row_prod, row_grad = tile_terms(feats, adjoint, vectors, other_feats, other_adj, other_vec)
        prod_sum = prod_sum + row_prod
        grad_sum = grad_sum + row_grad
    feat_grad_b = grad_sum.astype(jnp.bfloat16)
    local_output = lax.dot_general(
        hidden, feat_grad_b, (((0,), (0,)), ((), ())), preferred_element_type=jnp.float32
    )
    back = lax.dot_general(
        feat_grad_b, w_output, (((1,), (1,)), ((), ())), preferred_element_type=jnp.float32
    )
    hidden_f = hidden.astype(jnp.float32)
    hidden_grad = (back * (1.0 - hidden_f * hidden_f)).astype(jnp.bfloat16)
    local_input = lax.dot_general(
        points, hidden_grad, (((0,), (0,)), ((), ())), preferred_element_type=jnp.float32
    )
    grad_input, grad_output = lax.psum((local_input, local_output), "blk")
    return (prod_sum, grad_input, grad_output)


def solution(mesh):
    return jax.shard_map(
        local,
        mesh=mesh,
        in_specs=(P("blk", None), P(), P(), P(None, "blk"), P(None, "blk")),
        out_specs=(P(None, "blk"), P(), P()),
        check_vma=False,
    )
```

profile of v0, /device:TPU:1, one launch (start us, length us, event | category | flops | bytes accessed | tf_op | source)
XLA Modules:
  0.0 330.8 jit_solution(5332672743160394004)
XLA Ops:
  7.2 2.6 collective-permute-start.9
  9.8 1.0 collective-permute-start.8
  10.7 6.0 %collective-permute-start.11 = (bf16[17,1024]{1,0:T(8,128)(2,1)}, bf16[17,1024]{1,0:T(8,128)(2,1)S(1)}, u32[]{:S(2)}, u32[]{:S(2)}) collective-permute-start(bf16[17,1024]{1,0:T(8,128)(2,1)} %param.9), channel_id=1, source_target_pairs={{0,8},{1,9},{2,10},{3,11},{4,12},{5,13},{6,14},{7,15},{8,0},{9,1},... | collective-permute-start | bytes 104456 | tf_op jit(solution)/shard_map/ppermute | solution.py:10
  16.8 1.2 collective-permute-start.10
  18.0 1.0 fusion.63
  18.9 1.0 fusion.82
  21.4 1.1 fusion.28
  22.5 1.5 fusion.121
  24.5 0.8 collective-permute-start.2
  26.1 6.4 %collective-permute-done.2 = bf16[1024,128]{0,1:T(8,128)(2,1)S(1)} collective-permute-done((bf16[1024,128]{0,1:T(8,128)(2,1)S(1)}, bf16[1024,128]{0,1:T(8,128)(2,1)S(1)}, u32[]{:S(2)}, u32[]{:S(2)}) %collective-permute-start.2) | collective-permute-done | bytes 262176 | tf_op jit(solution)/shard_map/ppermute | solution.py:10
  32.5 1.2 collective-permute-start.4
  34.4 12.3 %collective-permute-done.4 = bf16[1024,128]{0,1:T(8,128)(2,1)S(1)} collective-permute-done((bf16[1024,128]{0,1:T(8,128)(2,1)S(1)}, bf16[1024,128]{0,1:T(8,128)(2,1)S(1)}, u32[]{:S(2)}, u32[]{:S(2)}) %collective-permute-start.4) | collective-permute-done | bytes 262176 | tf_op jit(solution)/shard_map/ppermute | solution.py:10
  46.7 1.5 collective-permute-start.6
  49.0 13.8 %collective-permute-done.6 = bf16[1024,128]{0,1:T(8,128)(2,1)S(1)} collective-permute-done((bf16[1024,128]{0,1:T(8,128)(2,1)S(1)}, bf16[1024,128]{0,1:T(8,128)(2,1)S(1)}, u32[]{:S(2)}, u32[]{:S(2)}) %collective-permute-start.6) | collective-permute-done | bytes 262176 | tf_op jit(solution)/shard_map/ppermute | solution.py:10
  62.8 0.7 fusion.127
  63.6 2.5 collective-permute-start.7
  66.6 1.5 fusion.120
  68.6 2.9 collective-permute-start.1
  71.4 1.5 fusion.119
  73.5 1.5 fusion.118
  75.6 1.5 fusion.122
  77.6 0.9 fusion.128
  78.5 1.1 fusion.81
  79.7 3.4 %fusion.24 = f32[1024,17]{0,1:T(8,128)S(1)} fusion(bf16[17,1024]{1,0:T(8,128)(2,1)S(1)} %collective-permute-done.3, f32[1024,1024]{0,1:T(8,128)} %copy-done.3, f32[1024]{0:T(1024)S(1)} %multiply_reduce_fusion.2, f32[1024]{0:T(1024)S(1)} %get-tuple-element.8), kind=kOutput, calls=%fused_computation.27 | convolution fusion | flops 41943040 | bytes 4306944 | tf_op jit(solution)/shard_map/dot_general | solution.py:23
  83.1 1.1 fusion.22
  84.2 1.1 copy-done.7
  85.3 1.1 fusion.20
  86.4 1.1 copy-done.2
  87.5 1.7 fusion.78
  89.2 231.7 %all-reduce.3.cloned.1.call-done = (f32[128,128]{0,1:T(8,128)}, f32[128,128]{1,0:T(8,128)}) async-done(((f32[128,128]{0,1:T(8,128)}, f32[128,128]{1,0:T(8,128)}), (f32[128,128]{0,1:T(8,128)}, f32[128,128]{1,0:T(8,128)})) %all-reduce.3.cloned.1.call-update) | async-done | bytes 131088 | tf_op jit(solution)/shard_map/psum | solution.py:63
  320.9 1.6 copy.13
  322.5 1.5 copy.21
  (47 shorter events, 6.9 us)
Async XLA Ops:
  7.2 10.8 %copy-start = (bf16[1024,128]{1,0:T(8,128)(2,1)S(1)}, bf16[1024,128]{1,0:T(8,128)(2,1)}, u32[]{:S(2)}) copy-start(bf16[1024,128]{1,0:T(8,128)(2,1)} %param.5) | copy-start | bytes 786436
  7.2 14.2 %copy-start.9 = (bf16[17,1024]{1,0:T(8,128)(2,1)S(1)}, bf16[17,1024]{1,0:T(8,128)(2,1)}, u32[]{:S(2)}) copy-start(bf16[17,1024]{1,0:T(8,128)(2,1)} %param.8) | copy-start | bytes 104452
  7.2 313.7 %all-reduce.3.cloned.1.call-start = ((), (), s32[]{:S(2)}) async-start(), calls=%async_computation | async-start | bytes 262144 | tf_op jit(solution)/shard_map/psum | solution.py:63
  7.2 56.4 %collective-permute-start.9 = (bf16[17,1024]{1,0:T(8,128)(2,1)}, bf16[17,1024]{1,0:T(8,128)(2,1)S(1)}, u32[]{:S(2)}, u32[]{:S(2)}) collective-permute-start(bf16[17,1024]{1,0:T(8,128)(2,1)} %param.9), channel_id=1, source_target_pairs={{0,2},{1,3},{2,0},{3,1},{4,6},{5,7},{6,4},{7,5},{8,10},{9,11},{10,... | collective-permute-start | bytes 104456 | tf_op jit(solution)/shard_map/ppermute | solution.py:10
  9.8 65.7 %collective-permute-start.8 = (bf16[17,1024]{1,0:T(8,128)(2,1)}, bf16[17,1024]{1,0:T(8,128)(2,1)S(1)}, u32[]{:S(2)}, u32[]{:S(2)}) collective-permute-start(bf16[17,1024]{1,0:T(8,128)(2,1)} %param.9), channel_id=1, source_target_pairs={{0,1},{1,0},{2,3},{3,2},{4,5},{5,4},{6,7},{7,6},{8,9},{9,8},{10,11... | collective-permute-start | bytes 104456 | tf_op jit(solution)/shard_map/ppermute | solution.py:10
  10.7 62.7 %collective-permute-start.11 = (bf16[17,1024]{1,0:T(8,128)(2,1)}, bf16[17,1024]{1,0:T(8,128)(2,1)S(1)}, u32[]{:S(2)}, u32[]{:S(2)}) collective-permute-start(bf16[17,1024]{1,0:T(8,128)(2,1)} %param.9), channel_id=1, source_target_pairs={{0,8},{1,9},{2,10},{3,11},{4,12},{5,13},{6,14},{7,15},{8,0},{9,1},... | collective-permute-start | bytes 104456 | tf_op jit(solution)/shard_map/ppermute | solution.py:10
  16.8 51.8 %collective-permute-start.10 = (bf16[17,1024]{1,0:T(8,128)(2,1)}, bf16[17,1024]{1,0:T(8,128)(2,1)S(1)}, u32[]{:S(2)}, u32[]{:S(2)}) collective-permute-start(bf16[17,1024]{1,0:T(8,128)(2,1)} %param.9), channel_id=1, source_target_pairs={{0,4},{1,5},{2,6},{3,7},{4,0},{5,1},{6,2},{7,3},{8,12},{9,13},{10,... | collective-permute-start | bytes 104456 | tf_op jit(solution)/shard_map/ppermute | solution.py:10
  20.0 4.5 %collective-permute-start = (bf16[1024,128]{0,1:T(8,128)(2,1)S(1)}, bf16[1024,128]{0,1:T(8,128)(2,1)S(1)}, u32[]{:S(2)}, u32[]{:S(2)}) collective-permute-start(bf16[1024,128]{0,1:T(8,128)(2,1)S(1)} %get-tuple-element.9), channel_id=1, source_target_pairs={{0,1},{1,0},{2,3},{3,2},{4,5},{5,4},{6,7},{7,6},{8,9},{9,8},{10,11... | collective-permute-start | bytes 786440 | tf_op jit(solution)/shard_map/ppermute | solution.py:10
  21.4 1.1 copy-start.10
  24.5 8.0 %collective-permute-start.2 = (bf16[1024,128]{0,1:T(8,128)(2,1)S(1)}, bf16[1024,128]{0,1:T(8,128)(2,1)S(1)}, u32[]{:S(2)}, u32[]{:S(2)}) collective-permute-start(bf16[1024,128]{0,1:T(8,128)(2,1)S(1)} %get-tuple-element.9), channel_id=1, source_target_pairs={{0,2},{1,3},{2,0},{3,1},{4,6},{5,7},{6,4},{7,5},{8,10},{9,11},{10,... | collective-permute-start | bytes 786440 | tf_op jit(solution)/shard_map/ppermute | solution.py:10
  26.1 49.5 %copy-start.1 = (f32[1024,1024]{0,1:T(8,128)}, f32[1024,1024]{0,1:T(8,128)S(1)}, u32[]{:S(2)}) copy-start(f32[1024,1024]{0,1:T(8,128)S(1)} %fusion.124) | copy-start | bytes 12582916
  32.5 14.2 %collective-permute-start.4 = (bf16[1024,128]{0,1:T(8,128)(2,1)S(1)}, bf16[1024,128]{0,1:T(8,128)(2,1)S(1)}, u32[]{:S(2)}, u32[]{:S(2)}) collective-permute-start(bf16[1024,128]{0,1:T(8,128)(2,1)S(1)} %get-tuple-element.9), channel_id=1, source_target_pairs={{0,4},{1,5},{2,6},{3,7},{4,0},{5,1},{6,2},{7,3},{8,12},{9,13},{10,... | collective-permute-start | bytes 786440 | tf_op jit(solution)/shard_map/ppermute | solution.py:10
  34.4 32.2 %copy-start.3 = (f32[1024,1024]{0,1:T(8,128)}, f32[1024,1024]{0,1:T(8,128)S(1)}, u32[]{:S(2)}) copy-start(f32[1024,1024]{0,1:T(8,128)S(1)} %fusion.125) | copy-start | bytes 12582916
  46.7 16.0 %collective-permute-start.6 = (bf16[1024,128]{0,1:T(8,128)(2,1)S(1)}, bf16[1024,128]{0,1:T(8,128)(2,1)S(1)}, u32[]{:S(2)}, u32[]{:S(2)}) collective-permute-start(bf16[1024,128]{0,1:T(8,128)(2,1)S(1)} %get-tuple-element.9), channel_id=1, source_target_pairs={{0,8},{1,9},{2,10},{3,11},{4,12},{5,13},{6,14},{7,15},{8,0},{9,1},... | collective-permute-start | bytes 786440 | tf_op jit(solution)/shard_map/ppermute | solution.py:10
  48.9 22.5 %copy-start.4 = (f32[1024,1024]{0,1:T(8,128)}, f32[1024,1024]{0,1:T(8,128)S(1)}, u32[]{:S(2)}) copy-start(f32[1024,1024]{0,1:T(8,128)S(1)} %fusion.126) | copy-start | bytes 12582916
  62.8 3.3 %collective-permute-start.3 = (bf16[17,1024]{1,0:T(8,128)(2,1)S(1)}, bf16[17,1024]{1,0:T(8,128)(2,1)S(1)}, u32[]{:S(2)}, u32[]{:S(2)}) collective-permute-start(bf16[17,1024]{1,0:T(8,128)(2,1)S(1)} %copy-done.9), channel_id=1, source_target_pairs={{0,2},{1,3},{2,0},{3,1},{4,6},{5,7},{6,4},{7,5},{8,10},{9,11},{10,... | collective-permute-start | bytes 104456 | tf_op jit(solution)/shard_map/ppermute | solution.py:10
  63.5 10.0 %copy-start.6 = (f32[1024,1024]{0,1:T(8,128)}, f32[1024,1024]{0,1:T(8,128)S(1)}, u32[]{:S(2)}) copy-start(f32[1024,1024]{0,1:T(8,128)S(1)} %fusion.127) | copy-start | bytes 12582916
  63.6 9.9 %collective-permute-start.7 = (bf16[17,1024]{1,0:T(8,128)(2,1)S(1)}, bf16[17,1024]{1,0:T(8,128)(2,1)S(1)}, u32[]{:S(2)}, u32[]{:S(2)}) collective-permute-start(bf16[17,1024]{1,0:T(8,128)(2,1)S(1)} %copy-done.9), channel_id=1, source_target_pairs={{0,8},{1,9},{2,10},{3,11},{4,12},{5,13},{6,14},{7,15},{8,0},{9,1},... | collective-permute-start | bytes 104456 | tf_op jit(solution)/shard_map/ppermute | solution.py:10
  66.1 5.4 %collective-permute-start.5 = (bf16[17,1024]{1,0:T(8,128)(2,1)S(1)}, bf16[17,1024]{1,0:T(8,128)(2,1)S(1)}, u32[]{:S(2)}, u32[]{:S(2)}) collective-permute-start(bf16[17,1024]{1,0:T(8,128)(2,1)S(1)} %copy-done.9), channel_id=1, source_target_pairs={{0,4},{1,5},{2,6},{3,7},{4,0},{5,1},{6,2},{7,3},{8,12},{9,13},{10,... | collective-permute-start | bytes 104456 | tf_op jit(solution)/shard_map/ppermute | solution.py:10
  68.6 6.9 %collective-permute-start.1 = (bf16[17,1024]{1,0:T(8,128)(2,1)S(1)}, bf16[17,1024]{1,0:T(8,128)(2,1)S(1)}, u32[]{:S(2)}, u32[]{:S(2)}) collective-permute-start(bf16[17,1024]{1,0:T(8,128)(2,1)S(1)} %copy-done.9), channel_id=1, source_target_pairs={{0,1},{1,0},{2,3},{3,2},{4,5},{5,4},{6,7},{7,6},{8,9},{9,8},{10,11... | collective-permute-start | bytes 104456 | tf_op jit(solution)/shard_map/ppermute | solution.py:10
  77.0 1.5 copy-start.8
  79.7 3.5 %copy-start.5 = (f32[1024,1024]{0,1:T(8,128)S(1)}, f32[1024,1024]{0,1:T(8,128)}, u32[]{:S(2)}) copy-start(f32[1024,1024]{0,1:T(8,128)} %copy-done.4) | copy-start | bytes 12582916
  83.1 2.2 copy-start.7
  85.3 2.2 copy-start.2
Sparse Core Ops, SparseCore 0:
  79.8 241.0 all-reduce.2
where the time goes:
time: 331 us
  waiting for transfers between devices  264 us (80%)
  matrix products  26 us (8%)
  starting transfers between devices  20.6 us (6%)
  between operations  14.3 us (4%)
  local copies, waits for them, and re-layouts  5.31 us (2%)
    psum x1, waiting for transfers between devices, local(): grad_input, grad_output = lax.psum((local_input, local_output), 'blk')  232 us
    ppermute x12, waiting for transfers between devices, from_partner(): lax.ppermute(x, axis, [(i, i ^ 1 << distance) for i in range(lax.axis_siz...  32.6 us
    ppermute x12, starting transfers between devices, from_partner(): lax.ppermute(x, axis, [(i, i ^ 1 << distance) for i in range(lax.axis_siz...  20.6 us
    dot_general x5, matrix products, tile_terms(): lax.dot_general(col_vec, kernel_b, (((1,), (1,)), ((), ())), preferred_el...  8.42 us
    dot_general x5, matrix products, tile_terms(): lax.dot_general(left, right, (((0,), (0,)), ((), ())), preferred_element_...  7.4 us
  transfers between devices with their start and end apart: 13, of which 4 were waited for; matrix products, arithmetic and copies ran while one was open for 7% of the time, Pallas kernels for 0%

commit v1 on v0

--- a/solution.py
+++ b/solution.py
@@ -1,13 +1,25 @@
 import jax
 import jax.numpy as jnp
 from jax import lax
-from jax.sharding import PartitionSpec as P
+from jax.sharding import Mesh, PartitionSpec as P
 
 ROUNDS = 4
+ALL = ("x", "y", "z", "c")
 
 
-def from_partner(x, axis, distance):
-    return lax.ppermute(x, axis, [(i, i ^ 1 << distance) for i in range(lax.axis_size(axis))])
+def from_partner(x, distance):
+    return lax.ppermute(x, ALL, [(i, i ^ 1 << distance) for i in range(lax.axis_size(ALL))])
+
+
+def swap_cores(x):
+    return lax.ppermute(x, "c", [(0, 1), (1, 0)])
+
+
+def sum_over(x, axes):
+    n = lax.axis_size(axes)
+    sent = jnp.broadcast_to(x.astype(jnp.bfloat16), (n,) + x.shape)
+    got = lax.all_to_all(sent, axes, 0, 0)
+    return jnp.sum(got.astype(jnp.float32), axis=0)
 
 
 def tile_terms(row_feats, row_adj, row_vec, col_feats, col_adj, col_vec):
@@ -44,7 +56,7 @@
     feats = jnp.dot(hidden, w_output, preferred_element_type=jnp.float32).astype(jnp.bfloat16)
     prod_sum, grad_sum = tile_terms(feats, adjoint, vectors, feats, adjoint, vectors)
     for level in range(ROUNDS):
-        other_feats, other_adj, other_vec = from_partner((feats, adjoint, vectors), "blk", level)
+        other_feats, other_adj, other_vec = from_partner((feats, adjoint, vectors), level)
         row_prod, row_grad = tile_terms(feats, adjoint, vectors, other_feats, other_adj, other_vec)
         prod_sum = prod_sum + row_prod
         grad_sum = grad_sum + row_grad
@@ -60,15 +72,23 @@
     local_input = lax.dot_general(
         points, hidden_grad, (((0,), (0,)), ((), ())), preferred_element_type=jnp.float32
     )
-    grad_input, grad_output = lax.psum((local_input, local_output), "blk")
+    second = lax.axis_index("c") == 1
+    mine = jnp.where(second, local_output, local_input)
+    mine = mine + swap_cores(jnp.where(second, local_input, local_output))
+    mine = sum_over(mine, ("z",))
+    mine = sum_over(mine, ("x", "y"))
+    other = swap_cores(mine)
+    grad_input = jnp.where(second, other, mine)
+    grad_output = jnp.where(second, mine, other)
     return (prod_sum, grad_input, grad_output)
 
 
 def solution(mesh):
+    grid = Mesh(mesh.devices.reshape(4, 4, 8, 2), ALL)
     return jax.shard_map(
         local,
-        mesh=mesh,
-        in_specs=(P("blk", None), P(), P(), P(None, "blk"), P(None, "blk")),
-        out_specs=(P(None, "blk"), P(), P()),
+        mesh=grid,
+        in_specs=(P(ALL, None), P(), P(), P(None, ALL), P(None, ALL)),
+        out_specs=(P(None, ALL), P(), P()),
         check_vma=False,
     )

time: 331 us -> 119 us (0.36)
  waiting for transfers between devices: 264 us -> 44.8 us
  starting transfers between devices: 20.6 us -> 36.8 us
  between operations: 14.3 us -> 0.96 us
  matrix products: 26 us -> 33.2 us
  local copies, waits for them, and re-layouts: 5.31 us -> 1.77 us
    psum x1 -> x0, waiting for transfers between devices: 232 us -> none  [local(): grad_input, grad_output = lax.psum((local_input, local_output), 'blk')]
    all_to_all x0 -> x2, starting transfers between devices: none -> 11.4 us  [sum_over(): got = lax.all_to_all(sent, axes, 0, 0)]
    all_to_all x0 -> x2, waiting for transfers between devices: none -> 11.3 us  [sum_over(): got = lax.all_to_all(sent, axes, 0, 0)]
    unnamed x24 -> x20, local copies, waits for them, and re-layouts: 5.31 us -> 0.11 us
    ppermute x12 -> x14, starting transfers between devices: 20.6 us -> 25.4 us  [the longest x12 20.4 us: from_partner(): lax.ppermute(x, ALL, [(i, i ^ 1 << distance) for i in range(lax.axis_size...]
    dot_general x5, matrix products: 8.42 us -> 12.9 us  [tile_terms(): lax.dot_general(col_vec, kernel_b, (((1,), (1,)), ((), ())), preferred_el...]
    ppermute x12 -> x14, waiting for transfers between devices: 32.6 us -> 33.5 us  [the longest x12 32.6 us: from_partner(): lax.ppermute(x, ALL, [(i, i ^ 1 << distance) for i in range(lax.axis_size...]
  transfers between devices with their start and end apart: 13 -> 16, of which waited for: 4 -> 6; matrix products, arithmetic and copies ran while one was open for 7% -> 26% of each run, Pallas kernels for 0% -> 0%
where the time goes in v1:
time: 119 us
  waiting for transfers between devices  44.8 us (38%)
  starting transfers between devices  36.8 us (31%)
  matrix products  33.2 us (28%)
  local copies, waits for them, and re-layouts  1.77 us (1%)
    ppermute x12, waiting for transfers between devices, from_partner(): lax.ppermute(x, ALL, [(i, i ^ 1 << distance) for i in range(lax.axis_size...  32.6 us
    ppermute x12, starting transfers between devices, from_partner(): lax.ppermute(x, ALL, [(i, i ^ 1 << distance) for i in range(lax.axis_size...  20.4 us
    dot_general x5, matrix products, tile_terms(): lax.dot_general(col_vec, kernel_b, (((1,), (1,)), ((), ())), preferred_el...  12.9 us
    all_to_all x2, starting transfers between devices, sum_over(): got = lax.all_to_all(sent, axes, 0, 0)  11.4 us
    all_to_all x2, waiting for transfers between devices, sum_over(): got = lax.all_to_all(sent, axes, 0, 0)  11.3 us
    dot_general x5, matrix products, tile_terms(): lax.dot_general(left, right, (((0,), (0,)), ((), ())), preferred_element_...  9.52 us
    dot_general x5, matrix products, tile_terms(): lax.dot_general(row_feats, col_feats, (((1,), (1,)), ((), ())), preferred...  5.7 us
    ppermute x2, starting transfers between devices, swap_cores(): return lax.ppermute(x, 'c', [(0, 1), (1, 0)])  4.96 us
  transfers between devices with their start and end apart: 16, of which 6 were waited for; matrix products, arithmetic and copies ran while one was open for 26% of the time, Pallas kernels for 0%

profile of v1, /device:TPU:1, one launch (start us, length us, event | category | flops | bytes accessed | tf_op | source)
XLA Modules:
  0.0 118.6 jit_solution(8497621130625494261)
XLA Ops:
  0.7 2.6 %collective-permute-start.9 = (bf16[17,1024]{1,0:T(8,128)(2,1)}, bf16[17,1024]{1,0:T(8,128)(2,1)S(1)}, u32[]{:S(2)}, u32[]{:S(2)}) collective-permute-start(bf16[17,1024]{1,0:T(8,128)(2,1)} %param.9), channel_id=1, source_target_pairs={{0,2},{1,3},{2,0},{3,1},{4,6},{5,7},{6,4},{7,5},{8,10},{9,11},{10,... | collective-permute-start | bytes 104456 | tf_op jit(solution)/shard_map/ppermute | solution.py:11
  3.2 1.0 collective-permute-start.8
  4.2 6.0 %collective-permute-start.11 = (bf16[17,1024]{1,0:T(8,128)(2,1)}, bf16[17,1024]{1,0:T(8,128)(2,1)S(1)}, u32[]{:S(2)}, u32[]{:S(2)}) collective-permute-start(bf16[17,1024]{1,0:T(8,128)(2,1)} %param.9), channel_id=1, source_target_pairs={{0,8},{1,9},{2,10},{3,11},{4,12},{5,13},{6,14},{7,15},{8,0},{9,1},... | collective-permute-start | bytes 104456 | tf_op jit(solution)/shard_map/ppermute | solution.py:11
  10.2 1.2 %collective-permute-start.10 = (bf16[17,1024]{1,0:T(8,128)(2,1)}, bf16[17,1024]{1,0:T(8,128)(2,1)S(1)}, u32[]{:S(2)}, u32[]{:S(2)}) collective-permute-start(bf16[17,1024]{1,0:T(8,128)(2,1)} %param.9), channel_id=1, source_target_pairs={{0,4},{1,5},{2,6},{3,7},{4,0},{5,1},{6,2},{7,3},{8,12},{9,13},{10,... | collective-permute-start | bytes 104456 | tf_op jit(solution)/shard_map/ppermute | solution.py:11
  11.4 1.0 fusion.63
  12.4 1.0 fusion.82
  14.0 2.7 %fusion.123 = f32[1024,1024]{0,1:T(8,128)} fusion(bf16[1024,128]{0,1:T(8,128)(2,1)S(1)} %get-tuple-element.6), kind=kOutput, calls=%fused_computation.110 | convolution fusion | flops 268435456 | bytes 4456448 | tf_op jit(solution)/shard_map/dot_general | solution.py:29
  16.8 3.6 %fusion.121 = (f32[1024]{0:T(1024)S(1)}, bf16[1024,1024]{0,1:T(8,128)(2,1)S(1)}) fusion(f32[1024,1024]{0,1:T(8,128)} %fusion.123, f32[1024]{0:T(1024)S(1)} %get-tuple-element.5, bf16[17,1024]{1,0:T(8,128)(2,1)S(1)} %copy-done.8, bf16[17,1024]{1,0:T(8,128)(2,1)S(1)} %copy-done.9), kind=kOutput, calls=%fused_computation.108 | convolution fusion | flops 79969280 | bytes 6369280 | tf_op jit(solution)/shard_map/dot_general | solution.py:40
  22.5 6.4 %collective-permute-done.2 = bf16[1024,128]{0,1:T(8,128)(2,1)S(1)} collective-permute-done((bf16[1024,128]{0,1:T(8,128)(2,1)S(1)}, bf16[1024,128]{0,1:T(8,128)(2,1)S(1)}, u32[]{:S(2)}, u32[]{:S(2)}) %collective-permute-start.2) | collective-permute-done | bytes 262176 | tf_op jit(solution)/shard_map/ppermute | solution.py:11
  28.9 1.2 collective-permute-start.4
  30.8 12.3 %collective-permute-done.4 = bf16[1024,128]{0,1:T(8,128)(2,1)S(1)} collective-permute-done((bf16[1024,128]{0,1:T(8,128)(2,1)S(1)}, bf16[1024,128]{0,1:T(8,128)(2,1)S(1)}, u32[]{:S(2)}, u32[]{:S(2)}) %collective-permute-start.4) | collective-permute-done | bytes 262176 | tf_op jit(solution)/shard_map/ppermute | solution.py:11
  43.1 1.5 %collective-permute-start.6 = (bf16[1024,128]{0,1:T(8,128)(2,1)S(1)}, bf16[1024,128]{0,1:T(8,128)(2,1)S(1)}, u32[]{:S(2)}, u32[]{:S(2)}) collective-permute-start(bf16[1024,128]{0,1:T(8,128)(2,1)S(1)} %get-tuple-element.6), channel_id=1, source_target_pairs={{0,8},{1,9},{2,10},{3,11},{4,12},{5,13},{6,14},{7,15},{8,0},{9,1},... | collective-permute-start | bytes 786440 | tf_op jit(solution)/shard_map/ppermute | solution.py:11
  45.4 13.8 %collective-permute-done.6 = bf16[1024,128]{0,1:T(8,128)(2,1)S(1)} collective-permute-done((bf16[1024,128]{0,1:T(8,128)(2,1)S(1)}, bf16[1024,128]{0,1:T(8,128)(2,1)S(1)}, u32[]{:S(2)}, u32[]{:S(2)}) %collective-permute-start.6) | collective-permute-done | bytes 262176 | tf_op jit(solution)/shard_map/ppermute | solution.py:11
  60.1 2.5 %collective-permute-start.7 = (bf16[17,1024]{1,0:T(8,128)(2,1)S(1)}, bf16[17,1024]{1,0:T(8,128)(2,1)S(1)}, u32[]{:S(2)}, u32[]{:S(2)}) collective-permute-start(bf16[17,1024]{1,0:T(8,128)(2,1)S(1)} %copy-done.9), channel_id=1, source_target_pairs={{0,8},{1,9},{2,10},{3,11},{4,12},{5,13},{6,14},{7,15},{8,0},{9,1},... | collective-permute-start | bytes 104456 | tf_op jit(solution)/shard_map/ppermute | solution.py:11
  63.0 1.5 %fusion.120 = (f32[1024]{0:T(1024)S(1)}, bf16[1024,1024]{0,1:T(8,128)(2,1)S(1)}) fusion(f32[1024,1024]{0,1:T(8,128)S(1)} %fusion.125, f32[1024]{0:T(1024)S(1)} %multiply_reduce_fusion.2, f32[1024]{0:T(1024)S(1)} %get-tuple-element.5, bf16[17,1024]{1,0:T(8,128)(2,1)S(1)} %collective-permute-done.9, bf16[17,1024]{1,0:T(8,128)(2,1)S(1)} %collective-permute-done.3, ...), kind=kOutput, calls=%fused_computation.107 | convolution fusion | flops 79969280 | bytes 6443008 | tf_op jit(solution)/shard_map/dot_general | solution.py:40
  65.1 2.6 %collective-permute-start.1 = (bf16[17,1024]{1,0:T(8,128)(2,1)S(1)}, bf16[17,1024]{1,0:T(8,128)(2,1)S(1)}, u32[]{:S(2)}, u32[]{:S(2)}) collective-permute-start(bf16[17,1024]{1,0:T(8,128)(2,1)S(1)} %copy-done.9), channel_id=1, source_target_pairs={{0,1},{1,0},{2,3},{3,2},{4,5},{5,4},{6,7},{7,6},{8,9},{9,8},{10,11... | collective-permute-start | bytes 104456 | tf_op jit(solution)/shard_map/ppermute | solution.py:11
  67.7 1.5 %fusion.119 = (f32[1024]{0:T(1024)S(1)}, bf16[1024,1024]{0,1:T(8,128)(2,1)S(1)}) fusion(f32[1024,1024]{0,1:T(8,128)S(1)} %fusion.126, f32[1024]{0:T(1024)S(1)} %multiply_reduce_fusion.1, f32[1024]{0:T(1024)S(1)} %get-tuple-element.5, bf16[17,1024]{1,0:T(8,128)(2,1)S(1)} %collective-permute-done.10, bf16[17,1024]{1,0:T(8,128)(2,1)S(1)} %collective-permute-done.5, ...), kind=kOutput, calls=%fused_computation.106 | convolution fusion | flops 79969280 | bytes 6443008 | tf_op jit(solution)/shard_map/dot_general | solution.py:40
  69.7 1.5 %fusion.118 = (f32[1024]{0:T(1024)S(1)}, bf16[1024,1024]{0,1:T(8,128)(2,1)S(1)}) fusion(f32[1024,1024]{0,1:T(8,128)S(1)} %fusion.127, f32[1024]{0:T(1024)S(1)} %multiply_reduce_fusion, f32[1024]{0:T(1024)S(1)} %get-tuple-element.5, bf16[17,1024]{1,0:T(8,128)(2,1)S(1)} %collective-permute-done.11, bf16[17,1024]{1,0:T(8,128)(2,1)S(1)} %collective-permute-done.7, ...), kind=kOutput, calls=%fused_computation.105 | convolution fusion | flops 79969280 | bytes 6443008 | tf_op jit(solution)/shard_map/dot_general | solution.py:40
  71.8 1.5 %fusion.122 = (f32[1024]{0:T(1024)S(1)}, bf16[1024,1024]{0,1:T(8,128)(2,1)S(1)}) fusion(f32[1024,1024]{0,1:T(8,128)S(1)} %fusion.124, f32[1024]{0:T(1024)S(1)} %multiply_reduce_fusion.3, f32[1024]{0:T(1024)S(1)} %get-tuple-element.5, bf16[17,1024]{1,0:T(8,128)(2,1)S(1)} %collective-permute-done.8, bf16[17,1024]{1,0:T(8,128)(2,1)S(1)} %collective-permute-done.1, ...), kind=kOutput, calls=%fused_computation.109 | convolution fusion | flops 79969280 | bytes 6443008 | tf_op jit(solution)/shard_map/dot_general | solution.py:40
  74.6 1.6 %collective-permute-start.12 = (f32[128,128]{1,0:T(8,128)S(1)}, f32[128,128]{1,0:T(8,128)S(1)}, u32[]{:S(2)}, u32[]{:S(2)}) collective-permute-start(f32[128,128]{1,0:T(8,128)S(1)} %get-tuple-element.17), channel_id=1, source_target_pairs={{0,1},{1,0},{2,3},{3,2},{4,5},{5,4},{6,7},{7,6},{8,9},{9,8},{10,11... | collective-permute-start | bytes 196616 | tf_op jit(solution)/shard_map/ppermute | solution.py:15
  76.2 0.9 collective-permute-done.12
  77.9 5.6 %all-to-all-start = ((bf16[8,128,128]{2,1,0:T(8,128)(2,1)}), bf16[8,128,128]{2,1,0:T(8,128)(2,1)S(1)}, u32[]{:S(2)}, u32[]{:S(2)}) async-start(bf16[8,128,128]{2,1,0:T(8,128)(2,1)} %broadcast_in_dim.4), calls=%async_computation | async-start | bytes 524288 | tf_op jit(solution)/shard_map/all_to_all | solution.py:21
  83.4 3.4 %fusion.28 = f32[1024,17]{0,1:T(8,128)S(1)} fusion(bf16[17,1024]{1,0:T(8,128)(2,1)S(1)} %copy-done.9, f32[1024,1024]{0,1:T(8,128)} %fusion.123, f32[1024]{0:T(1024)S(1)} %get-tuple-element.5), kind=kOutput, calls=%fused_computation.29 | convolution fusion | flops 41943040 | bytes 4302848 | tf_op jit(solution)/shard_map/dot_general | solution.py:35
  86.9 1.1 fusion.24
  88.0 6.6 %all-to-all-done = bf16[8,128,128]{2,1,0:T(8,128)(2,1)S(1)} async-done(((bf16[8,128,128]{2,1,0:T(8,128)(2,1)}), bf16[8,128,128]{2,1,0:T(8,128)(2,1)S(1)}, u32[]{:S(2)}, u32[]{:S(2)}) %all-to-all-start) | async-done | bytes 262176 | tf_op jit(solution)/shard_map/all_to_all | solution.py:21
  94.6 0.9 broadcast_in_dim.5
  95.6 5.9 %all-to-all-start.1 = ((bf16[16,128,128]{2,1,0:T(8,128)(2,1)}), bf16[16,128,128]{2,1,0:T(8,128)(2,1)S(1)}, u32[]{:S(2)}, u32[]{:S(2)}) async-start(bf16[16,128,128]{2,1,0:T(8,128)(2,1)} %broadcast_in_dim.5), calls=%async_computation.1 | async-start | bytes 1048576 | tf_op jit(solution)/shard_map/all_to_all | solution.py:21
  101.5 3.4 %fusion.22 = f32[1024,17]{0,1:T(8,128)S(1)} fusion(bf16[17,1024]{1,0:T(8,128)(2,1)S(1)} %collective-permute-done.5, f32[1024,1024]{0,1:T(8,128)} %copy-done.2, f32[1024]{0:T(1024)S(1)} %multiply_reduce_fusion.1, f32[1024]{0:T(1024)S(1)} %get-tuple-element.5), kind=kOutput, calls=%fused_computation.26 | convolution fusion | flops 41943040 | bytes 4306944 | tf_op jit(solution)/shard_map/dot_general | solution.py:35
  104.9 1.1 fusion.20
  106.0 4.7 %all-to-all-done.1 = bf16[16,128,128]{2,1,0:T(8,128)(2,1)S(1)} async-done(((bf16[16,128,128]{2,1,0:T(8,128)(2,1)}), bf16[16,128,128]{2,1,0:T(8,128)(2,1)S(1)}, u32[]{:S(2)}, u32[]{:S(2)}) %all-to-all-start.1) | async-done | bytes 524320 | tf_op jit(solution)/shard_map/all_to_all | solution.py:21
  110.7 3.3 %collective-permute-start.13 = (f32[128,128]{1,0:T(8,128)S(1)}, f32[128,128]{1,0:T(8,128)S(1)}, u32[]{:S(2)}, u32[]{:S(2)}) collective-permute-start(f32[128,128]{1,0:T(8,128)S(1)} %convert_reduce_fusion), channel_id=1, source_target_pairs={{0,1},{1,0},{2,3},{3,2},{4,5},{5,4},{6,7},{7,6},{8,9},{9,8},{10,11... | collective-permute-start | bytes 196616 | tf_op jit(solution)/shard_map/ppermute | solution.py:15
  114.0 3.9 %fusion.78 = f32[17,1024]{1,0:T(8,128)} fusion(f32[1024,17]{0,1:T(8,128)S(1)} %fusion.20, f32[1024,17]{0,1:T(8,128)S(1)} %fusion.22, f32[1024,17]{0,1:T(8,128)S(1)} %fusion.24, f32[1024,17]{0,1:T(8,128)S(1)} %fusion.28, bf16[17,1024]{1,0:T(8,128)(2,1)S(1)} %collective-permute-done.1, f32[1024,1024]{0,1:T(8,128)} %copy-done.1, ...), kind=kOutput, calls=%fused_computation.57 | convolution fusion | flops 42012672 | bytes 4585472 | tf_op jit(solution)/shard_map/dot_general | solution.py:35
  (54 shorter events, 10.0 us)
Async XLA Ops:
  0.6 10.8 %copy-start = (bf16[1024,128]{1,0:T(8,128)(2,1)S(1)}, bf16[1024,128]{1,0:T(8,128)(2,1)}, u32[]{:S(2)}) copy-start(bf16[1024,128]{1,0:T(8,128)(2,1)} %param.5) | copy-start | bytes 786436
  0.6 16.1 %copy-start.8 = (bf16[17,1024]{1,0:T(8,128)(2,1)S(1)}, bf16[17,1024]{1,0:T(8,128)(2,1)}, u32[]{:S(2)}) copy-start(bf16[17,1024]{1,0:T(8,128)(2,1)} %param.9) | copy-start | bytes 104452
  0.7 16.1 %copy-start.9 = (bf16[17,1024]{1,0:T(8,128)(2,1)S(1)}, bf16[17,1024]{1,0:T(8,128)(2,1)}, u32[]{:S(2)}) copy-start(bf16[17,1024]{1,0:T(8,128)(2,1)} %param.8) | copy-start | bytes 104452
  0.7 59.4 %collective-permute-start.9 = (bf16[17,1024]{1,0:T(8,128)(2,1)}, bf16[17,1024]{1,0:T(8,128)(2,1)S(1)}, u32[]{:S(2)}, u32[]{:S(2)}) collective-permute-start(bf16[17,1024]{1,0:T(8,128)(2,1)} %param.9), channel_id=1, source_target_pairs={{0,2},{1,3},{2,0},{3,1},{4,6},{5,7},{6,4},{7,5},{8,10},{9,11},{10,... | collective-permute-start | bytes 104456 | tf_op jit(solution)/shard_map/ppermute | solution.py:11
  3.2 68.5 %collective-permute-start.8 = (bf16[17,1024]{1,0:T(8,128)(2,1)}, bf16[17,1024]{1,0:T(8,128)(2,1)S(1)}, u32[]{:S(2)}, u32[]{:S(2)}) collective-permute-start(bf16[17,1024]{1,0:T(8,128)(2,1)} %param.9), channel_id=1, source_target_pairs={{0,1},{1,0},{2,3},{3,2},{4,5},{5,4},{6,7},{7,6},{8,9},{9,8},{10,11... | collective-permute-start | bytes 104456 | tf_op jit(solution)/shard_map/ppermute | solution.py:11
  4.2 65.5 %collective-permute-start.11 = (bf16[17,1024]{1,0:T(8,128)(2,1)}, bf16[17,1024]{1,0:T(8,128)(2,1)S(1)}, u32[]{:S(2)}, u32[]{:S(2)}) collective-permute-start(bf16[17,1024]{1,0:T(8,128)(2,1)} %param.9), channel_id=1, source_target_pairs={{0,8},{1,9},{2,10},{3,11},{4,12},{5,13},{6,14},{7,15},{8,0},{9,1},... | collective-permute-start | bytes 104456 | tf_op jit(solution)/shard_map/ppermute | solution.py:11
  10.2 54.9 %collective-permute-start.10 = (bf16[17,1024]{1,0:T(8,128)(2,1)}, bf16[17,1024]{1,0:T(8,128)(2,1)S(1)}, u32[]{:S(2)}, u32[]{:S(2)}) collective-permute-start(bf16[17,1024]{1,0:T(8,128)(2,1)} %param.9), channel_id=1, source_target_pairs={{0,4},{1,5},{2,6},{3,7},{4,0},{5,1},{6,2},{7,3},{8,12},{9,13},{10,... | collective-permute-start | bytes 104456 | tf_op jit(solution)/shard_map/ppermute | solution.py:11
  13.4 7.5 %collective-permute-start = (bf16[1024,128]{0,1:T(8,128)(2,1)S(1)}, bf16[1024,128]{0,1:T(8,128)(2,1)S(1)}, u32[]{:S(2)}, u32[]{:S(2)}) collective-permute-start(bf16[1024,128]{0,1:T(8,128)(2,1)S(1)} %get-tuple-element.6), channel_id=1, source_target_pairs={{0,1},{1,0},{2,3},{3,2},{4,5},{5,4},{6,7},{7,6},{8,9},{9,8},{10,11... | collective-permute-start | bytes 786440 | tf_op jit(solution)/shard_map/ppermute | solution.py:11
  20.9 8.0 %collective-permute-start.2 = (bf16[1024,128]{0,1:T(8,128)(2,1)S(1)}, bf16[1024,128]{0,1:T(8,128)(2,1)S(1)}, u32[]{:S(2)}, u32[]{:S(2)}) collective-permute-start(bf16[1024,128]{0,1:T(8,128)(2,1)S(1)} %get-tuple-element.6), channel_id=1, source_target_pairs={{0,2},{1,3},{2,0},{3,1},{4,6},{5,7},{6,4},{7,5},{8,10},{9,11},{10,... | collective-permute-start | bytes 786440 | tf_op jit(solution)/shard_map/ppermute | solution.py:11
  22.5 49.3 %copy-start.1 = (f32[1024,1024]{0,1:T(8,128)}, f32[1024,1024]{0,1:T(8,128)S(1)}, u32[]{:S(2)}) copy-start(f32[1024,1024]{0,1:T(8,128)S(1)} %fusion.124) | copy-start | bytes 12582916
  28.9 14.2 %collective-permute-start.4 = (bf16[1024,128]{0,1:T(8,128)(2,1)S(1)}, bf16[1024,128]{0,1:T(8,128)(2,1)S(1)}, u32[]{:S(2)}, u32[]{:S(2)}) collective-permute-start(bf16[1024,128]{0,1:T(8,128)(2,1)S(1)} %get-tuple-element.6), channel_id=1, source_target_pairs={{0,4},{1,5},{2,6},{3,7},{4,0},{5,1},{6,2},{7,3},{8,12},{9,13},{10,... | collective-permute-start | bytes 786440 | tf_op jit(solution)/shard_map/ppermute | solution.py:11
  30.8 32.2 %copy-start.5 = (f32[1024,1024]{0,1:T(8,128)}, f32[1024,1024]{0,1:T(8,128)S(1)}, u32[]{:S(2)}) copy-start(f32[1024,1024]{0,1:T(8,128)S(1)} %fusion.125) | copy-start | bytes 12582916
  43.1 16.1 %collective-permute-start.6 = (bf16[1024,128]{0,1:T(8,128)(2,1)S(1)}, bf16[1024,128]{0,1:T(8,128)(2,1)S(1)}, u32[]{:S(2)}, u32[]{:S(2)}) collective-permute-start(bf16[1024,128]{0,1:T(8,128)(2,1)S(1)} %get-tuple-element.6), channel_id=1, source_target_pairs={{0,8},{1,9},{2,10},{3,11},{4,12},{5,13},{6,14},{7,15},{8,0},{9,1},... | collective-permute-start | bytes 786440 | tf_op jit(solution)/shard_map/ppermute | solution.py:11
  45.4 22.3 %copy-start.2 = (f32[1024,1024]{0,1:T(8,128)}, f32[1024,1024]{0,1:T(8,128)S(1)}, u32[]{:S(2)}) copy-start(f32[1024,1024]{0,1:T(8,128)S(1)} %fusion.126) | copy-start | bytes 12582916
  59.2 3.3 %collective-permute-start.3 = (bf16[17,1024]{1,0:T(8,128)(2,1)S(1)}, bf16[17,1024]{1,0:T(8,128)(2,1)S(1)}, u32[]{:S(2)}, u32[]{:S(2)}) collective-permute-start(bf16[17,1024]{1,0:T(8,128)(2,1)S(1)} %copy-done.9), channel_id=1, source_target_pairs={{0,2},{1,3},{2,0},{3,1},{4,6},{5,7},{6,4},{7,5},{8,10},{9,11},{10,... | collective-permute-start | bytes 104456 | tf_op jit(solution)/shard_map/ppermute | solution.py:11
  60.0 9.8 %copy-start.3 = (f32[1024,1024]{0,1:T(8,128)}, f32[1024,1024]{0,1:T(8,128)S(1)}, u32[]{:S(2)}) copy-start(f32[1024,1024]{0,1:T(8,128)S(1)} %fusion.127) | copy-start | bytes 12582916
  60.1 9.7 %collective-permute-start.7 = (bf16[17,1024]{1,0:T(8,128)(2,1)S(1)}, bf16[17,1024]{1,0:T(8,128)(2,1)S(1)}, u32[]{:S(2)}, u32[]{:S(2)}) collective-permute-start(bf16[17,1024]{1,0:T(8,128)(2,1)S(1)} %copy-done.9), channel_id=1, source_target_pairs={{0,8},{1,9},{2,10},{3,11},{4,12},{5,13},{6,14},{7,15},{8,0},{9,1},... | collective-permute-start | bytes 104456 | tf_op jit(solution)/shard_map/ppermute | solution.py:11
  62.5 5.2 %collective-permute-start.5 = (bf16[17,1024]{1,0:T(8,128)(2,1)S(1)}, bf16[17,1024]{1,0:T(8,128)(2,1)S(1)}, u32[]{:S(2)}, u32[]{:S(2)}) collective-permute-start(bf16[17,1024]{1,0:T(8,128)(2,1)S(1)} %copy-done.9), channel_id=1, source_target_pairs={{0,4},{1,5},{2,6},{3,7},{4,0},{5,1},{6,2},{7,3},{8,12},{9,13},{10,... | collective-permute-start | bytes 104456 | tf_op jit(solution)/shard_map/ppermute | solution.py:11
  65.1 6.7 %collective-permute-start.1 = (bf16[17,1024]{1,0:T(8,128)(2,1)S(1)}, bf16[17,1024]{1,0:T(8,128)(2,1)S(1)}, u32[]{:S(2)}, u32[]{:S(2)}) collective-permute-start(bf16[17,1024]{1,0:T(8,128)(2,1)S(1)} %copy-done.9), channel_id=1, source_target_pairs={{0,1},{1,0},{2,3},{3,2},{4,5},{5,4},{6,7},{7,6},{8,9},{9,8},{10,11... | collective-permute-start | bytes 104456 | tf_op jit(solution)/shard_map/ppermute | solution.py:11
  73.3 0.8 copy-start.7
  74.6 2.5 %collective-permute-start.12 = (f32[128,128]{1,0:T(8,128)S(1)}, f32[128,128]{1,0:T(8,128)S(1)}, u32[]{:S(2)}, u32[]{:S(2)}) collective-permute-start(f32[128,128]{1,0:T(8,128)S(1)} %get-tuple-element.17), channel_id=1, source_target_pairs={{0,1},{1,0},{2,3},{3,2},{4,5},{5,4},{6,7},{7,6},{8,9},{9,8},{10,11... | collective-permute-start | bytes 196616 | tf_op jit(solution)/shard_map/ppermute | solution.py:15
  77.9 16.7 %all-to-all-start = ((bf16[8,128,128]{2,1,0:T(8,128)(2,1)}), bf16[8,128,128]{2,1,0:T(8,128)(2,1)S(1)}, u32[]{:S(2)}, u32[]{:S(2)}) async-start(bf16[8,128,128]{2,1,0:T(8,128)(2,1)} %broadcast_in_dim.4), calls=%async_computation | async-start | bytes 524288 | tf_op jit(solution)/shard_map/all_to_all | solution.py:21
  83.4 3.4 %copy-start.6 = (f32[1024,1024]{0,1:T(8,128)S(1)}, f32[1024,1024]{0,1:T(8,128)}, u32[]{:S(2)}) copy-start(f32[1024,1024]{0,1:T(8,128)} %copy-done.5) | copy-start | bytes 12582916
  95.6 15.1 %all-to-all-start.1 = ((bf16[16,128,128]{2,1,0:T(8,128)(2,1)}), bf16[16,128,128]{2,1,0:T(8,128)(2,1)S(1)}, u32[]{:S(2)}, u32[]{:S(2)}) async-start(bf16[16,128,128]{2,1,0:T(8,128)(2,1)} %broadcast_in_dim.5), calls=%async_computation.1 | async-start | bytes 1048576 | tf_op jit(solution)/shard_map/all_to_all | solution.py:21
  101.4 3.5 %copy-start.4 = (f32[1024,1024]{0,1:T(8,128)S(1)}, f32[1024,1024]{0,1:T(8,128)}, u32[]{:S(2)}) copy-start(f32[1024,1024]{0,1:T(8,128)} %copy-done.3) | copy-start | bytes 12582916
  110.7 7.2 %collective-permute-start.13 = (f32[128,128]{1,0:T(8,128)S(1)}, f32[128,128]{1,0:T(8,128)S(1)}, u32[]{:S(2)}, u32[]{:S(2)}) collective-permute-start(f32[128,128]{1,0:T(8,128)S(1)} %convert_reduce_fusion), channel_id=1, source_target_pairs={{0,1},{1,0},{2,3},{3,2},{4,5},{5,4},{6,7},{7,6},{8,9},{9,8},{10,11... | collective-permute-start | bytes 196616 | tf_op jit(solution)/shard_map/ppermute | solution.py:15

commit v2 on v1

v2 whole, which is shorter than its diff:
```python
import functools
import math

import jax
import jax.numpy as jnp
from jax import lax
from jax.experimental import pallas as pl
from jax.experimental.pallas import tpu as pltpu
from jax.sharding import Mesh, PartitionSpec as P

ALL = ("x", "y", "z", "c")
CHUNK = 256
LOG2E = math.log2(math.e)
F32 = jnp.float32
BF16 = jnp.bfloat16


def bit(i, k):
    return (i >> k) & 1


def far_target(i):
    return i ^ 8 if bit(i, 3) ^ bit(i, 2) ^ bit(i, 0) == 0 else i ^ 4


def near_target(i):
    return i ^ 1 if bit(i, 1) ^ bit(i, 0) == 0 else i ^ 2


def send(x, target):
    return lax.ppermute(x, ALL, [(i, target(i)) for i in range(lax.axis_size(ALL))])


def send_back(x, target):
    return lax.ppermute(x, ALL, [(target(i), i) for i in range(lax.axis_size(ALL))])


def swap_cores(x):
    return lax.ppermute(x, "c", [(0, 1), (1, 0)])


def sum_over(x, axes):
    n = lax.axis_size(axes)
    sent = jnp.broadcast_to(x.astype(BF16), (n,) + x.shape)
    got = lax.all_to_all(sent, axes, 0, 0)
    return jnp.sum(got.astype(F32), axis=0)


def dot(a, b):
    return jnp.dot(a, b, preferred_element_type=F32)


def dot_nt(a, b):
    return lax.dot_general(a, b, (((1,), (1,)), ((), ())), preferred_element_type=F32)


def forward(pts, w_in, w_out):
    hid_t = jnp.tanh(dot_nt(w_in.astype(F32).T.astype(BF16), pts)).astype(BF16)
    feats_t = dot(w_out.astype(F32).T.astype(BF16), hid_t).astype(BF16)
    n = pts.shape[0]
    ones = (lax.broadcasted_iota(jnp.int32, (16, n), 0) == 0).astype(F32).astype(BF16)
    return hid_t, feats_t, jnp.concatenate([feats_t, ones], axis=0)


def half_square(feats, axis, feat):
    return jnp.sum(jnp.square(feats.astype(F32)), axis=axis, keepdims=True) * (-LOG2E / (feat / 4.0))


def kernel_and_weight(rows, row_sq, row_av, col_feats_t, col_sq, col_va, feat):
    inner = dot(rows, col_feats_t)
    kernel = jnp.exp2(inner * (2.0 * LOG2E / (feat / 4.0)) + (row_sq + col_sq))
    weight = dot(row_av, col_va) * kernel
    return kernel.astype(BF16), weight.astype(BF16)


def grad_of(sums, feats_t, feat):
    return (-8.0 / feat) * (sums[feat : feat + 1] * feats_t.astype(F32) - sums[:feat])


def backward(grad_t, hid_t, pts, w_out):
    grad_b = grad_t.astype(BF16)
    g_out = dot_nt(hid_t, grad_b)
    hid = hid_t.astype(F32)
    hid_grad = (dot(w_out, grad_b) * (1.0 - hid * hid)).astype(BF16)
    return dot(hid_grad, pts), g_out


def own_kernel(pts, w_in, w_out, va, av, feats, feats1_t, hid_t, av_t, row_sq, prod, grad):
    feat = w_out.shape[1]
    hid_t[...], feats_t, feats1_t[...] = forward(pts[...], w_in[...], w_out[...])
    feats[...] = feats_t.astype(F32).T.astype(BF16)
    av_t[...] = av[...].astype(F32).T.astype(BF16)
    row_sq[...] = half_square(feats[...], 1, feat)
    col_sq = half_square(feats_t, 0, feat)
    n = pts.shape[0]
    for r in range(0, n, CHUNK):
        here = pl.ds(r, CHUNK)
        kernel, weight = kernel_and_weight(
            feats[here, :], row_sq[here, :], av_t[here, :], feats_t, col_sq, va[...], feat
        )
        prod[:, here] = dot_nt(va[...], kernel)
        sums = dot_nt(feats1_t[...], weight)
        grad[:, here] = grad_of(sums, feats_t[:, r : r + CHUNK], feat)


def pair_kernel(
    last, pts_c, va_c, w_in, w_out, feats, feats1_t, av_t, row_sq, va, prod, grad, *refs
):
    if last:
        hid_t, pts, second, g_in_t, g_out, prod_new, prod_c, keep, give, col_prod, col_sums = refs
    else:
        prod_new, prod_c, grad_new, g_in_new, g_out_new, col_prod, col_sums = refs
    feat = w_out.shape[1]
    hid_c, feats_c, feats1_c = forward(pts_c[...], w_in[...], w_out[...])
    col_sq = half_square(feats_c, 0, feat)
    n = pts_c.shape[0]
    grads = []
    for r in range(0, n, CHUNK):
        here = pl.ds(r, CHUNK)
        kernel, weight = kernel_and_weight(
            feats[here, :], row_sq[here, :], av_t[here, :], feats_c, col_sq, va_c[...], feat
        )
        from_rows = dot(va[:, here], kernel)
        sums_rows = dot(feats1_t[:, here], weight)
        if r == 0:
            col_prod[...] = from_rows
            col_sums[...] = sums_rows
        else:
            col_prod[...] += from_rows
            col_sums[...] += sums_rows
        prod_new[:, here] = prod[:, here] + dot_nt(va_c[...], kernel)
        sums = dot_nt(feats1_c, weight)
        total = grad[:, here] + grad_of(sums, feats1_t[:feat, here], feat)
        if last:
            grads.append(total)
        else:
            grad_new[:, here] = total
    prod_c[...] = col_prod[: prod_c.shape[0]]
    gi_c, go_c = backward(grad_of(col_sums[...], feats_c, feat), hid_c, pts_c[...], w_out[...])
    if not last:
        g_in_new[...] = gi_c
        g_out_new[...] = go_c
        return
    gi, go = backward(jnp.concatenate(grads, axis=1), hid_t[...], pts[...], w_out[...])
    g_in = (g_in_t[...] + gi_c + gi).T
    g_o = g_out[...] + go_c + go
    is_second = second[0] == 1
    keep[...] = jnp.where(is_second, g_o, g_in)
    give[...] = jnp.where(is_second, g_in, g_o)


def call(body, ins, outs, scratch=(), smem=None):
    vmem = pl.BlockSpec(memory_space=pltpu.VMEM)
    specs = [pl.BlockSpec(memory_space=pltpu.SMEM) if i == smem else vmem for i in range(len(ins))]
    return pl.pallas_call(
        body,
        out_shape=[jax.ShapeDtypeStruct(s, d) for s, d in outs],
        in_specs=specs,
        out_specs=[vmem] * len(outs),
        scratch_shapes=[pltpu.VMEM(s, d) for s, d in scratch],
        compiler_params=pltpu.CompilerParams(vmem_limit_bytes=32 * 1024 * 1024),
    )(*ins)


def local(points, w_input, w_output, vectors, adjoint):
    nvec, n = vectors.shape
    feat, hid, din = w_output.shape[1], w_output.shape[0], w_input.shape[0]
    blank = jnp.zeros((-2 * nvec % 8, n), BF16)
    va = jnp.concatenate([vectors, adjoint, blank], axis=0)
    av = jnp.concatenate([adjoint, vectors, blank], axis=0)
    k = va.shape[0]
    far_points, far_va = send(points, far_target), send(va, far_target)
    near_points, near_va = send(points, near_target), send(va, near_target)

    feats, feats1_t, hid_t, av_t, row_sq, prod, grad = call(
        own_kernel,
        (points, w_input, w_output, va, av),
        (
            ((n, feat), BF16),
            ((feat + 16, n), BF16),
            ((hid, n), BF16),
            ((n, k), BF16),
            ((n, 1), F32),
            ((k, n), F32),
            ((feat, n), F32),
        ),
    )
    own = (feats, feats1_t, av_t, row_sq, va)
    scratch = (((k, n), F32), ((feat + 16, n), F32))
    prod, near_back, grad, g_in, g_out = call(
        functools.partial(pair_kernel, False),
        (near_points, near_va, w_input, w_output) + own + (prod, grad),
        (((k, n), F32), ((nvec, n), F32), ((feat, n), F32), ((hid, din), F32), ((hid, feat), F32)),
        scratch,
    )
    near_back = send_back(near_back, near_target)
    second = lax.axis_index("c").astype(jnp.int32).reshape(1)
    ins = (far_points, far_va, w_input, w_output) + own + (prod, grad, hid_t, points, second, g_in, g_out)
    prod, far_back, keep, give = call(
        functools.partial(pair_kernel, True),
        ins,
        (((k, n), F32), ((nvec, n), F32), ((hid, feat), F32), ((hid, feat), F32)),
        scratch,
        smem=13,
    )
    mine = keep + swap_cores(give)
    mine = sum_over(mine, ("z",))
    far_back = send_back(far_back, far_target)
    mine = sum_over(mine, ("x", "y"))
    other = swap_cores(mine)
    is_second = second[0] == 1
    grad_input = jnp.where(is_second, other, mine)
    grad_output = jnp.where(is_second, mine, other)
    products = prod[:nvec] + near_back + far_back
    return (products, grad_input, grad_output)


def solution(mesh):
    grid = Mesh(mesh.devices.reshape(4, 4, 8, 2), ALL)
    return jax.shard_map(
        local,
        mesh=grid,
        in_specs=(P(ALL, None), P(), P(), P(None, ALL), P(None, ALL)),
        out_specs=(P(None, ALL), P(), P()),
        check_vma=False,
    )
```

time: 119 us -> 70.3 us (0.59)
  matrix products: 33.2 us -> 0 us
  waiting for transfers between devices: 44.8 us -> 12.7 us
  blocking collectives: 0 us -> 16.8 us
  starting transfers between devices: 36.8 us -> 22.8 us
  Pallas kernels: 0 us -> 11.8 us
  other arithmetic: 1.07 us -> 2.41 us
    dot_general x24 -> x0, matrix products: 33.2 us -> none  [the longest x5 12.9 us: tile_terms(): lax.dot_general(col_vec, kernel_b, (((1,), (1,)), ((), ())), preferred_el...]
    ppermute x12 -> x6, waiting for transfers between devices: 32.6 us -> 4.18 us  [the longest x4 4.17 us: send(): lax.ppermute(x, ALL, [(i, target(i)) for i in range(lax.axis_size(ALL))])]
    all_to_all x0 -> x1, blocking collectives: none -> 16.8 us  [sum_over(): got = lax.all_to_all(sent, axes, 0, 0)]
    pallas_call x0 -> x3, Pallas kernels: none -> 11.8 us  [call(): pl.pallas_call(body, out_shape=[jax.ShapeDtypeStruct(s, d) for s, d in ou...]
    ppermute x12 -> x6, starting transfers between devices: 20.4 us -> 12.6 us  [the longest x4 10.5 us: send(): lax.ppermute(x, ALL, [(i, target(i)) for i in range(lax.axis_size(ALL))])]
    all_to_all x2 -> x1, starting transfers between devices: 11.4 us -> 6.76 us  [sum_over(): got = lax.all_to_all(sent, axes, 0, 0)]
    all_to_all x2 -> x1, waiting for transfers between devices: 11.3 us -> 7.09 us  [sum_over(): got = lax.all_to_all(sent, axes, 0, 0)]
    ppermute x2, starting transfers between devices: 4.96 us -> 3.41 us  [swap_cores(): return lax.ppermute(x, 'c', [(0, 1), (1, 0)])]
  transfers between devices with their start and end apart: 16 -> 9, of which waited for: 6 -> 4; matrix products, arithmetic and copies ran while one was open for 26% -> 3% of each run, Pallas kernels for 0% -> 10%
where the time goes in v2:
time: 70.3 us; the launch traced here: 69.8 us
  starting transfers between devices  22.8 us (32%)
  blocking collectives  16.8 us (24%)
  waiting for transfers between devices  12.7 us (18%)
  Pallas kernels  11.8 us (17%)
  local copies, waits for them, and re-layouts  2.54 us (4%)
  other arithmetic  2.41 us (3%)
  between operations  0.72 us (1%)
    all_to_all x1, blocking collectives, sum_over(): got = lax.all_to_all(sent, axes, 0, 0)  16.8 us
    pallas_call x3, Pallas kernels, call(): pl.pallas_call(body, out_shape=[jax.ShapeDtypeStruct(s, d) for s, d in ou...  11.8 us
    ppermute x4, starting transfers between devices, send(): lax.ppermute(x, ALL, [(i, target(i)) for i in range(lax.axis_size(ALL))])  10.5 us
    all_to_all x1, waiting for transfers between devices, sum_over(): got = lax.all_to_all(sent, axes, 0, 0)  7.09 us
    all_to_all x1, starting transfers between devices, sum_over(): got = lax.all_to_all(sent, axes, 0, 0)  6.76 us
    ppermute x4, waiting for transfers between devices, send(): lax.ppermute(x, ALL, [(i, target(i)) for i in range(lax.axis_size(ALL))])  4.17 us
    ppermute x2, starting transfers between devices, swap_cores(): return lax.ppermute(x, 'c', [(0, 1), (1, 0)])  3.41 us
    ppermute x2, starting transfers between devices, send_back(): lax.ppermute(x, ALL, [(target(i), i) for i in range(lax.axis_size(ALL))])  2.13 us
  transfers between devices with their start and end apart: 9, of which 4 were waited for; matrix products, arithmetic and copies ran while one was open for 3% of the time, Pallas kernels for 10%

profile of v2, /device:TPU:1, one launch (start us, length us, event | category | flops | bytes accessed | tf_op | source)
XLA Modules:
  0.0 69.8 jit_solution(16254674635210772357)
XLA Ops:
  0.6 0.0 copy-start
  0.6 2.6 %collective-permute-start.2 = (bf16[1024,128]{1,0:T(8,128)(2,1)}, bf16[1024,128]{1,0:T(8,128)(2,1)S(1)}, u32[]{:S(2)}, u32[]{:S(2)}) collective-permute-start(bf16[1024,128]{1,0:T(8,128)(2,1)} %refs_1_.1), channel_id=1, source_target_pairs={{0,1},{1,3},{2,0},{3,2},{4,5},{5,7},{6,4},{7,6},{8,9},{9,11},{10,8... | collective-permute-start | bytes 786440 | tf_op jit(solution)/shard_map/ppermute | solution.py:31
  3.2 3.0 %collective-permute-start = (bf16[1024,128]{1,0:T(8,128)(2,1)}, bf16[1024,128]{1,0:T(8,128)(2,1)S(1)}, u32[]{:S(2)}, u32[]{:S(2)}) collective-permute-start(bf16[1024,128]{1,0:T(8,128)(2,1)} %refs_1_.1), channel_id=1, source_target_pairs={{0,8},{1,5},{2,10},{3,7},{4,0},{5,13},{6,2},{7,15},{8,12},{9,1},{1... | collective-permute-start | bytes 786440 | tf_op jit(solution)/shard_map/ppermute | solution.py:31
  6.2 0.1 pad.5.clone
  6.3 1.0 %maximum_maximum_fusion.1 = (bf16[40,1024]{1,0:T(8,128)(2,1)S(1)}, bf16[40,1024]{1,0:T(8,128)(2,1)S(1)}) fusion(bf16[17,1024]{1,0:T(8,128)(2,1)} %param.8, bf16[17,1024]{1,0:T(8,128)(2,1)} %param.9, bf16[40]{0:T(256)(128)(2,1)S(1)} %pad.5.clone), kind=kLoop, calls=%fused_computation.3 | loop fusion | flops 450560 | bytes 233552 | tf_op jit(solution)/shard_map/concatenate | solution.py:170
  7.2 0.8 %collective-permute-start.3 = (bf16[40,1024]{1,0:T(8,128)(2,1)S(1)}, bf16[40,1024]{1,0:T(8,128)(2,1)S(1)}, u32[]{:S(2)}, u32[]{:S(2)}) collective-permute-start(bf16[40,1024]{1,0:T(8,128)(2,1)S(1)} %get-tuple-element.38.va), channel_id=1, source_target_pairs={{0,1},{1,3},{2,0},{3,2},{4,5},{5,7},{6,4},{7,6},{8,9},{9,11},{10,8... | collective-permute-start | bytes 245768 | tf_op jit(solution)/shard_map/ppermute | solution.py:31
  8.0 4.2 %collective-permute-start.1 = (bf16[40,1024]{1,0:T(8,128)(2,1)S(1)}, bf16[40,1024]{1,0:T(8,128)(2,1)S(1)}, u32[]{:S(2)}, u32[]{:S(2)}) collective-permute-start(bf16[40,1024]{1,0:T(8,128)(2,1)S(1)} %get-tuple-element.38.va), channel_id=1, source_target_pairs={{0,8},{1,5},{2,10},{3,7},{4,0},{5,13},{6,2},{7,15},{8,12},{9,1},{1... | collective-permute-start | bytes 245768 | tf_op jit(solution)/shard_map/ppermute | solution.py:31
  12.2 0.0 copy-done
  12.2 0.8 %copy-done.1 = bf16[128,128]{1,0:T(8,128)(2,1)S(1)} copy-done((bf16[128,128]{1,0:T(8,128)(2,1)S(1)}, bf16[128,128]{1,0:T(8,128)(2,1)}, u32[]{:S(2)}) %copy-start.1) | copy-done | bytes 32792
  13.0 0.8 %copy-done.2 = bf16[128,128]{1,0:T(8,128)(2,1)S(1)} copy-done((bf16[128,128]{1,0:T(8,128)(2,1)S(1)}, bf16[128,128]{1,0:T(8,128)(2,1)}, u32[]{:S(2)}) %copy-start.2) | copy-done | bytes 32792
  13.7 3.1 %shard_map.76 = (bf16[1024,128]{1,0:T(8,128)(2,1)S(1)}, bf16[144,1024]{1,0:T(8,128)(2,1)S(1)}, bf16[128,1024]{1,0:T(8,128)(2,1)S(1)}, bf16[1024,40]{1,0:T(8,128)...) custom-call(bf16[1024,128]{1,0:T(8,128)(2,1)S(1)} %copy-done, ...), custom_call_target="tpu_custom_call" | custom-call | tf_op jit(solution)/shard_map/pallas_call | solution.py:155
  16.8 0.0 collective-permute-done.3.va_c
  16.8 0.0 collective-permute-done.2.pts_c
  16.8 4.3 %shard_map.77 = (f32[40,1024]{1,0:T(8,128)S(1)}, f32[17,1024]{1,0:T(8,128)S(1)}, f32[128,1024]{1,0:T(8,128)S(1)}, f32[128,128]{1,0:T(8,128)S(1)}, f32[128,128]{1,0:T(8,128)S(1)}) custom-call(bf16[1024,128]{1,0:T(8,128)(2,1)S(1)} %collective-permute-done.2.pts_c, bf16[40,1024]{1,0:T(8,128)(2,1)S(1)} %collective-permute-done.3.va_c, ...), custom_call_target="tpu_custom_call" | custom-call | tf_op jit(solution)/shard_map/pallas_call | solution.py:155
  21.1 4.2 %collective-permute-done.1.va_c = bf16[40,1024]{1,0:T(8,128)(2,1)S(1)} collective-permute-done((bf16[40,1024]{1,0:T(8,128)(2,1)S(1)}, bf16[40,1024]{1,0:T(8,128)(2,1)S(1)}, u32[]{:S(2)}, u32[]{:S(2)}) %collective-permute-start.1) | collective-permute-done | bytes 81952 | tf_op jit(solution)/shard_map/ppermute | solution.py:31
  25.3 0.0 collective-permute-done.pts_c
  25.3 4.5 %shard_map.78 = (f32[40,1024]{1,0:T(8,128)S(1)}, f32[17,1024]{1,0:T(8,128)S(1)}, f32[128,128]{1,0:T(8,128)S(1)}, f32[128,128]{1,0:T(8,128)S(1)}) custom-call(bf16[1024,128]{1,0:T(8,128)(2,1)S(1)} %collective-permute-done.pts_c, bf16[40,1024]{1,0:T(8,128)(2,1)S(1)} %collective-permute-done.1.va_c, bf16[128,128]{1,0:T(8,128)(2,1)S(1)} %copy-done.1, ...), custom_call_target="tpu_custom_call" | custom-call | tf_op jit(solution)/shard_map/pallas_call | solution.py:155
  29.8 0.1 collective-permute-start.6
  29.9 1.2 %collective-permute-done.6 = f32[128,128]{1,0:T(8,128)S(1)} collective-permute-done((f32[128,128]{1,0:T(8,128)S(1)}, f32[128,128]{1,0:T(8,128)S(1)}, u32[]{:S(2)}, u32[]{:S(2)}) %collective-permute-start.6) | collective-permute-done | bytes 65568 | tf_op jit(solution)/shard_map/ppermute | solution.py:39
  31.2 16.8 %all_to_all.10 = bf16[8,128,128]{2,1,0:T(8,128)(2,1)S(1)} all-to-all(bf16[8,128,128]{2,1,0:T(8,128)(2,1)S(1)} %broadcast_in_dim.10), channel_id=1, replica_groups=mesh['x'=4,'y'=4,'z'=8,'c'=2] {'z'}, dimensions={0} | all-to-all | bytes 524288 | tf_op jit(solution)/shard_map/all_to_all | solution.py:45
  48.0 0.9 %broadcast_in_dim.11 = bf16[16,128,128]{2,1,0:T(8,128)(2,1)} broadcast(bf16[128,128]{1,0:T(8,128)(2,1)S(1)} %reduce_sum.21), dimensions={1,2} | broadcast | bytes 557056 | tf_op jit(solution)/shard_map/broadcast_in_dim | solution.py:44
  48.9 6.8 %all-to-all-start.1 = ((bf16[16,128,128]{2,1,0:T(8,128)(2,1)}), bf16[16,128,128]{2,1,0:T(8,128)(2,1)S(1)}, u32[]{:S(2)}, u32[]{:S(2)}) async-start(bf16[16,128,128]{2,1,0:T(8,128)(2,1)} %broadcast_in_dim.11), calls=%async_computation.1 | async-start | bytes 1048576 | tf_op jit(solution)/shard_map/all_to_all | solution.py:45
  55.7 0.6 collective-permute-start.5
  56.3 1.5 %collective-permute-start.4 = (f32[17,1024]{1,0:T(8,128)S(1)}, f32[17,1024]{1,0:T(8,128)S(1)}, u32[]{:S(2)}, u32[]{:S(2)}) collective-permute-start(f32[17,1024]{1,0:T(8,128)S(1)} %get-tuple-element.31), channel_id=1, source_target_pairs={{1,0},{3,1},{0,2},{2,3},{5,4},{7,5},{4,6},{6,7},{9,8},{11,9},{8,10... | collective-permute-start | bytes 208904 | tf_op jit(solution)/shard_map/ppermute | solution.py:35
  57.8 7.1 %all-to-all-done.1 = bf16[16,128,128]{2,1,0:T(8,128)(2,1)S(1)} async-done(((bf16[16,128,128]{2,1,0:T(8,128)(2,1)}), bf16[16,128,128]{2,1,0:T(8,128)(2,1)S(1)}, u32[]{:S(2)}, u32[]{:S(2)}) %all-to-all-start.1) | async-done | bytes 524320 | tf_op jit(solution)/shard_map/all_to_all | solution.py:45
  64.9 0.1 convert_reduce_fusion
  65.0 3.3 %collective-permute-start.7 = (f32[128,128]{1,0:T(8,128)S(1)}, f32[128,128]{1,0:T(8,128)S(1)}, u32[]{:S(2)}, u32[]{:S(2)}) collective-permute-start(f32[128,128]{1,0:T(8,128)S(1)} %convert_reduce_fusion), channel_id=1, source_target_pairs={{0,1},{1,0},{2,3},{3,2},{4,5},{5,4},{6,7},{7,6},{8,9},{9,8},{10,11... | collective-permute-start | bytes 196616 | tf_op jit(solution)/shard_map/ppermute | solution.py:39
  68.3 0.0 collective-permute-done.5
  68.3 0.0 collective-permute-done.4
  68.3 0.7 add_add_fusion
  69.0 0.2 collective-permute-done.7
  69.2 0.7 broadcast_select_fusion
  (6 shorter events, 0.1 us)
Async XLA Ops:
  0.6 11.6 %copy-start = (bf16[1024,128]{1,0:T(8,128)(2,1)S(1)}, bf16[1024,128]{1,0:T(8,128)(2,1)}, u32[]{:S(2)}) copy-start(bf16[1024,128]{1,0:T(8,128)(2,1)} %refs_1_.1) | copy-start | bytes 786436
  0.6 16.2 %collective-permute-start.2 = (bf16[1024,128]{1,0:T(8,128)(2,1)}, bf16[1024,128]{1,0:T(8,128)(2,1)S(1)}, u32[]{:S(2)}, u32[]{:S(2)}) collective-permute-start(bf16[1024,128]{1,0:T(8,128)(2,1)} %refs_1_.1), channel_id=1, source_target_pairs={{0,1},{1,3},{2,0},{3,2},{4,5},{5,7},{6,4},{7,6},{8,9},{9,11},{10,8... | collective-permute-start | bytes 786440 | tf_op jit(solution)/shard_map/ppermute | solution.py:31
  3.2 22.1 %collective-permute-start = (bf16[1024,128]{1,0:T(8,128)(2,1)}, bf16[1024,128]{1,0:T(8,128)(2,1)S(1)}, u32[]{:S(2)}, u32[]{:S(2)}) collective-permute-start(bf16[1024,128]{1,0:T(8,128)(2,1)} %refs_1_.1), channel_id=1, source_target_pairs={{0,8},{1,5},{2,10},{3,7},{4,0},{5,13},{6,2},{7,15},{8,12},{9,1},{1... | collective-permute-start | bytes 786440 | tf_op jit(solution)/shard_map/ppermute | solution.py:31
  7.2 9.6 %collective-permute-start.3 = (bf16[40,1024]{1,0:T(8,128)(2,1)S(1)}, bf16[40,1024]{1,0:T(8,128)(2,1)S(1)}, u32[]{:S(2)}, u32[]{:S(2)}) collective-permute-start(bf16[40,1024]{1,0:T(8,128)(2,1)S(1)} %get-tuple-element.38.va), channel_id=1, source_target_pairs={{0,1},{1,3},{2,0},{3,2},{4,5},{5,7},{6,4},{7,6},{8,9},{9,11},{10,8... | collective-permute-start | bytes 245768 | tf_op jit(solution)/shard_map/ppermute | solution.py:31
  8.0 17.3 %collective-permute-start.1 = (bf16[40,1024]{1,0:T(8,128)(2,1)S(1)}, bf16[40,1024]{1,0:T(8,128)(2,1)S(1)}, u32[]{:S(2)}, u32[]{:S(2)}) collective-permute-start(bf16[40,1024]{1,0:T(8,128)(2,1)S(1)} %get-tuple-element.38.va), channel_id=1, source_target_pairs={{0,8},{1,5},{2,10},{3,7},{4,0},{5,13},{6,2},{7,15},{8,12},{9,1},{1... | collective-permute-start | bytes 245768 | tf_op jit(solution)/shard_map/ppermute | solution.py:31
  12.2 0.8 %copy-start.1 = (bf16[128,128]{1,0:T(8,128)(2,1)S(1)}, bf16[128,128]{1,0:T(8,128)(2,1)}, u32[]{:S(2)}) copy-start(bf16[128,128]{1,0:T(8,128)(2,1)} %w_in.5) | copy-start | bytes 98308
  13.0 0.8 %copy-start.2 = (bf16[128,128]{1,0:T(8,128)(2,1)S(1)}, bf16[128,128]{1,0:T(8,128)(2,1)}, u32[]{:S(2)}) copy-start(bf16[128,128]{1,0:T(8,128)(2,1)} %w_out.5) | copy-start | bytes 98308
  29.8 1.3 %collective-permute-start.6 = (f32[128,128]{1,0:T(8,128)S(1)}, f32[128,128]{1,0:T(8,128)S(1)}, u32[]{:S(2)}, u32[]{:S(2)}) collective-permute-start(f32[128,128]{1,0:T(8,128)S(1)} %get-tuple-element.34), channel_id=1, source_target_pairs={{0,1},{1,0},{2,3},{3,2},{4,5},{5,4},{6,7},{7,6},{8,9},{9,8},{10,11... | collective-permute-start | bytes 196616 | tf_op jit(solution)/shard_map/ppermute | solution.py:39
  48.9 16.0 %all-to-all-start.1 = ((bf16[16,128,128]{2,1,0:T(8,128)(2,1)}), bf16[16,128,128]{2,1,0:T(8,128)(2,1)S(1)}, u32[]{:S(2)}, u32[]{:S(2)}) async-start(bf16[16,128,128]{2,1,0:T(8,128)(2,1)} %broadcast_in_dim.11), calls=%async_computation.1 | async-start | bytes 1048576 | tf_op jit(solution)/shard_map/all_to_all | solution.py:45
  55.7 12.6 %collective-permute-start.5 = (f32[17,1024]{1,0:T(8,128)S(1)}, f32[17,1024]{1,0:T(8,128)S(1)}, u32[]{:S(2)}, u32[]{:S(2)}) collective-permute-start(f32[17,1024]{1,0:T(8,128)S(1)} %get-tuple-element.32), channel_id=1, source_target_pairs={{8,0},{5,1},{10,2},{7,3},{0,4},{13,5},{2,6},{15,7},{12,8},{1,9},{1... | collective-permute-start | bytes 208904 | tf_op jit(solution)/shard_map/ppermute | solution.py:35
  56.3 12.0 %collective-permute-start.4 = (f32[17,1024]{1,0:T(8,128)S(1)}, f32[17,1024]{1,0:T(8,128)S(1)}, u32[]{:S(2)}, u32[]{:S(2)}) collective-permute-start(f32[17,1024]{1,0:T(8,128)S(1)} %get-tuple-element.31), channel_id=1, source_target_pairs={{1,0},{3,1},{0,2},{2,3},{5,4},{7,5},{4,6},{6,7},{9,8},{11,9},{8,10... | collective-permute-start | bytes 208904 | tf_op jit(solution)/shard_map/ppermute | solution.py:35
  65.0 4.2 %collective-permute-start.7 = (f32[128,128]{1,0:T(8,128)S(1)}, f32[128,128]{1,0:T(8,128)S(1)}, u32[]{:S(2)}, u32[]{:S(2)}) collective-permute-start(f32[128,128]{1,0:T(8,128)S(1)} %convert_reduce_fusion), channel_id=1, source_target_pairs={{0,1},{1,0},{2,3},{3,2},{4,5},{5,4},{6,7},{7,6},{8,9},{9,8},{10,11... | collective-permute-start | bytes 196616 | tf_op jit(solution)/shard_map/ppermute | solution.py:39

commit v3 on v2

--- a/solution.py
+++ b/solution.py
@@ -45,6 +45,13 @@
     got = lax.all_to_all(sent, axes, 0, 0)
     return jnp.sum(got.astype(F32), axis=0)
 
+
+def join(x, masks):
+    mine = lax.reduce_precision(x, 8, 7)
+    got = [send(mine.astype(BF16), lambda i, m=m: i ^ m).astype(F32) for m in masks]
+    if len(masks) == 1:
+        return mine + got[0]
+    return (mine + got[0]) + (got[1] + got[2])
 
 def dot(a, b):
     return jnp.dot(a, b, preferred_element_type=F32)
@@ -158,7 +165,7 @@
         in_specs=specs,
         out_specs=[vmem] * len(outs),
         scratch_shapes=[pltpu.VMEM(s, d) for s, d in scratch],
-        compiler_params=pltpu.CompilerParams(vmem_limit_bytes=32 * 1024 * 1024),
+        compiler_params=pltpu.CompilerParams(vmem_limit_bytes=16 * 1024 * 1024),
     )(*ins)
 
 
@@ -193,7 +200,6 @@
         (((k, n), F32), ((nvec, n), F32), ((feat, n), F32), ((hid, din), F32), ((hid, feat), F32)),
         scratch,
     )
-    near_back = send_back(near_back, near_target)
     second = lax.axis_index("c").astype(jnp.int32).reshape(1)
     ins = (far_points, far_va, w_input, w_output) + own + (prod, grad, hid_t, points, second, g_in, g_out)
     prod, far_back, keep, give = call(
@@ -204,9 +210,13 @@
         smem=13,
     )
     mine = keep + swap_cores(give)
-    mine = sum_over(mine, ("z",))
+    mine = join(mine, [8])
+    mine, far_back = lax.optimization_barrier((mine, far_back))
     far_back = send_back(far_back, far_target)
-    mine = sum_over(mine, ("x", "y"))
+    mine, near_back = lax.optimization_barrier((mine, near_back))
+    near_back = send_back(near_back, near_target)
+    mine = join(mine, [2, 4, 6])
+    mine = sum_over(mine, ('x', 'y'))
     other = swap_cores(mine)
     is_second = second[0] == 1
     grad_input = jnp.where(is_second, other, mine)

time: 70.3 us -> 67.7 us (0.963)
  blocking collectives: 16.8 us -> 0 us
  starting transfers between devices: 22.8 us -> 36 us
  waiting for transfers between devices: 12.7 us -> 13.8 us
    all_to_all x1 -> x0, blocking collectives: 16.8 us -> none  [sum_over(): got = lax.all_to_all(sent, axes, 0, 0)]
    ppermute x4 -> x8, waiting for transfers between devices: 4.17 us -> 11.1 us  [send(): lax.ppermute(x, ALL, [(i, target(i)) for i in range(lax.axis_size(ALL))])]
    ppermute x4 -> x8, starting transfers between devices: 10.5 us -> 17.1 us  [send(): lax.ppermute(x, ALL, [(i, target(i)) for i in range(lax.axis_size(ALL))])]
    all_to_all x1, waiting for transfers between devices: 7.09 us -> 1.24 us  [sum_over(): got = lax.all_to_all(sent, axes, 0, 0)]
    ppermute x2, starting transfers between devices: 2.13 us -> 7.71 us  [send_back(): lax.ppermute(x, ALL, [(target(i), i) for i in range(lax.axis_size(ALL))])]
    ppermute x2, starting transfers between devices: 3.41 us -> 4.47 us  [swap_cores(): return lax.ppermute(x, 'c', [(0, 1), (1, 0)])]
  transfers between devices with their start and end apart: 9 -> 13, of which waited for: 4 -> 8; matrix products, arithmetic and copies ran while one was open for 3% -> 3% of each run, Pallas kernels for 10% -> 11%
where the time goes in v3:
time: 67.7 us; the launch traced here: 67.3 us
  starting transfers between devices  36 us (53%)
  waiting for transfers between devices  13.8 us (20%)
  Pallas kernels  11.8 us (17%)
  local copies, waits for them, and re-layouts  2.5 us (4%)
  other arithmetic  2.42 us (4%)
  between operations  0.73 us (1%)
    ppermute x8, starting transfers between devices, send(): lax.ppermute(x, ALL, [(i, target(i)) for i in range(lax.axis_size(ALL))])  17.1 us
    pallas_call x3, Pallas kernels, call(): pl.pallas_call(body, out_shape=[jax.ShapeDtypeStruct(s, d) for s, d in ou...  11.8 us
    ppermute x8, waiting for transfers between devices, send(): lax.ppermute(x, ALL, [(i, target(i)) for i in range(lax.axis_size(ALL))])  11.1 us
    ppermute x2, starting transfers between devices, send_back(): lax.ppermute(x, ALL, [(target(i), i) for i in range(lax.axis_size(ALL))])  7.71 us
    all_to_all x1, starting transfers between devices, sum_over(): got = lax.all_to_all(sent, axes, 0, 0)  6.75 us
    ppermute x2, starting transfers between devices, swap_cores(): return lax.ppermute(x, 'c', [(0, 1), (1, 0)])  4.47 us
    unnamed x6, local copies, waits for them, and re-layouts  1.52 us
    ppermute x2, waiting for transfers between devices, swap_cores(): return lax.ppermute(x, 'c', [(0, 1), (1, 0)])  1.48 us
  transfers between devices with their start and end apart: 13, of which 8 were waited for; matrix products, arithmetic and copies ran while one was open for 3% of the time, Pallas kernels for 11%

profile of v3, /device:TPU:1, one launch (start us, length us, event | category | flops | bytes accessed | tf_op | source)
XLA Modules:
  0.0 67.3 jit_solution(4536524208884059752)
XLA Ops:
  0.6 2.6 %collective-permute-start.2 = (bf16[1024,128]{1,0:T(8,128)(2,1)}, bf16[1024,128]{1,0:T(8,128)(2,1)S(1)}, u32[]{:S(2)}, u32[]{:S(2)}) collective-permute-start(bf16[1024,128]{1,0:T(8,128)(2,1)} %refs_1_.1), channel_id=1, source_target_pairs={{0,1},{1,3},{2,0},{3,2},{4,5},{5,7},{6,4},{7,6},{8,9},{9,11},{10,8... | collective-permute-start | bytes 786440 | tf_op jit(solution)/shard_map/ppermute | solution.py:31
  3.2 3.0 %collective-permute-start = (bf16[1024,128]{1,0:T(8,128)(2,1)}, bf16[1024,128]{1,0:T(8,128)(2,1)S(1)}, u32[]{:S(2)}, u32[]{:S(2)}) collective-permute-start(bf16[1024,128]{1,0:T(8,128)(2,1)} %refs_1_.1), channel_id=1, source_target_pairs={{0,8},{1,5},{2,10},{3,7},{4,0},{5,13},{6,2},{7,15},{8,12},{9,1},{1... | collective-permute-start | bytes 786440 | tf_op jit(solution)/shard_map/ppermute | solution.py:31
  6.2 0.1 pad.5.clone
  6.3 1.0 %maximum_maximum_fusion.1 = (bf16[40,1024]{1,0:T(8,128)(2,1)S(1)}, bf16[40,1024]{1,0:T(8,128)(2,1)S(1)}) fusion(bf16[17,1024]{1,0:T(8,128)(2,1)} %param.8, bf16[17,1024]{1,0:T(8,128)(2,1)} %param.9, bf16[40]{0:T(256)(128)(2,1)S(1)} %pad.5.clone), kind=kLoop, calls=%fused_computation.3 | loop fusion | flops 450560 | bytes 233552 | tf_op jit(solution)/shard_map/concatenate | solution.py:177
  7.2 0.8 %collective-permute-start.3 = (bf16[40,1024]{1,0:T(8,128)(2,1)S(1)}, bf16[40,1024]{1,0:T(8,128)(2,1)S(1)}, u32[]{:S(2)}, u32[]{:S(2)}) collective-permute-start(bf16[40,1024]{1,0:T(8,128)(2,1)S(1)} %get-tuple-element.46.va), channel_id=1, source_target_pairs={{0,1},{1,3},{2,0},{3,2},{4,5},{5,7},{6,4},{7,6},{8,9},{9,11},{10,8... | collective-permute-start | bytes 245768 | tf_op jit(solution)/shard_map/ppermute | solution.py:31
  8.0 4.2 %collective-permute-start.1 = (bf16[40,1024]{1,0:T(8,128)(2,1)S(1)}, bf16[40,1024]{1,0:T(8,128)(2,1)S(1)}, u32[]{:S(2)}, u32[]{:S(2)}) collective-permute-start(bf16[40,1024]{1,0:T(8,128)(2,1)S(1)} %get-tuple-element.46.va), channel_id=1, source_target_pairs={{0,8},{1,5},{2,10},{3,7},{4,0},{5,13},{6,2},{7,15},{8,12},{9,1},{1... | collective-permute-start | bytes 245768 | tf_op jit(solution)/shard_map/ppermute | solution.py:31
  12.2 0.8 %copy-done.1 = bf16[128,128]{1,0:T(8,128)(2,1)S(1)} copy-done((bf16[128,128]{1,0:T(8,128)(2,1)S(1)}, bf16[128,128]{1,0:T(8,128)(2,1)}, u32[]{:S(2)}) %copy-start.1) | copy-done | bytes 32792
  13.0 0.8 %copy-done.2 = bf16[128,128]{1,0:T(8,128)(2,1)S(1)} copy-done((bf16[128,128]{1,0:T(8,128)(2,1)S(1)}, bf16[128,128]{1,0:T(8,128)(2,1)}, u32[]{:S(2)}) %copy-start.2) | copy-done | bytes 32792
  13.7 3.1 %shard_map.76 = (bf16[1024,128]{1,0:T(8,128)(2,1)S(1)}, bf16[144,1024]{1,0:T(8,128)(2,1)S(1)}, bf16[128,1024]{1,0:T(8,128)(2,1)S(1)}, bf16[1024,40]{1,0:T(8,128)...) custom-call(bf16[1024,128]{1,0:T(8,128)(2,1)S(1)} %copy-done, ...), custom_call_target="tpu_custom_call" | custom-call | tf_op jit(solution)/shard_map/pallas_call | solution.py:162
  16.8 0.0 collective-permute-done.3.va_c
  16.8 4.3 %shard_map.77 = (f32[40,1024]{1,0:T(8,128)S(1)}, f32[17,1024]{1,0:T(8,128)S(1)}, f32[128,1024]{1,0:T(8,128)S(1)}, f32[128,128]{1,0:T(8,128)S(1)}, f32[128,128]{1,0:T(8,128)S(1)}) custom-call(bf16[1024,128]{1,0:T(8,128)(2,1)S(1)} %collective-permute-done.2.pts_c, bf16[40,1024]{1,0:T(8,128)(2,1)S(1)} %collective-permute-done.3.va_c, ...), custom_call_target="tpu_custom_call" | custom-call | tf_op jit(solution)/shard_map/pallas_call | solution.py:162
  21.1 4.2 %collective-permute-done.1.va_c = bf16[40,1024]{1,0:T(8,128)(2,1)S(1)} collective-permute-done((bf16[40,1024]{1,0:T(8,128)(2,1)S(1)}, bf16[40,1024]{1,0:T(8,128)(2,1)S(1)}, u32[]{:S(2)}, u32[]{:S(2)}) %collective-permute-start.1) | collective-permute-done | bytes 81952 | tf_op jit(solution)/shard_map/ppermute | solution.py:31
  25.3 4.5 %shard_map.78 = (f32[40,1024]{1,0:T(8,128)S(1)}, f32[17,1024]{1,0:T(8,128)S(1)}, f32[128,128]{1,0:T(8,128)S(1)}, f32[128,128]{1,0:T(8,128)S(1)}) custom-call(bf16[1024,128]{1,0:T(8,128)(2,1)S(1)} %collective-permute-done.pts_c, bf16[40,1024]{1,0:T(8,128)(2,1)S(1)} %collective-permute-done.1.va_c, bf16[128,128]{1,0:T(8,128)(2,1)S(1)} %copy-done.1, ...), custom_call_target="tpu_custom_call" | custom-call | tf_op jit(solution)/shard_map/pallas_call | solution.py:162
  29.8 0.1 collective-permute-start.4
  29.9 1.2 %collective-permute-done.4 = f32[128,128]{1,0:T(8,128)S(1)} collective-permute-done((f32[128,128]{1,0:T(8,128)S(1)}, f32[128,128]{1,0:T(8,128)S(1)}, u32[]{:S(2)}, u32[]{:S(2)}) %collective-permute-start.4) | collective-permute-done | bytes 65568 | tf_op jit(solution)/shard_map/ppermute | solution.py:39
  31.1 3.0 %collective-permute-start.5 = (bf16[128,128]{1,0:T(8,128)(2,1)S(1)}, bf16[128,128]{1,0:T(8,128)(2,1)S(1)}, u32[]{:S(2)}, u32[]{:S(2)}) collective-permute-start(bf16[128,128]{1,0:T(8,128)(2,1)S(1)} %fusion), channel_id=1, source_target_pairs={{0,8},{1,9},{2,10},{3,11},{4,12},{5,13},{6,14},{7,15},{8,0},{9,1},... | collective-permute-start | bytes 98312 | tf_op jit(solution)/shard_map/ppermute | solution.py:31
  34.1 3.8 %collective-permute-done.5 = bf16[128,128]{1,0:T(8,128)(2,1)S(1)} collective-permute-done((bf16[128,128]{1,0:T(8,128)(2,1)S(1)}, bf16[128,128]{1,0:T(8,128)(2,1)S(1)}, u32[]{:S(2)}, u32[]{:S(2)}) %collective-permute-start.5) | collective-permute-done | bytes 32800 | tf_op jit(solution)/shard_map/ppermute | solution.py:31
  37.9 3.0 %collective-permute-start.10 = (bf16[128,128]{1,0:T(8,128)(2,1)S(1)}, bf16[128,128]{1,0:T(8,128)(2,1)S(1)}, u32[]{:S(2)}, u32[]{:S(2)}) collective-permute-start(bf16[128,128]{1,0:T(8,128)(2,1)S(1)} %reduce-precision_convert_fusion), channel_id=1, source_target_pairs={{0,6},{1,7},{2,4},{3,5},{4,2},{5,3},{6,0},{7,1},{8,14},{9,15},{10,... | collective-permute-start | bytes 98312 | tf_op jit(solution)/shard_map/ppermute | solution.py:31
  41.0 0.6 collective-permute-start.9
  41.6 1.0 %collective-permute-done.10 = bf16[128,128]{1,0:T(8,128)(2,1)S(1)} collective-permute-done((bf16[128,128]{1,0:T(8,128)(2,1)S(1)}, bf16[128,128]{1,0:T(8,128)(2,1)S(1)}, u32[]{:S(2)}, u32[]{:S(2)}) %collective-permute-start.10) | collective-permute-done | bytes 32800 | tf_op jit(solution)/shard_map/ppermute | solution.py:31
  42.6 1.4 %collective-permute-done.8 = bf16[128,128]{1,0:T(8,128)(2,1)S(1)} collective-permute-done((bf16[128,128]{1,0:T(8,128)(2,1)S(1)}, bf16[128,128]{1,0:T(8,128)(2,1)S(1)}, u32[]{:S(2)}, u32[]{:S(2)}) %collective-permute-start.8) | collective-permute-done | bytes 32800 | tf_op jit(solution)/shard_map/ppermute | solution.py:31
  44.0 0.7 %collective-permute-done.9 = bf16[128,128]{1,0:T(8,128)(2,1)S(1)} collective-permute-done((bf16[128,128]{1,0:T(8,128)(2,1)S(1)}, bf16[128,128]{1,0:T(8,128)(2,1)S(1)}, u32[]{:S(2)}, u32[]{:S(2)}) %collective-permute-start.9) | collective-permute-done | bytes 32800 | tf_op jit(solution)/shard_map/ppermute | solution.py:31
  44.7 0.9 %broadcast_in_dim.7 = bf16[16,128,128]{2,1,0:T(8,128)(2,1)} broadcast(bf16[128,128]{1,0:T(8,128)(2,1)S(1)} %add_convert_fusion), dimensions={1,2} | broadcast | bytes 557056 | tf_op jit(solution)/shard_map/broadcast_in_dim | solution.py:44
  45.6 6.8 %all-to-all-start = ((bf16[16,128,128]{2,1,0:T(8,128)(2,1)}), bf16[16,128,128]{2,1,0:T(8,128)(2,1)S(1)}, u32[]{:S(2)}, u32[]{:S(2)}) async-start(bf16[16,128,128]{2,1,0:T(8,128)(2,1)} %broadcast_in_dim.7), calls=%async_computation | async-start | bytes 1048576 | tf_op jit(solution)/shard_map/all_to_all | solution.py:45
  52.4 3.2 %collective-permute-start.6 = (f32[17,1024]{1,0:T(8,128)S(1)}, f32[17,1024]{1,0:T(8,128)S(1)}, u32[]{:S(2)}, u32[]{:S(2)}) collective-permute-start(f32[17,1024]{1,0:T(8,128)S(1)} %get-tuple-element.40), channel_id=1, source_target_pairs={{1,0},{3,1},{0,2},{2,3},{5,4},{7,5},{4,6},{6,7},{9,8},{11,9},{8,10... | collective-permute-start | bytes 208904 | tf_op jit(solution)/shard_map/ppermute | solution.py:35
  55.6 4.5 %collective-permute-start.7 = (f32[17,1024]{1,0:T(8,128)S(1)}, f32[17,1024]{1,0:T(8,128)S(1)}, u32[]{:S(2)}, u32[]{:S(2)}) collective-permute-start(f32[17,1024]{1,0:T(8,128)S(1)} %get-tuple-element.41), channel_id=1, source_target_pairs={{8,0},{5,1},{10,2},{7,3},{0,4},{13,5},{2,6},{15,7},{12,8},{1,9},{1... | collective-permute-start | bytes 208904 | tf_op jit(solution)/shard_map/ppermute | solution.py:35
  60.1 1.2 %all-to-all-done = bf16[16,128,128]{2,1,0:T(8,128)(2,1)S(1)} async-done(((bf16[16,128,128]{2,1,0:T(8,128)(2,1)}), bf16[16,128,128]{2,1,0:T(8,128)(2,1)S(1)}, u32[]{:S(2)}, u32[]{:S(2)}) %all-to-all-start) | async-done | bytes 524320 | tf_op jit(solution)/shard_map/all_to_all | solution.py:45
  61.3 0.1 convert_reduce_fusion
  61.4 4.4 %collective-permute-start.11 = (f32[128,128]{1,0:T(8,128)S(1)}, f32[128,128]{1,0:T(8,128)S(1)}, u32[]{:S(2)}, u32[]{:S(2)}) collective-permute-start(f32[128,128]{1,0:T(8,128)S(1)} %convert_reduce_fusion), channel_id=1, source_target_pairs={{0,1},{1,0},{2,3},{3,2},{4,5},{5,4},{6,7},{7,6},{8,9},{9,8},{10,11... | collective-permute-start | bytes 196616 | tf_op jit(solution)/shard_map/ppermute | solution.py:39
  65.8 0.7 add_add_fusion
  66.4 0.2 collective-permute-done.11
  66.7 0.7 broadcast_select_fusion
  (14 shorter events, 0.1 us)
Async XLA Ops:
  0.6 11.6 %copy-start = (bf16[1024,128]{1,0:T(8,128)(2,1)S(1)}, bf16[1024,128]{1,0:T(8,128)(2,1)}, u32[]{:S(2)}) copy-start(bf16[1024,128]{1,0:T(8,128)(2,1)} %refs_1_.1) | copy-start | bytes 786436
  0.6 16.2 %collective-permute-start.2 = (bf16[1024,128]{1,0:T(8,128)(2,1)}, bf16[1024,128]{1,0:T(8,128)(2,1)S(1)}, u32[]{:S(2)}, u32[]{:S(2)}) collective-permute-start(bf16[1024,128]{1,0:T(8,128)(2,1)} %refs_1_.1), channel_id=1, source_target_pairs={{0,1},{1,3},{2,0},{3,2},{4,5},{5,7},{6,4},{7,6},{8,9},{9,11},{10,8... | collective-permute-start | bytes 786440 | tf_op jit(solution)/shard_map/ppermute | solution.py:31
  3.2 22.1 %collective-permute-start = (bf16[1024,128]{1,0:T(8,128)(2,1)}, bf16[1024,128]{1,0:T(8,128)(2,1)S(1)}, u32[]{:S(2)}, u32[]{:S(2)}) collective-permute-start(bf16[1024,128]{1,0:T(8,128)(2,1)} %refs_1_.1), channel_id=1, source_target_pairs={{0,8},{1,5},{2,10},{3,7},{4,0},{5,13},{6,2},{7,15},{8,12},{9,1},{1... | collective-permute-start | bytes 786440 | tf_op jit(solution)/shard_map/ppermute | solution.py:31
  7.2 9.6 %collective-permute-start.3 = (bf16[40,1024]{1,0:T(8,128)(2,1)S(1)}, bf16[40,1024]{1,0:T(8,128)(2,1)S(1)}, u32[]{:S(2)}, u32[]{:S(2)}) collective-permute-start(bf16[40,1024]{1,0:T(8,128)(2,1)S(1)} %get-tuple-element.46.va), channel_id=1, source_target_pairs={{0,1},{1,3},{2,0},{3,2},{4,5},{5,7},{6,4},{7,6},{8,9},{9,11},{10,8... | collective-permute-start | bytes 245768 | tf_op jit(solution)/shard_map/ppermute | solution.py:31
  8.0 17.3 %collective-permute-start.1 = (bf16[40,1024]{1,0:T(8,128)(2,1)S(1)}, bf16[40,1024]{1,0:T(8,128)(2,1)S(1)}, u32[]{:S(2)}, u32[]{:S(2)}) collective-permute-start(bf16[40,1024]{1,0:T(8,128)(2,1)S(1)} %get-tuple-element.46.va), channel_id=1, source_target_pairs={{0,8},{1,5},{2,10},{3,7},{4,0},{5,13},{6,2},{7,15},{8,12},{9,1},{1... | collective-permute-start | bytes 245768 | tf_op jit(solution)/shard_map/ppermute | solution.py:31
  12.2 0.8 %copy-start.1 = (bf16[128,128]{1,0:T(8,128)(2,1)S(1)}, bf16[128,128]{1,0:T(8,128)(2,1)}, u32[]{:S(2)}) copy-start(bf16[128,128]{1,0:T(8,128)(2,1)} %w_in.5) | copy-start | bytes 98308
  13.0 0.8 %copy-start.2 = (bf16[128,128]{1,0:T(8,128)(2,1)S(1)}, bf16[128,128]{1,0:T(8,128)(2,1)}, u32[]{:S(2)}) copy-start(bf16[128,128]{1,0:T(8,128)(2,1)} %w_out.5) | copy-start | bytes 98308
  29.8 1.3 %collective-permute-start.4 = (f32[128,128]{1,0:T(8,128)S(1)}, f32[128,128]{1,0:T(8,128)S(1)}, u32[]{:S(2)}, u32[]{:S(2)}) collective-permute-start(f32[128,128]{1,0:T(8,128)S(1)} %get-tuple-element.36), channel_id=1, source_target_pairs={{0,1},{1,0},{2,3},{3,2},{4,5},{5,4},{6,7},{7,6},{8,9},{9,8},{10,11... | collective-permute-start | bytes 196616 | tf_op jit(solution)/shard_map/ppermute | solution.py:39
  31.1 6.8 %collective-permute-start.5 = (bf16[128,128]{1,0:T(8,128)(2,1)S(1)}, bf16[128,128]{1,0:T(8,128)(2,1)S(1)}, u32[]{:S(2)}, u32[]{:S(2)}) collective-permute-start(bf16[128,128]{1,0:T(8,128)(2,1)S(1)} %fusion), channel_id=1, source_target_pairs={{0,8},{1,9},{2,10},{3,11},{4,12},{5,13},{6,14},{7,15},{8,0},{9,1},... | collective-permute-start | bytes 98312 | tf_op jit(solution)/shard_map/ppermute | solution.py:31
  37.9 4.7 %collective-permute-start.10 = (bf16[128,128]{1,0:T(8,128)(2,1)S(1)}, bf16[128,128]{1,0:T(8,128)(2,1)S(1)}, u32[]{:S(2)}, u32[]{:S(2)}) collective-permute-start(bf16[128,128]{1,0:T(8,128)(2,1)S(1)} %reduce-precision_convert_fusion), channel_id=1, source_target_pairs={{0,6},{1,7},{2,4},{3,5},{4,2},{5,3},{6,0},{7,1},{8,14},{9,15},{10,... | collective-permute-start | bytes 98312 | tf_op jit(solution)/shard_map/ppermute | solution.py:31
  41.0 3.1 %collective-permute-start.8 = (bf16[128,128]{1,0:T(8,128)(2,1)S(1)}, bf16[128,128]{1,0:T(8,128)(2,1)S(1)}, u32[]{:S(2)}, u32[]{:S(2)}) collective-permute-start(bf16[128,128]{1,0:T(8,128)(2,1)S(1)} %reduce-precision_convert_fusion), channel_id=1, source_target_pairs={{0,2},{1,3},{2,0},{3,1},{4,6},{5,7},{6,4},{7,5},{8,10},{9,11},{10,... | collective-permute-start | bytes 98312 | tf_op jit(solution)/shard_map/ppermute | solution.py:31
  41.0 3.7 %collective-permute-start.9 = (bf16[128,128]{1,0:T(8,128)(2,1)S(1)}, bf16[128,128]{1,0:T(8,128)(2,1)S(1)}, u32[]{:S(2)}, u32[]{:S(2)}) collective-permute-start(bf16[128,128]{1,0:T(8,128)(2,1)S(1)} %reduce-precision_convert_fusion), channel_id=1, source_target_pairs={{0,4},{1,5},{2,6},{3,7},{4,0},{5,1},{6,2},{7,3},{8,12},{9,13},{10,... | collective-permute-start | bytes 98312 | tf_op jit(solution)/shard_map/ppermute | solution.py:31
  45.6 15.7 %all-to-all-start = ((bf16[16,128,128]{2,1,0:T(8,128)(2,1)}), bf16[16,128,128]{2,1,0:T(8,128)(2,1)S(1)}, u32[]{:S(2)}, u32[]{:S(2)}) async-start(bf16[16,128,128]{2,1,0:T(8,128)(2,1)} %broadcast_in_dim.7), calls=%async_computation | async-start | bytes 1048576 | tf_op jit(solution)/shard_map/all_to_all | solution.py:45
  52.4 13.4 %collective-permute-start.6 = (f32[17,1024]{1,0:T(8,128)S(1)}, f32[17,1024]{1,0:T(8,128)S(1)}, u32[]{:S(2)}, u32[]{:S(2)}) collective-permute-start(f32[17,1024]{1,0:T(8,128)S(1)} %get-tuple-element.40), channel_id=1, source_target_pairs={{1,0},{3,1},{0,2},{2,3},{5,4},{7,5},{4,6},{6,7},{9,8},{11,9},{8,10... | collective-permute-start | bytes 208904 | tf_op jit(solution)/shard_map/ppermute | solution.py:35
  55.6 10.2 %collective-permute-start.7 = (f32[17,1024]{1,0:T(8,128)S(1)}, f32[17,1024]{1,0:T(8,128)S(1)}, u32[]{:S(2)}, u32[]{:S(2)}) collective-permute-start(f32[17,1024]{1,0:T(8,128)S(1)} %get-tuple-element.41), channel_id=1, source_target_pairs={{8,0},{5,1},{10,2},{7,3},{0,4},{13,5},{2,6},{15,7},{12,8},{1,9},{1... | collective-permute-start | bytes 208904 | tf_op jit(solution)/shard_map/ppermute | solution.py:35
  61.4 5.3 %collective-permute-start.11 = (f32[128,128]{1,0:T(8,128)S(1)}, f32[128,128]{1,0:T(8,128)S(1)}, u32[]{:S(2)}, u32[]{:S(2)}) collective-permute-start(f32[128,128]{1,0:T(8,128)S(1)} %convert_reduce_fusion), channel_id=1, source_target_pairs={{0,1},{1,0},{2,3},{3,2},{4,5},{5,4},{6,7},{7,6},{8,9},{9,8},{10,11... | collective-permute-start | bytes 196616 | tf_op jit(solution)/shard_map/ppermute | solution.py:39

commit v4 on v3

--- a/solution.py
+++ b/solution.py
@@ -61,9 +61,13 @@
     return lax.dot_general(a, b, (((1,), (1,)), ((), ())), preferred_element_type=F32)
 
 
-def forward(pts, w_in, w_out):
-    hid_t = jnp.tanh(dot_nt(w_in.astype(F32).T.astype(BF16), pts)).astype(BF16)
-    feats_t = dot(w_out.astype(F32).T.astype(BF16), hid_t).astype(BF16)
+def transposed(x):
+    return x.astype(F32).T.astype(BF16)
+
+
+def forward(pts, w_in_t, w_out_t):
+    hid_t = jnp.tanh(dot_nt(w_in_t, pts)).astype(BF16)
+    feats_t = dot(w_out_t, hid_t).astype(BF16)
     n = pts.shape[0]
     ones = (lax.broadcasted_iota(jnp.int32, (16, n), 0) == 0).astype(F32).astype(BF16)
     return hid_t, feats_t, jnp.concatenate([feats_t, ones], axis=0)
@@ -73,11 +77,9 @@
     return jnp.sum(jnp.square(feats.astype(F32)), axis=axis, keepdims=True) * (-LOG2E / (feat / 4.0))
 
 
-def kernel_and_weight(rows, row_sq, row_av, col_feats_t, col_sq, col_va, feat):
+def kernel_rows(rows, row_sq, col_feats_t, col_sq, feat):
     inner = dot(rows, col_feats_t)
-    kernel = jnp.exp2(inner * (2.0 * LOG2E / (feat / 4.0)) + (row_sq + col_sq))
-    weight = dot(row_av, col_va) * kernel
-    return kernel.astype(BF16), weight.astype(BF16)
+    return jnp.exp2(inner * (2.0 * LOG2E / (feat / 4.0)) + (row_sq + col_sq))
 
 
 def grad_of(sums, feats_t, feat):
@@ -92,58 +94,67 @@
     return dot(hid_grad, pts), g_out
 
 
-def own_kernel(pts, w_in, w_out, va, av, feats, feats1_t, hid_t, av_t, row_sq, prod, grad):
+def own_kernel(
+    pts, w_in, w_out, va, av, w_in_t, w_out_t, feats, feats1_t, hid_t, av_t, row_sq, prod, grad
+):
     feat = w_out.shape[1]
-    hid_t[...], feats_t, feats1_t[...] = forward(pts[...], w_in[...], w_out[...])
-    feats[...] = feats_t.astype(F32).T.astype(BF16)
-    av_t[...] = av[...].astype(F32).T.astype(BF16)
+    w_in_t[...] = transposed(w_in[...])
+    w_out_t[...] = transposed(w_out[...])
+    hid_t[...], feats_t, feats1_t[...] = forward(pts[...], w_in_t[...], w_out_t[...])
+    feats[...] = transposed(feats_t)
+    av_t[...] = transposed(av[...])
     row_sq[...] = half_square(feats[...], 1, feat)
     col_sq = half_square(feats_t, 0, feat)
     n = pts.shape[0]
     for r in range(0, n, CHUNK):
         here = pl.ds(r, CHUNK)
-        kernel, weight = kernel_and_weight(
-            feats[here, :], row_sq[here, :], av_t[here, :], feats_t, col_sq, va[...], feat
-        )
-        prod[:, here] = dot_nt(va[...], kernel)
+        kernel = kernel_rows(feats[here, :], row_sq[here, :], feats_t, col_sq, feat)
+        weight = (dot(av_t[here, :], va[...]) * kernel).astype(BF16)
+        prod[:, here] = dot_nt(va[...], kernel.astype(BF16))
         sums = dot_nt(feats1_t[...], weight)
         grad[:, here] = grad_of(sums, feats_t[:, r : r + CHUNK], feat)
 
 
+def meet_kernel(pts_c, w_in_t, w_out_t, feats, row_sq, va, hid_c, feats1_c, kernel, prod_c):
+    n, feat = feats.shape
+    hid_c[...], feats_c, feats1_c[...] = forward(pts_c[...], w_in_t[...], w_out_t[...])
+    col_sq = half_square(feats_c, 0, feat)
+    for r in range(0, n, CHUNK):
+        here = pl.ds(r, CHUNK)
+        kernel[here, :] = kernel_rows(
+            feats[here, :], row_sq[here, :], feats_c, col_sq, feat
+        ).astype(BF16)
+    for r in range(0, n, CHUNK):
+        here = pl.ds(r, CHUNK)
+        prod_c[:, here] = dot(va[...], kernel[:, here])[: prod_c.shape[0]]
+
+
 def pair_kernel(
-    last, pts_c, va_c, w_in, w_out, feats, feats1_t, av_t, row_sq, va, prod, grad, *refs
+    last, pts_c, va_c, hid_c, feats1_c, kernel, w_out, feats1_t, av_t, prod, grad, *refs
 ):
     if last:
-        hid_t, pts, second, g_in_t, g_out, prod_new, prod_c, keep, give, col_prod, col_sums = refs
+        hid_t, pts, second, g_in_t, g_out, prod_new, keep, give, weight = refs
     else:
-        prod_new, prod_c, grad_new, g_in_new, g_out_new, col_prod, col_sums = refs
+        prod_new, grad_new, g_in_new, g_out_new, weight = refs
     feat = w_out.shape[1]
-    hid_c, feats_c, feats1_c = forward(pts_c[...], w_in[...], w_out[...])
-    col_sq = half_square(feats_c, 0, feat)
     n = pts_c.shape[0]
     grads = []
     for r in range(0, n, CHUNK):
         here = pl.ds(r, CHUNK)
-        kernel, weight = kernel_and_weight(
-            feats[here, :], row_sq[here, :], av_t[here, :], feats_c, col_sq, va_c[...], feat
-        )
-        from_rows = dot(va[:, here], kernel)
-        sums_rows = dot(feats1_t[:, here], weight)
-        if r == 0:
-            col_prod[...] = from_rows
-            col_sums[...] = sums_rows
-        else:
-            col_prod[...] += from_rows
-            col_sums[...] += sums_rows
-        prod_new[:, here] = prod[:, here] + dot_nt(va_c[...], kernel)
-        sums = dot_nt(feats1_c, weight)
+        pairing = dot(av_t[here, :], va_c[...])
+        weight[here, :] = (pairing * kernel[here, :].astype(F32)).astype(BF16)
+        prod_new[:, here] = prod[:, here] + dot_nt(va_c[...], kernel[here, :])
+        sums = dot_nt(feats1_c[...], weight[here, :])
         total = grad[:, here] + grad_of(sums, feats1_t[:feat, here], feat)
         if last:
             grads.append(total)
         else:
             grad_new[:, here] = total
-    prod_c[...] = col_prod[: prod_c.shape[0]]
-    gi_c, go_c = backward(grad_of(col_sums[...], feats_c, feat), hid_c, pts_c[...], w_out[...])
+    grads_c = []
+    for r in range(0, n, CHUNK):
+        here = pl.ds(r, CHUNK)
+        grads_c.append(grad_of(dot(feats1_t[...], weight[:, here]), feats1_c[:feat, here], feat))
+    gi_c, go_c = backward(jnp.concatenate(grads_c, axis=1), hid_c[...], pts_c[...], w_out[...])
     if not last:
         g_in_new[...] = gi_c
         g_out_new[...] = go_c
@@ -179,10 +190,12 @@
     far_points, far_va = send(points, far_target), send(va, far_target)
     near_points, near_va = send(points, near_target), send(va, near_target)
 
-    feats, feats1_t, hid_t, av_t, row_sq, prod, grad = call(
+    w_in_t, w_out_t, feats, feats1_t, hid_t, av_t, row_sq, prod, grad = call(
         own_kernel,
         (points, w_input, w_output, va, av),
         (
+            ((hid, din), BF16),
+            ((feat, hid), BF16),
             ((n, feat), BF16),
             ((feat + 16, n), BF16),
             ((hid, n), BF16),
@@ -192,22 +205,32 @@
             ((feat, n), F32),
         ),
     )
-    own = (feats, feats1_t, av_t, row_sq, va)
-    scratch = (((k, n), F32), ((feat + 16, n), F32))
-    prod, near_back, grad, g_in, g_out = call(
+
+    def meet(block_points):
+        return call(
+            meet_kernel,
+            (block_points, w_in_t, w_out_t, feats, row_sq, va),
+            (((hid, n), BF16), ((feat + 16, n), BF16), ((n, n), BF16), ((nvec, n), F32)),
+        )
+
+    scratch = (((n, n), BF16),)
+    hid_c, feats1_c, kernel, near_back = meet(near_points)
+    prod, grad, g_in, g_out = call(
         functools.partial(pair_kernel, False),
-        (near_points, near_va, w_input, w_output) + own + (prod, grad),
-        (((k, n), F32), ((nvec, n), F32), ((feat, n), F32), ((hid, din), F32), ((hid, feat), F32)),
+        (near_points, near_va, hid_c, feats1_c, kernel, w_output, feats1_t, av_t, prod, grad),
+        (((k, n), F32), ((feat, n), F32), ((hid, din), F32), ((hid, feat), F32)),
         scratch,
     )
     second = lax.axis_index("c").astype(jnp.int32).reshape(1)
-    ins = (far_points, far_va, w_input, w_output) + own + (prod, grad, hid_t, points, second, g_in, g_out)
-    prod, far_back, keep, give = call(
+    prod, late_points = lax.optimization_barrier((prod, far_points))
+    hid_c, feats1_c, kernel, far_back = meet(late_points)
+    prod, keep, give = call(
         functools.partial(pair_kernel, True),
-        ins,
-        (((k, n), F32), ((nvec, n), F32), ((hid, feat), F32), ((hid, feat), F32)),
+        (late_points, far_va, hid_c, feats1_c, kernel, w_output, feats1_t, av_t, prod, grad)
+        + (hid_t, points, second, g_in, g_out),
+        (((k, n), F32), ((hid, feat), F32), ((hid, feat), F32)),
         scratch,
-        smem=13,
+        smem=12,
     )
     mine = keep + swap_cores(give)
     mine = join(mine, [8])

time: 67.7 us -> 66 us (0.975)
  waiting for transfers between devices: 13.8 us -> 11.8 us
  local copies, waits for them, and re-layouts: 2.5 us -> 3.46 us
    ppermute x8, waiting for transfers between devices: 11.1 us -> 8.78 us  [send(): lax.ppermute(x, ALL, [(i, target(i)) for i in range(lax.axis_size(ALL))])]
    unnamed x6 -> x8, local copies, waits for them, and re-layouts: 1.52 us -> 2.47 us
    pallas_call x3 -> x5, Pallas kernels: 11.8 us -> 11.5 us  [call(): pl.pallas_call(body, out_shape=[jax.ShapeDtypeStruct(s, d) for s, d in ou...]
  transfers between devices with their start and end apart: 13 -> 13, of which waited for: 8 -> 9; matrix products, arithmetic and copies ran while one was open for 3% -> 3% of each run, Pallas kernels for 11% -> 13%
where the time goes in v4:
time: 66 us; the launch traced here: 65.6 us
  starting transfers between devices  35.6 us (54%)
  waiting for transfers between devices  11.8 us (18%)
  Pallas kernels  11.5 us (17%)
  local copies, waits for them, and re-layouts  3.46 us (5%)
  other arithmetic  2.42 us (4%)
  between operations  0.75 us (1%)
    ppermute x8, starting transfers between devices, send(): lax.ppermute(x, ALL, [(i, target(i)) for i in range(lax.axis_size(ALL))])  17 us
    pallas_call x5, Pallas kernels, call(): pl.pallas_call(body, out_shape=[jax.ShapeDtypeStruct(s, d) for s, d in ou...  11.5 us
    ppermute x8, waiting for transfers between devices, send(): lax.ppermute(x, ALL, [(i, target(i)) for i in range(lax.axis_size(ALL))])  8.78 us
    ppermute x2, starting transfers between devices, send_back(): lax.ppermute(x, ALL, [(target(i), i) for i in range(lax.axis_size(ALL))])  7.37 us
    all_to_all x1, starting transfers between devices, sum_over(): got = lax.all_to_all(sent, axes, 0, 0)  6.75 us
    ppermute x2, starting transfers between devices, swap_cores(): return lax.ppermute(x, 'c', [(0, 1), (1, 0)])  4.47 us
    unnamed x8, local copies, waits for them, and re-layouts  2.47 us
    all_to_all x1, waiting for transfers between devices, sum_over(): got = lax.all_to_all(sent, axes, 0, 0)  1.58 us
  transfers between devices with their start and end apart: 13, of which 9 were waited for; matrix products, arithmetic and copies ran while one was open for 3% of the time, Pallas kernels for 13%

profile of v4, /device:TPU:1, one launch (start us, length us, event | category | flops | bytes accessed | tf_op | source)
XLA Modules:
  0.0 65.6 jit_solution(13061576161241509956)
XLA Ops:
  0.6 2.6 %collective-permute-start = (bf16[1024,128]{1,0:T(8,128)(2,1)}, bf16[1024,128]{1,0:T(8,128)(2,1)S(1)}, u32[]{:S(2)}, u32[]{:S(2)}) collective-permute-start(bf16[1024,128]{1,0:T(8,128)(2,1)} %refs_1_.1), channel_id=1, source_target_pairs={{0,1},{1,3},{2,0},{3,2},{4,5},{5,7},{6,4},{7,6},{8,9},{9,11},{10,8... | collective-permute-start | bytes 786440 | tf_op jit(solution)/shard_map/ppermute | solution.py:31
  3.2 3.0 %collective-permute-start.2 = (bf16[1024,128]{1,0:T(8,128)(2,1)}, bf16[1024,128]{1,0:T(8,128)(2,1)S(1)}, u32[]{:S(2)}, u32[]{:S(2)}) collective-permute-start(bf16[1024,128]{1,0:T(8,128)(2,1)} %refs_1_.1), channel_id=1, source_target_pairs={{0,8},{1,5},{2,10},{3,7},{4,0},{5,13},{6,2},{7,15},{8,12},{9,1},{1... | collective-permute-start | bytes 786440 | tf_op jit(solution)/shard_map/ppermute | solution.py:31
  6.3 1.0 %maximum_maximum_fusion.1 = (bf16[40,1024]{1,0:T(8,128)(2,1)S(1)}, bf16[40,1024]{1,0:T(8,128)(2,1)S(1)}) fusion(bf16[17,1024]{1,0:T(8,128)(2,1)} %param.8, bf16[17,1024]{1,0:T(8,128)(2,1)} %param.9, bf16[40]{0:T(256)(128)(2,1)S(1)} %pad.5.clone), kind=kLoop, calls=%fused_computation.3 | loop fusion | flops 450560 | bytes 233552 | tf_op jit(solution)/shard_map/concatenate | solution.py:188
  7.2 0.8 %collective-permute-start.1 = (bf16[40,1024]{1,0:T(8,128)(2,1)S(1)}, bf16[40,1024]{1,0:T(8,128)(2,1)S(1)}, u32[]{:S(2)}, u32[]{:S(2)}) collective-permute-start(bf16[40,1024]{1,0:T(8,128)(2,1)S(1)} %get-tuple-element.66.va), channel_id=1, source_target_pairs={{0,1},{1,3},{2,0},{3,2},{4,5},{5,7},{6,4},{7,6},{8,9},{9,11},{10,8... | collective-permute-start | bytes 245768 | tf_op jit(solution)/shard_map/ppermute | solution.py:31
  8.0 4.2 %collective-permute-start.3 = (bf16[40,1024]{1,0:T(8,128)(2,1)S(1)}, bf16[40,1024]{1,0:T(8,128)(2,1)S(1)}, u32[]{:S(2)}, u32[]{:S(2)}) collective-permute-start(bf16[40,1024]{1,0:T(8,128)(2,1)S(1)} %get-tuple-element.66.va), channel_id=1, source_target_pairs={{0,8},{1,5},{2,10},{3,7},{4,0},{5,13},{6,2},{7,15},{8,12},{9,1},{1... | collective-permute-start | bytes 245768 | tf_op jit(solution)/shard_map/ppermute | solution.py:31
  12.2 0.9 %copy-done = bf16[1024,128]{1,0:T(8,128)(2,1)S(1)} copy-done((bf16[1024,128]{1,0:T(8,128)(2,1)S(1)}, bf16[1024,128]{1,0:T(8,128)(2,1)}, u32[]{:S(2)}) %copy-start) | copy-done | bytes 262168
  13.2 0.8 %copy-done.2 = bf16[128,128]{1,0:T(8,128)(2,1)S(1)} copy-done((bf16[128,128]{1,0:T(8,128)(2,1)S(1)}, bf16[128,128]{1,0:T(8,128)(2,1)}, u32[]{:S(2)}) %copy-start.2) | copy-done | bytes 32792
  13.9 0.8 %copy-done.3 = bf16[128,128]{1,0:T(8,128)(2,1)S(1)} copy-done((bf16[128,128]{1,0:T(8,128)(2,1)S(1)}, bf16[128,128]{1,0:T(8,128)(2,1)}, u32[]{:S(2)}) %copy-start.3) | copy-done | bytes 32792
  14.7 3.1 %shard_map.76 = (bf16[128,128]{1,0:T(8,128)(2,1)S(1)}, bf16[128,128]{1,0:T(8,128)(2,1)S(1)}, bf16[1024,128]{1,0:T(8,128)(2,1)S(1)}, bf16[144,1024]{1,0:T(8,128)(...) custom-call(bf16[1024,128]{1,0:T(8,128)(2,1)S(1)} %copy-done, ...), custom_call_target="tpu_custom_call" | custom-call | tf_op jit(solution)/shard_map/pallas_call | solution.py:173
  17.7 1.6 %shard_map.77 = (bf16[128,1024]{1,0:T(8,128)(2,1)S(1)}, bf16[144,1024]{1,0:T(8,128)(2,1)S(1)}, bf16[1024,1024]{1,0:T(8,128)(2,1)S(1)}, f32[17,1024]{1,0:T(8,128)S(1)}) custom-call(bf16[1024,128]{1,0:T(8,128)(2,1)S(1)} %collective-permute-done.pts_c, bf16[128,128]{1,0:T(8,128)(2,1)S(1)} %get-tuple-element.33.w_in_t, ...), custom_call_target="tpu_custom_call" | custom-call | tf_op jit(solution)/shard_map/pallas_call | solution.py:173
  19.4 2.5 %shard_map.78 = (f32[40,1024]{1,0:T(8,128)S(1)}, f32[128,1024]{1,0:T(8,128)S(1)}, f32[128,128]{1,0:T(8,128)S(1)}, f32[128,128]{1,0:T(8,128)S(1)}) custom-call(bf16[1024,128]{1,0:T(8,128)(2,1)S(1)} %collective-permute-done.pts_c, bf16[40,1024]{1,0:T(8,128)(2,1)S(1)} %collective-permute-done.1.va_c, bf16[128,1024]{1,0:T(8,128)(2,1)S(1)} %get-tuple-element.37.hid_c, ...), custom_call_target="tpu_custom_call" | custom-call | tf_op jit(solution)/shard_map/pallas_call | solution.py:173
  21.9 1.6 %collective-permute-done.2.pts_c = bf16[1024,128]{1,0:T(8,128)(2,1)S(1)} collective-permute-done((bf16[1024,128]{1,0:T(8,128)(2,1)}, bf16[1024,128]{1,0:T(8,128)(2,1)S(1)}, u32[]{:S(2)}, u32[]{:S(2)}) %collective-permute-start.2) | collective-permute-done | bytes 262176 | tf_op jit(solution)/shard_map/ppermute | solution.py:31
  23.4 1.6 %shard_map.79 = (bf16[128,1024]{1,0:T(8,128)(2,1)S(1)}, bf16[144,1024]{1,0:T(8,128)(2,1)S(1)}, bf16[1024,1024]{1,0:T(8,128)(2,1)S(1)}, f32[17,1024]{1,0:T(8,128)S(1)}) custom-call(bf16[1024,128]{1,0:T(8,128)(2,1)S(1)} %collective-permute-done.2.pts_c, bf16[128,128]{1,0:T(8,128)(2,1)S(1)} %get-tuple-element.33.w_in_t, ...), custom_call_target="tpu_custom_call" | custom-call | tf_op jit(solution)/shard_map/pallas_call | solution.py:173
  25.1 0.2 collective-permute-done.3.va_c
  25.2 2.7 %shard_map.80 = (f32[40,1024]{1,0:T(8,128)S(1)}, f32[128,128]{1,0:T(8,128)S(1)}, f32[128,128]{1,0:T(8,128)S(1)}) custom-call(bf16[1024,128]{1,0:T(8,128)(2,1)S(1)} %collective-permute-done.2.pts_c, bf16[40,1024]{1,0:T(8,128)(2,1)S(1)} %collective-permute-done.3.va_c, bf16[128,1024]{1,0:T(8,128)(2,1)S(1)} %get-tuple-element.46.hid_c, ...), custom_call_target="tpu_custom_call" | custom-call | tf_op jit(solution)/shard_map/pallas_call | solution.py:173
  28.1 1.2 %collective-permute-done.4 = f32[128,128]{1,0:T(8,128)S(1)} collective-permute-done((f32[128,128]{1,0:T(8,128)S(1)}, f32[128,128]{1,0:T(8,128)S(1)}, u32[]{:S(2)}, u32[]{:S(2)}) %collective-permute-start.4) | collective-permute-done | bytes 65568 | tf_op jit(solution)/shard_map/ppermute | solution.py:39
  29.3 2.8 %collective-permute-start.5 = (bf16[128,128]{1,0:T(8,128)(2,1)S(1)}, bf16[128,128]{1,0:T(8,128)(2,1)S(1)}, u32[]{:S(2)}, u32[]{:S(2)}) collective-permute-start(bf16[128,128]{1,0:T(8,128)(2,1)S(1)} %fusion), channel_id=1, source_target_pairs={{0,8},{1,9},{2,10},{3,11},{4,12},{5,13},{6,14},{7,15},{8,0},{9,1},... | collective-permute-start | bytes 98312 | tf_op jit(solution)/shard_map/ppermute | solution.py:31
  32.2 4.0 %collective-permute-done.5 = bf16[128,128]{1,0:T(8,128)(2,1)S(1)} collective-permute-done((bf16[128,128]{1,0:T(8,128)(2,1)S(1)}, bf16[128,128]{1,0:T(8,128)(2,1)S(1)}, u32[]{:S(2)}, u32[]{:S(2)}) %collective-permute-start.5) | collective-permute-done | bytes 32800 | tf_op jit(solution)/shard_map/ppermute | solution.py:31
  36.2 3.0 %collective-permute-start.10 = (bf16[128,128]{1,0:T(8,128)(2,1)S(1)}, bf16[128,128]{1,0:T(8,128)(2,1)S(1)}, u32[]{:S(2)}, u32[]{:S(2)}) collective-permute-start(bf16[128,128]{1,0:T(8,128)(2,1)S(1)} %reduce-precision_convert_fusion), channel_id=1, source_target_pairs={{0,6},{1,7},{2,4},{3,5},{4,2},{5,3},{6,0},{7,1},{8,14},{9,15},{10,... | collective-permute-start | bytes 98312 | tf_op jit(solution)/shard_map/ppermute | solution.py:31
  39.2 0.6 collective-permute-start.9
  39.8 1.0 %collective-permute-done.10 = bf16[128,128]{1,0:T(8,128)(2,1)S(1)} collective-permute-done((bf16[128,128]{1,0:T(8,128)(2,1)S(1)}, bf16[128,128]{1,0:T(8,128)(2,1)S(1)}, u32[]{:S(2)}, u32[]{:S(2)}) %collective-permute-start.10) | collective-permute-done | bytes 32800 | tf_op jit(solution)/shard_map/ppermute | solution.py:31
  40.8 1.4 %collective-permute-done.8 = bf16[128,128]{1,0:T(8,128)(2,1)S(1)} collective-permute-done((bf16[128,128]{1,0:T(8,128)(2,1)S(1)}, bf16[128,128]{1,0:T(8,128)(2,1)S(1)}, u32[]{:S(2)}, u32[]{:S(2)}) %collective-permute-start.8) | collective-permute-done | bytes 32800 | tf_op jit(solution)/shard_map/ppermute | solution.py:31
  42.2 0.7 %collective-permute-done.9 = bf16[128,128]{1,0:T(8,128)(2,1)S(1)} collective-permute-done((bf16[128,128]{1,0:T(8,128)(2,1)S(1)}, bf16[128,128]{1,0:T(8,128)(2,1)S(1)}, u32[]{:S(2)}, u32[]{:S(2)}) %collective-permute-start.9) | collective-permute-done | bytes 32800 | tf_op jit(solution)/shard_map/ppermute | solution.py:31
  42.9 0.9 %broadcast_in_dim.7 = bf16[16,128,128]{2,1,0:T(8,128)(2,1)} broadcast(bf16[128,128]{1,0:T(8,128)(2,1)S(1)} %add_convert_fusion), dimensions={1,2} | broadcast | bytes 557056 | tf_op jit(solution)/shard_map/broadcast_in_dim | solution.py:44
  43.8 6.8 %all-to-all-start = ((bf16[16,128,128]{2,1,0:T(8,128)(2,1)}), bf16[16,128,128]{2,1,0:T(8,128)(2,1)S(1)}, u32[]{:S(2)}, u32[]{:S(2)}) async-start(bf16[16,128,128]{2,1,0:T(8,128)(2,1)} %broadcast_in_dim.7), calls=%async_computation | async-start | bytes 1048576 | tf_op jit(solution)/shard_map/all_to_all | solution.py:45
  50.6 3.2 %collective-permute-start.6 = (f32[17,1024]{1,0:T(8,128)S(1)}, f32[17,1024]{1,0:T(8,128)S(1)}, u32[]{:S(2)}, u32[]{:S(2)}) collective-permute-start(f32[17,1024]{1,0:T(8,128)S(1)} %get-tuple-element.60), channel_id=1, source_target_pairs={{1,0},{3,1},{0,2},{2,3},{5,4},{7,5},{4,6},{6,7},{9,8},{11,9},{8,10... | collective-permute-start | bytes 208904 | tf_op jit(solution)/shard_map/ppermute | solution.py:35
  53.8 4.1 %collective-permute-start.7 = (f32[17,1024]{1,0:T(8,128)S(1)}, f32[17,1024]{1,0:T(8,128)S(1)}, u32[]{:S(2)}, u32[]{:S(2)}) collective-permute-start(f32[17,1024]{1,0:T(8,128)S(1)} %get-tuple-element.61), channel_id=1, source_target_pairs={{8,0},{5,1},{10,2},{7,3},{0,4},{13,5},{2,6},{15,7},{12,8},{1,9},{1... | collective-permute-start | bytes 208904 | tf_op jit(solution)/shard_map/ppermute | solution.py:35
  58.0 1.6 %all-to-all-done = bf16[16,128,128]{2,1,0:T(8,128)(2,1)S(1)} async-done(((bf16[16,128,128]{2,1,0:T(8,128)(2,1)}), bf16[16,128,128]{2,1,0:T(8,128)(2,1)S(1)}, u32[]{:S(2)}, u32[]{:S(2)}) %all-to-all-start) | async-done | bytes 524320 | tf_op jit(solution)/shard_map/all_to_all | solution.py:45
  59.6 4.4 %collective-permute-start.11 = (f32[128,128]{1,0:T(8,128)S(1)}, f32[128,128]{1,0:T(8,128)S(1)}, u32[]{:S(2)}, u32[]{:S(2)}) collective-permute-start(f32[128,128]{1,0:T(8,128)S(1)} %convert_reduce_fusion), channel_id=1, source_target_pairs={{0,1},{1,0},{2,3},{3,2},{4,5},{5,4},{6,7},{7,6},{8,9},{9,8},{10,11... | collective-permute-start | bytes 196616 | tf_op jit(solution)/shard_map/ppermute | solution.py:39
  64.0 0.7 %add_add_fusion = f32[17,1024]{1,0:T(8,128)} fusion(f32[17,1024]{1,0:T(8,128)S(1)} %collective-permute-done.7, f32[17,1024]{1,0:T(8,128)S(1)} %collective-permute-done.6, f32[40,1024]{1,0:T(8,128)S(1)} %get-tuple-element.54), kind=kLoop, calls=%fused_computation.1 | loop fusion | flops 34816 | bytes 278528 | tf_op jit(solution)/shard_map/add | solution.py:247
  64.7 0.2 collective-permute-done.11
  64.9 0.7 %broadcast_select_fusion = (f32[128,128]{1,0:T(8,128)}, f32[128,128]{1,0:T(8,128)}) fusion(f32[128,128]{1,0:T(8,128)S(1)} %convert_reduce_fusion, f32[128,128]{1,0:T(8,128)S(1)} %collective-permute-done.11, pred[]{:T(512)S(6)} %eq.3), kind=kLoop, calls=%fused_computation.8 | loop fusion | flops 32768 | bytes 262145 | tf_op jit(solution)/shard_map/jit(_where)/select_n | solution.py:246
  (18 shorter events, 0.3 us)
Async XLA Ops:
  0.6 17.1 %collective-permute-start = (bf16[1024,128]{1,0:T(8,128)(2,1)}, bf16[1024,128]{1,0:T(8,128)(2,1)S(1)}, u32[]{:S(2)}, u32[]{:S(2)}) collective-permute-start(bf16[1024,128]{1,0:T(8,128)(2,1)} %refs_1_.1), channel_id=1, source_target_pairs={{0,1},{1,3},{2,0},{3,2},{4,5},{5,7},{6,4},{7,6},{8,9},{9,11},{10,8... | collective-permute-start | bytes 786440 | tf_op jit(solution)/shard_map/ppermute | solution.py:31
  3.2 20.3 %collective-permute-start.2 = (bf16[1024,128]{1,0:T(8,128)(2,1)}, bf16[1024,128]{1,0:T(8,128)(2,1)S(1)}, u32[]{:S(2)}, u32[]{:S(2)}) collective-permute-start(bf16[1024,128]{1,0:T(8,128)(2,1)} %refs_1_.1), channel_id=1, source_target_pairs={{0,8},{1,5},{2,10},{3,7},{4,0},{5,13},{6,2},{7,15},{8,12},{9,1},{1... | collective-permute-start | bytes 786440 | tf_op jit(solution)/shard_map/ppermute | solution.py:31
  7.2 12.1 %collective-permute-start.1 = (bf16[40,1024]{1,0:T(8,128)(2,1)S(1)}, bf16[40,1024]{1,0:T(8,128)(2,1)S(1)}, u32[]{:S(2)}, u32[]{:S(2)}) collective-permute-start(bf16[40,1024]{1,0:T(8,128)(2,1)S(1)} %get-tuple-element.66.va), channel_id=1, source_target_pairs={{0,1},{1,3},{2,0},{3,2},{4,5},{5,7},{6,4},{7,6},{8,9},{9,11},{10,8... | collective-permute-start | bytes 245768 | tf_op jit(solution)/shard_map/ppermute | solution.py:31
  8.0 17.3 %collective-permute-start.3 = (bf16[40,1024]{1,0:T(8,128)(2,1)S(1)}, bf16[40,1024]{1,0:T(8,128)(2,1)S(1)}, u32[]{:S(2)}, u32[]{:S(2)}) collective-permute-start(bf16[40,1024]{1,0:T(8,128)(2,1)S(1)} %get-tuple-element.66.va), channel_id=1, source_target_pairs={{0,8},{1,5},{2,10},{3,7},{4,0},{5,13},{6,2},{7,15},{8,12},{9,1},{1... | collective-permute-start | bytes 245768 | tf_op jit(solution)/shard_map/ppermute | solution.py:31
  12.2 0.9 %copy-start = (bf16[1024,128]{1,0:T(8,128)(2,1)S(1)}, bf16[1024,128]{1,0:T(8,128)(2,1)}, u32[]{:S(2)}) copy-start(bf16[1024,128]{1,0:T(8,128)(2,1)} %refs_1_.1) | copy-start | bytes 786436
  13.2 0.8 %copy-start.2 = (bf16[128,128]{1,0:T(8,128)(2,1)S(1)}, bf16[128,128]{1,0:T(8,128)(2,1)}, u32[]{:S(2)}) copy-start(bf16[128,128]{1,0:T(8,128)(2,1)} %w_out.5) | copy-start | bytes 98308
  13.9 0.8 %copy-start.3 = (bf16[128,128]{1,0:T(8,128)(2,1)S(1)}, bf16[128,128]{1,0:T(8,128)(2,1)}, u32[]{:S(2)}) copy-start(bf16[128,128]{1,0:T(8,128)(2,1)} %w_in.1) | copy-start | bytes 98308
  19.4 5.9 %copy-start.1 = (bf16[1024,128]{1,0:T(8,128)(2,1)S(1)}, bf16[1024,128]{1,0:T(8,128)(2,1)}, u32[]{:S(2)}) copy-start(bf16[1024,128]{1,0:T(8,128)(2,1)} %refs_1_.1) | copy-start | bytes 786436
  28.0 1.3 %collective-permute-start.4 = (f32[128,128]{1,0:T(8,128)S(1)}, f32[128,128]{1,0:T(8,128)S(1)}, u32[]{:S(2)}, u32[]{:S(2)}) collective-permute-start(f32[128,128]{1,0:T(8,128)S(1)} %get-tuple-element.56), channel_id=1, source_target_pairs={{0,1},{1,0},{2,3},{3,2},{4,5},{5,4},{6,7},{7,6},{8,9},{9,8},{10,11... | collective-permute-start | bytes 196616 | tf_op jit(solution)/shard_map/ppermute | solution.py:39
  29.3 6.8 %collective-permute-start.5 = (bf16[128,128]{1,0:T(8,128)(2,1)S(1)}, bf16[128,128]{1,0:T(8,128)(2,1)S(1)}, u32[]{:S(2)}, u32[]{:S(2)}) collective-permute-start(bf16[128,128]{1,0:T(8,128)(2,1)S(1)} %fusion), channel_id=1, source_target_pairs={{0,8},{1,9},{2,10},{3,11},{4,12},{5,13},{6,14},{7,15},{8,0},{9,1},... | collective-permute-start | bytes 98312 | tf_op jit(solution)/shard_map/ppermute | solution.py:31
  36.2 4.7 %collective-permute-start.10 = (bf16[128,128]{1,0:T(8,128)(2,1)S(1)}, bf16[128,128]{1,0:T(8,128)(2,1)S(1)}, u32[]{:S(2)}, u32[]{:S(2)}) collective-permute-start(bf16[128,128]{1,0:T(8,128)(2,1)S(1)} %reduce-precision_convert_fusion), channel_id=1, source_target_pairs={{0,6},{1,7},{2,4},{3,5},{4,2},{5,3},{6,0},{7,1},{8,14},{9,15},{10,... | collective-permute-start | bytes 98312 | tf_op jit(solution)/shard_map/ppermute | solution.py:31
  39.2 3.1 %collective-permute-start.8 = (bf16[128,128]{1,0:T(8,128)(2,1)S(1)}, bf16[128,128]{1,0:T(8,128)(2,1)S(1)}, u32[]{:S(2)}, u32[]{:S(2)}) collective-permute-start(bf16[128,128]{1,0:T(8,128)(2,1)S(1)} %reduce-precision_convert_fusion), channel_id=1, source_target_pairs={{0,2},{1,3},{2,0},{3,1},{4,6},{5,7},{6,4},{7,5},{8,10},{9,11},{10,... | collective-permute-start | bytes 98312 | tf_op jit(solution)/shard_map/ppermute | solution.py:31
  39.2 3.7 %collective-permute-start.9 = (bf16[128,128]{1,0:T(8,128)(2,1)S(1)}, bf16[128,128]{1,0:T(8,128)(2,1)S(1)}, u32[]{:S(2)}, u32[]{:S(2)}) collective-permute-start(bf16[128,128]{1,0:T(8,128)(2,1)S(1)} %reduce-precision_convert_fusion), channel_id=1, source_target_pairs={{0,4},{1,5},{2,6},{3,7},{4,0},{5,1},{6,2},{7,3},{8,12},{9,13},{10,... | collective-permute-start | bytes 98312 | tf_op jit(solution)/shard_map/ppermute | solution.py:31
  43.8 15.7 %all-to-all-start = ((bf16[16,128,128]{2,1,0:T(8,128)(2,1)}), bf16[16,128,128]{2,1,0:T(8,128)(2,1)S(1)}, u32[]{:S(2)}, u32[]{:S(2)}) async-start(bf16[16,128,128]{2,1,0:T(8,128)(2,1)} %broadcast_in_dim.7), calls=%async_computation | async-start | bytes 1048576 | tf_op jit(solution)/shard_map/all_to_all | solution.py:45
  50.6 13.4 %collective-permute-start.6 = (f32[17,1024]{1,0:T(8,128)S(1)}, f32[17,1024]{1,0:T(8,128)S(1)}, u32[]{:S(2)}, u32[]{:S(2)}) collective-permute-start(f32[17,1024]{1,0:T(8,128)S(1)} %get-tuple-element.60), channel_id=1, source_target_pairs={{1,0},{3,1},{0,2},{2,3},{5,4},{7,5},{4,6},{6,7},{9,8},{11,9},{8,10... | collective-permute-start | bytes 208904 | tf_op jit(solution)/shard_map/ppermute | solution.py:35
  53.8 10.2 %collective-permute-start.7 = (f32[17,1024]{1,0:T(8,128)S(1)}, f32[17,1024]{1,0:T(8,128)S(1)}, u32[]{:S(2)}, u32[]{:S(2)}) collective-permute-start(f32[17,1024]{1,0:T(8,128)S(1)} %get-tuple-element.61), channel_id=1, source_target_pairs={{8,0},{5,1},{10,2},{7,3},{0,4},{13,5},{2,6},{15,7},{12,8},{1,9},{1... | collective-permute-start | bytes 208904 | tf_op jit(solution)/shard_map/ppermute | solution.py:35
  59.6 5.3 %collective-permute-start.11 = (f32[128,128]{1,0:T(8,128)S(1)}, f32[128,128]{1,0:T(8,128)S(1)}, u32[]{:S(2)}, u32[]{:S(2)}) collective-permute-start(f32[128,128]{1,0:T(8,128)S(1)} %convert_reduce_fusion), channel_id=1, source_target_pairs={{0,1},{1,0},{2,3},{3,2},{4,5},{5,4},{6,7},{7,6},{8,9},{9,8},{10,11... | collective-permute-start | bytes 196616 | tf_op jit(solution)/shard_map/ppermute | solution.py:39

commit v5 on v4

--- a/solution.py
+++ b/solution.py
@@ -20,7 +20,7 @@
 
 
 def far_target(i):
-    return i ^ 8 if bit(i, 3) ^ bit(i, 2) ^ bit(i, 0) == 0 else i ^ 4
+    return i ^ 8 if bit(i, 3) ^ bit(i, 2) ^ bit(i, 0) == 1 else i ^ 4
 
 
 def near_target(i):
@@ -222,6 +222,7 @@
         scratch,
     )
     second = lax.axis_index("c").astype(jnp.int32).reshape(1)
+    near_back = send_back(near_back, near_target)
     prod, late_points = lax.optimization_barrier((prod, far_points))
     hid_c, feats1_c, kernel, far_back = meet(late_points)
     prod, keep, give = call(
@@ -233,11 +234,8 @@
         smem=12,
     )
     mine = keep + swap_cores(give)
+    far_back = send_back(far_back, far_target)
     mine = join(mine, [8])
-    mine, far_back = lax.optimization_barrier((mine, far_back))
-    far_back = send_back(far_back, far_target)
-    mine, near_back = lax.optimization_barrier((mine, near_back))
-    near_back = send_back(near_back, near_target)
     mine = join(mine, [2, 4, 6])
     mine = sum_over(mine, ('x', 'y'))
     other = swap_cores(mine)

time: 66 us -> 65.3 us (0.989)
  waiting for transfers between devices: 11.8 us -> 5.56 us
  starting transfers between devices: 35.6 us -> 41.2 us
    ppermute x8, waiting for transfers between devices: 8.78 us -> 3.71 us  [send(): lax.ppermute(x, ALL, [(i, target(i)) for i in range(lax.axis_size(ALL))])]
    ppermute x8, starting transfers between devices: 17 us -> 20.7 us  [send(): lax.ppermute(x, ALL, [(i, target(i)) for i in range(lax.axis_size(ALL))])]
    ppermute x2, starting transfers between devices: 7.37 us -> 8.3 us  [send_back(): lax.ppermute(x, ALL, [(target(i), i) for i in range(lax.axis_size(ALL))])]
    all_to_all x1, waiting for transfers between devices: 1.58 us -> 0.71 us  [sum_over(): got = lax.all_to_all(sent, axes, 0, 0)]
  transfers between devices with their start and end apart: 13 -> 13, of which waited for: 9 -> 6; matrix products, arithmetic and copies ran while one was open for 3% -> 3% of each run, Pallas kernels for 13% -> 14%
where the time goes in v5:
time: 65.3 us; the launch traced here: 64.9 us
  starting transfers between devices  41.2 us (63%)
  Pallas kernels  11.5 us (18%)
  waiting for transfers between devices  5.56 us (9%)
  local copies, waits for them, and re-layouts  3.46 us (5%)
  other arithmetic  2.43 us (4%)
  between operations  0.75 us (1%)
    ppermute x8, starting transfers between devices, send(): lax.ppermute(x, ALL, [(i, target(i)) for i in range(lax.axis_size(ALL))])  20.7 us
    pallas_call x5, Pallas kernels, call(): pl.pallas_call(body, out_shape=[jax.ShapeDtypeStruct(s, d) for s, d in ou...  11.5 us
    ppermute x2, starting transfers between devices, send_back(): lax.ppermute(x, ALL, [(target(i), i) for i in range(lax.axis_size(ALL))])  8.3 us
    all_to_all x1, starting transfers between devices, sum_over(): got = lax.all_to_all(sent, axes, 0, 0)  7.23 us
    ppermute x2, starting transfers between devices, swap_cores(): return lax.ppermute(x, 'c', [(0, 1), (1, 0)])  4.96 us
    ppermute x8, waiting for transfers between devices, send(): lax.ppermute(x, ALL, [(i, target(i)) for i in range(lax.axis_size(ALL))])  3.71 us
    unnamed x8, local copies, waits for them, and re-layouts  2.47 us
  transfers between devices with their start and end apart: 13, of which 6 were waited for; matrix products, arithmetic and copies ran while one was open for 3% of the time, Pallas kernels for 14%

profile of v5, /device:TPU:1, one launch (start us, length us, event | category | flops | bytes accessed | tf_op | source)
XLA Modules:
  0.0 64.9 jit_solution(6445046373893612685)
XLA Ops:
  0.6 2.6 %collective-permute-start = (bf16[1024,128]{1,0:T(8,128)(2,1)}, bf16[1024,128]{1,0:T(8,128)(2,1)S(1)}, u32[]{:S(2)}, u32[]{:S(2)}) collective-permute-start(bf16[1024,128]{1,0:T(8,128)(2,1)} %refs_1_.1), channel_id=1, source_target_pairs={{0,1},{1,3},{2,0},{3,2},{4,5},{5,7},{6,4},{7,6},{8,9},{9,11},{10,8... | collective-permute-start | bytes 786440 | tf_op jit(solution)/shard_map/ppermute | solution.py:31
  3.2 6.0 %collective-permute-start.2 = (bf16[1024,128]{1,0:T(8,128)(2,1)}, bf16[1024,128]{1,0:T(8,128)(2,1)S(1)}, u32[]{:S(2)}, u32[]{:S(2)}) collective-permute-start(bf16[1024,128]{1,0:T(8,128)(2,1)} %refs_1_.1), channel_id=1, source_target_pairs={{0,4},{1,9},{2,6},{3,11},{4,12},{5,1},{6,14},{7,3},{8,0},{9,13},{1... | collective-permute-start | bytes 786440 | tf_op jit(solution)/shard_map/ppermute | solution.py:31
  9.2 0.1 pad.5.clone
  9.3 1.0 %maximum_maximum_fusion.1 = (bf16[40,1024]{1,0:T(8,128)(2,1)S(1)}, bf16[40,1024]{1,0:T(8,128)(2,1)S(1)}) fusion(bf16[17,1024]{1,0:T(8,128)(2,1)} %param.8, bf16[17,1024]{1,0:T(8,128)(2,1)} %param.9, bf16[40]{0:T(256)(128)(2,1)S(1)} %pad.5.clone), kind=kLoop, calls=%fused_computation.3 | loop fusion | flops 450560 | bytes 233552 | tf_op jit(solution)/shard_map/concatenate | solution.py:188
  10.2 0.8 %collective-permute-start.1 = (bf16[40,1024]{1,0:T(8,128)(2,1)S(1)}, bf16[40,1024]{1,0:T(8,128)(2,1)S(1)}, u32[]{:S(2)}, u32[]{:S(2)}) collective-permute-start(bf16[40,1024]{1,0:T(8,128)(2,1)S(1)} %get-tuple-element.58.va), channel_id=1, source_target_pairs={{0,1},{1,3},{2,0},{3,2},{4,5},{5,7},{6,4},{7,6},{8,9},{9,11},{10,8... | collective-permute-start | bytes 245768 | tf_op jit(solution)/shard_map/ppermute | solution.py:31
  11.0 1.2 %collective-permute-start.3 = (bf16[40,1024]{1,0:T(8,128)(2,1)S(1)}, bf16[40,1024]{1,0:T(8,128)(2,1)S(1)}, u32[]{:S(2)}, u32[]{:S(2)}) collective-permute-start(bf16[40,1024]{1,0:T(8,128)(2,1)S(1)} %get-tuple-element.58.va), channel_id=1, source_target_pairs={{0,4},{1,9},{2,6},{3,11},{4,12},{5,1},{6,14},{7,3},{8,0},{9,13},{1... | collective-permute-start | bytes 245768 | tf_op jit(solution)/shard_map/ppermute | solution.py:31
  12.2 0.9 %copy-done = bf16[1024,128]{1,0:T(8,128)(2,1)S(1)} copy-done((bf16[1024,128]{1,0:T(8,128)(2,1)S(1)}, bf16[1024,128]{1,0:T(8,128)(2,1)}, u32[]{:S(2)}) %copy-start) | copy-done | bytes 262168
  13.2 0.8 %copy-done.2 = bf16[128,128]{1,0:T(8,128)(2,1)S(1)} copy-done((bf16[128,128]{1,0:T(8,128)(2,1)S(1)}, bf16[128,128]{1,0:T(8,128)(2,1)}, u32[]{:S(2)}) %copy-start.2) | copy-done | bytes 32792
  13.9 0.8 %copy-done.3 = bf16[128,128]{1,0:T(8,128)(2,1)S(1)} copy-done((bf16[128,128]{1,0:T(8,128)(2,1)S(1)}, bf16[128,128]{1,0:T(8,128)(2,1)}, u32[]{:S(2)}) %copy-start.3) | copy-done | bytes 32792
  14.7 3.1 %shard_map.76 = (bf16[128,128]{1,0:T(8,128)(2,1)S(1)}, bf16[128,128]{1,0:T(8,128)(2,1)S(1)}, bf16[1024,128]{1,0:T(8,128)(2,1)S(1)}, bf16[144,1024]{1,0:T(8,128)(...) custom-call(bf16[1024,128]{1,0:T(8,128)(2,1)S(1)} %copy-done, ...), custom_call_target="tpu_custom_call" | custom-call | tf_op jit(solution)/shard_map/pallas_call | solution.py:173
  17.7 1.6 %shard_map.77 = (bf16[128,1024]{1,0:T(8,128)(2,1)S(1)}, bf16[144,1024]{1,0:T(8,128)(2,1)S(1)}, bf16[1024,1024]{1,0:T(8,128)(2,1)S(1)}, f32[17,1024]{1,0:T(8,128)S(1)}) custom-call(bf16[1024,128]{1,0:T(8,128)(2,1)S(1)} %collective-permute-done.pts_c, bf16[128,128]{1,0:T(8,128)(2,1)S(1)} %get-tuple-element.29.w_in_t, ...), custom_call_target="tpu_custom_call" | custom-call | tf_op jit(solution)/shard_map/pallas_call | solution.py:173
  19.4 2.5 %shard_map.78 = (f32[40,1024]{1,0:T(8,128)S(1)}, f32[128,1024]{1,0:T(8,128)S(1)}, f32[128,128]{1,0:T(8,128)S(1)}, f32[128,128]{1,0:T(8,128)S(1)}) custom-call(bf16[1024,128]{1,0:T(8,128)(2,1)S(1)} %collective-permute-done.pts_c, bf16[40,1024]{1,0:T(8,128)(2,1)S(1)} %collective-permute-done.1.va_c, bf16[128,1024]{1,0:T(8,128)(2,1)S(1)} %get-tuple-element.33.hid_c, ...), custom_call_target="tpu_custom_call" | custom-call | tf_op jit(solution)/shard_map/pallas_call | solution.py:173
  21.9 1.6 %shard_map.79 = (bf16[128,1024]{1,0:T(8,128)(2,1)S(1)}, bf16[144,1024]{1,0:T(8,128)(2,1)S(1)}, bf16[1024,1024]{1,0:T(8,128)(2,1)S(1)}, f32[17,1024]{1,0:T(8,128)S(1)}) custom-call(bf16[1024,128]{1,0:T(8,128)(2,1)S(1)} %collective-permute-done.2.pts_c, bf16[128,128]{1,0:T(8,128)(2,1)S(1)} %get-tuple-element.29.w_in_t, ...), custom_call_target="tpu_custom_call" | custom-call | tf_op jit(solution)/shard_map/pallas_call | solution.py:173
  23.6 2.7 %shard_map.80 = (f32[40,1024]{1,0:T(8,128)S(1)}, f32[128,128]{1,0:T(8,128)S(1)}, f32[128,128]{1,0:T(8,128)S(1)}) custom-call(bf16[1024,128]{1,0:T(8,128)(2,1)S(1)} %collective-permute-done.2.pts_c, bf16[40,1024]{1,0:T(8,128)(2,1)S(1)} %collective-permute-done.3.va_c, bf16[128,1024]{1,0:T(8,128)(2,1)S(1)} %get-tuple-element.42.hid_c, ...), custom_call_target="tpu_custom_call" | custom-call | tf_op jit(solution)/shard_map/pallas_call | solution.py:173
  26.3 1.0 %collective-permute-start.6 = (f32[128,128]{1,0:T(8,128)S(1)}, f32[128,128]{1,0:T(8,128)S(1)}, u32[]{:S(2)}, u32[]{:S(2)}) collective-permute-start(f32[128,128]{1,0:T(8,128)S(1)} %get-tuple-element.54), channel_id=1, source_target_pairs={{0,1},{1,0},{2,3},{3,2},{4,5},{5,4},{6,7},{7,6},{8,9},{9,8},{10,11... | collective-permute-start | bytes 196616 | tf_op jit(solution)/shard_map/ppermute | solution.py:39
  27.3 0.9 %collective-permute-done.6 = f32[128,128]{1,0:T(8,128)S(1)} collective-permute-done((f32[128,128]{1,0:T(8,128)S(1)}, f32[128,128]{1,0:T(8,128)S(1)}, u32[]{:S(2)}, u32[]{:S(2)}) %collective-permute-start.6) | collective-permute-done | bytes 65568 | tf_op jit(solution)/shard_map/ppermute | solution.py:39
  28.2 6.5 %collective-permute-start.7 = (bf16[128,128]{1,0:T(8,128)(2,1)S(1)}, bf16[128,128]{1,0:T(8,128)(2,1)S(1)}, u32[]{:S(2)}, u32[]{:S(2)}) collective-permute-start(bf16[128,128]{1,0:T(8,128)(2,1)S(1)} %fusion.1), channel_id=1, source_target_pairs={{0,8},{1,9},{2,10},{3,11},{4,12},{5,13},{6,14},{7,15},{8,0},{9,1},... | collective-permute-start | bytes 98312 | tf_op jit(solution)/shard_map/ppermute | solution.py:31
  34.7 1.3 %collective-permute-done.7 = bf16[128,128]{1,0:T(8,128)(2,1)S(1)} collective-permute-done((bf16[128,128]{1,0:T(8,128)(2,1)S(1)}, bf16[128,128]{1,0:T(8,128)(2,1)S(1)}, u32[]{:S(2)}, u32[]{:S(2)}) %collective-permute-start.7) | collective-permute-done | bytes 32800 | tf_op jit(solution)/shard_map/ppermute | solution.py:31
  36.1 0.8 %collective-permute-start.10 = (bf16[128,128]{1,0:T(8,128)(2,1)S(1)}, bf16[128,128]{1,0:T(8,128)(2,1)S(1)}, u32[]{:S(2)}, u32[]{:S(2)}) collective-permute-start(bf16[128,128]{1,0:T(8,128)(2,1)S(1)} %fusion), channel_id=1, source_target_pairs={{0,6},{1,7},{2,4},{3,5},{4,2},{5,3},{6,0},{7,1},{8,14},{9,15},{10,... | collective-permute-start | bytes 98312 | tf_op jit(solution)/shard_map/ppermute | solution.py:31
  36.9 1.4 %collective-permute-start.8 = (bf16[128,128]{1,0:T(8,128)(2,1)S(1)}, bf16[128,128]{1,0:T(8,128)(2,1)S(1)}, u32[]{:S(2)}, u32[]{:S(2)}) collective-permute-start(bf16[128,128]{1,0:T(8,128)(2,1)S(1)} %fusion), channel_id=1, source_target_pairs={{0,2},{1,3},{2,0},{3,1},{4,6},{5,7},{6,4},{7,5},{8,10},{9,11},{10,... | collective-permute-start | bytes 98312 | tf_op jit(solution)/shard_map/ppermute | solution.py:31
  38.3 1.4 %collective-permute-start.9 = (bf16[128,128]{1,0:T(8,128)(2,1)S(1)}, bf16[128,128]{1,0:T(8,128)(2,1)S(1)}, u32[]{:S(2)}, u32[]{:S(2)}) collective-permute-start(bf16[128,128]{1,0:T(8,128)(2,1)S(1)} %fusion), channel_id=1, source_target_pairs={{0,4},{1,5},{2,6},{3,7},{4,0},{5,1},{6,2},{7,3},{8,12},{9,13},{10,... | collective-permute-start | bytes 98312 | tf_op jit(solution)/shard_map/ppermute | solution.py:31
  39.7 1.1 %collective-permute-done.10 = bf16[128,128]{1,0:T(8,128)(2,1)S(1)} collective-permute-done((bf16[128,128]{1,0:T(8,128)(2,1)S(1)}, bf16[128,128]{1,0:T(8,128)(2,1)S(1)}, u32[]{:S(2)}, u32[]{:S(2)}) %collective-permute-start.10) | collective-permute-done | bytes 32800 | tf_op jit(solution)/shard_map/ppermute | solution.py:31
  40.8 1.3 %collective-permute-done.9 = bf16[128,128]{1,0:T(8,128)(2,1)S(1)} collective-permute-done((bf16[128,128]{1,0:T(8,128)(2,1)S(1)}, bf16[128,128]{1,0:T(8,128)(2,1)S(1)}, u32[]{:S(2)}, u32[]{:S(2)}) %collective-permute-start.9) | collective-permute-done | bytes 32800 | tf_op jit(solution)/shard_map/ppermute | solution.py:31
  42.1 0.9 %broadcast_in_dim.7 = bf16[16,128,128]{2,1,0:T(8,128)(2,1)} broadcast(bf16[128,128]{1,0:T(8,128)(2,1)S(1)} %add_convert_fusion), dimensions={1,2} | broadcast | bytes 557056 | tf_op jit(solution)/shard_map/broadcast_in_dim | solution.py:44
  43.0 7.2 %all-to-all-start = ((bf16[16,128,128]{2,1,0:T(8,128)(2,1)}), bf16[16,128,128]{2,1,0:T(8,128)(2,1)S(1)}, u32[]{:S(2)}, u32[]{:S(2)}) async-start(bf16[16,128,128]{2,1,0:T(8,128)(2,1)} %broadcast_in_dim.7), calls=%async_computation | async-start | bytes 1048576 | tf_op jit(solution)/shard_map/all_to_all | solution.py:45
  50.3 0.8 %collective-permute-start.5 = (f32[17,1024]{1,0:T(8,128)S(1)}, f32[17,1024]{1,0:T(8,128)S(1)}, u32[]{:S(2)}, u32[]{:S(2)}) collective-permute-start(f32[17,1024]{1,0:T(8,128)S(1)} %get-tuple-element.52), channel_id=1, source_target_pairs={{4,0},{9,1},{6,2},{11,3},{12,4},{1,5},{14,6},{3,7},{0,8},{13,9},{2... | collective-permute-start | bytes 208904 | tf_op jit(solution)/shard_map/ppermute | solution.py:35
  51.0 7.5 %collective-permute-start.4 = (f32[17,1024]{1,0:T(8,128)S(1)}, f32[17,1024]{1,0:T(8,128)S(1)}, u32[]{:S(2)}, u32[]{:S(2)}) collective-permute-start(f32[17,1024]{1,0:T(8,128)S(1)} %get-tuple-element.51), channel_id=1, source_target_pairs={{1,0},{3,1},{0,2},{2,3},{5,4},{7,5},{4,6},{6,7},{9,8},{11,9},{8,10... | collective-permute-start | bytes 208904 | tf_op jit(solution)/shard_map/ppermute | solution.py:35
  58.6 0.7 %all-to-all-done = bf16[16,128,128]{2,1,0:T(8,128)(2,1)S(1)} async-done(((bf16[16,128,128]{2,1,0:T(8,128)(2,1)}), bf16[16,128,128]{2,1,0:T(8,128)(2,1)S(1)}, u32[]{:S(2)}, u32[]{:S(2)}) %all-to-all-start) | async-done | bytes 524320 | tf_op jit(solution)/shard_map/all_to_all | solution.py:45
  59.4 4.0 %collective-permute-start.11 = (f32[128,128]{1,0:T(8,128)S(1)}, f32[128,128]{1,0:T(8,128)S(1)}, u32[]{:S(2)}, u32[]{:S(2)}) collective-permute-start(f32[128,128]{1,0:T(8,128)S(1)} %convert_reduce_fusion), channel_id=1, source_target_pairs={{0,1},{1,0},{2,3},{3,2},{4,5},{5,4},{6,7},{7,6},{8,9},{9,8},{10,11... | collective-permute-start | bytes 196616 | tf_op jit(solution)/shard_map/ppermute | solution.py:39
  63.4 0.7 %add_add_fusion = f32[17,1024]{1,0:T(8,128)} fusion(f32[17,1024]{1,0:T(8,128)S(1)} %collective-permute-done.5, f32[17,1024]{1,0:T(8,128)S(1)} %collective-permute-done.4, f32[40,1024]{1,0:T(8,128)S(1)} %get-tuple-element.50), kind=kLoop, calls=%fused_computation.1 | loop fusion | flops 34816 | bytes 278528 | tf_op jit(solution)/shard_map/add | solution.py:245
  64.0 0.2 collective-permute-done.11
  64.3 0.7 %broadcast_select_fusion = (f32[128,128]{1,0:T(8,128)}, f32[128,128]{1,0:T(8,128)}) fusion(f32[128,128]{1,0:T(8,128)S(1)} %convert_reduce_fusion, f32[128,128]{1,0:T(8,128)S(1)} %collective-permute-done.11, pred[]{:T(512)S(6)} %eq.3), kind=kLoop, calls=%fused_computation.8 | loop fusion | flops 32768 | bytes 262145 | tf_op jit(solution)/shard_map/jit(_where)/select_n | solution.py:244
  (17 shorter events, 0.2 us)
Async XLA Ops:
  0.6 17.1 %collective-permute-start = (bf16[1024,128]{1,0:T(8,128)(2,1)}, bf16[1024,128]{1,0:T(8,128)(2,1)S(1)}, u32[]{:S(2)}, u32[]{:S(2)}) collective-permute-start(bf16[1024,128]{1,0:T(8,128)(2,1)} %refs_1_.1), channel_id=1, source_target_pairs={{0,1},{1,3},{2,0},{3,2},{4,5},{5,7},{6,4},{7,6},{8,9},{9,11},{10,8... | collective-permute-start | bytes 786440 | tf_op jit(solution)/shard_map/ppermute | solution.py:31
  3.2 18.7 %collective-permute-start.2 = (bf16[1024,128]{1,0:T(8,128)(2,1)}, bf16[1024,128]{1,0:T(8,128)(2,1)S(1)}, u32[]{:S(2)}, u32[]{:S(2)}) collective-permute-start(bf16[1024,128]{1,0:T(8,128)(2,1)} %refs_1_.1), channel_id=1, source_target_pairs={{0,4},{1,9},{2,6},{3,11},{4,12},{5,1},{6,14},{7,3},{8,0},{9,13},{1... | collective-permute-start | bytes 786440 | tf_op jit(solution)/shard_map/ppermute | solution.py:31
  10.2 9.1 %collective-permute-start.1 = (bf16[40,1024]{1,0:T(8,128)(2,1)S(1)}, bf16[40,1024]{1,0:T(8,128)(2,1)S(1)}, u32[]{:S(2)}, u32[]{:S(2)}) collective-permute-start(bf16[40,1024]{1,0:T(8,128)(2,1)S(1)} %get-tuple-element.58.va), channel_id=1, source_target_pairs={{0,1},{1,3},{2,0},{3,2},{4,5},{5,7},{6,4},{7,6},{8,9},{9,11},{10,8... | collective-permute-start | bytes 245768 | tf_op jit(solution)/shard_map/ppermute | solution.py:31
  11.0 12.5 %collective-permute-start.3 = (bf16[40,1024]{1,0:T(8,128)(2,1)S(1)}, bf16[40,1024]{1,0:T(8,128)(2,1)S(1)}, u32[]{:S(2)}, u32[]{:S(2)}) collective-permute-start(bf16[40,1024]{1,0:T(8,128)(2,1)S(1)} %get-tuple-element.58.va), channel_id=1, source_target_pairs={{0,4},{1,9},{2,6},{3,11},{4,12},{5,1},{6,14},{7,3},{8,0},{9,13},{1... | collective-permute-start | bytes 245768 | tf_op jit(solution)/shard_map/ppermute | solution.py:31
  12.2 0.9 %copy-start = (bf16[1024,128]{1,0:T(8,128)(2,1)S(1)}, bf16[1024,128]{1,0:T(8,128)(2,1)}, u32[]{:S(2)}) copy-start(bf16[1024,128]{1,0:T(8,128)(2,1)} %refs_1_.1) | copy-start | bytes 786436
  13.2 0.8 %copy-start.2 = (bf16[128,128]{1,0:T(8,128)(2,1)S(1)}, bf16[128,128]{1,0:T(8,128)(2,1)}, u32[]{:S(2)}) copy-start(bf16[128,128]{1,0:T(8,128)(2,1)} %w_out.5) | copy-start | bytes 98308
  13.9 0.8 %copy-start.3 = (bf16[128,128]{1,0:T(8,128)(2,1)S(1)}, bf16[128,128]{1,0:T(8,128)(2,1)}, u32[]{:S(2)}) copy-start(bf16[128,128]{1,0:T(8,128)(2,1)} %w_in.1) | copy-start | bytes 98308
  19.4 4.2 %copy-start.1 = (bf16[1024,128]{1,0:T(8,128)(2,1)S(1)}, bf16[1024,128]{1,0:T(8,128)(2,1)}, u32[]{:S(2)}) copy-start(bf16[1024,128]{1,0:T(8,128)(2,1)} %refs_1_.1) | copy-start | bytes 786436
  26.3 1.9 %collective-permute-start.6 = (f32[128,128]{1,0:T(8,128)S(1)}, f32[128,128]{1,0:T(8,128)S(1)}, u32[]{:S(2)}, u32[]{:S(2)}) collective-permute-start(f32[128,128]{1,0:T(8,128)S(1)} %get-tuple-element.54), channel_id=1, source_target_pairs={{0,1},{1,0},{2,3},{3,2},{4,5},{5,4},{6,7},{7,6},{8,9},{9,8},{10,11... | collective-permute-start | bytes 196616 | tf_op jit(solution)/shard_map/ppermute | solution.py:39
  28.2 7.8 %collective-permute-start.7 = (bf16[128,128]{1,0:T(8,128)(2,1)S(1)}, bf16[128,128]{1,0:T(8,128)(2,1)S(1)}, u32[]{:S(2)}, u32[]{:S(2)}) collective-permute-start(bf16[128,128]{1,0:T(8,128)(2,1)S(1)} %fusion.1), channel_id=1, source_target_pairs={{0,8},{1,9},{2,10},{3,11},{4,12},{5,13},{6,14},{7,15},{8,0},{9,1},... | collective-permute-start | bytes 98312 | tf_op jit(solution)/shard_map/ppermute | solution.py:31
  36.1 4.8 %collective-permute-start.10 = (bf16[128,128]{1,0:T(8,128)(2,1)S(1)}, bf16[128,128]{1,0:T(8,128)(2,1)S(1)}, u32[]{:S(2)}, u32[]{:S(2)}) collective-permute-start(bf16[128,128]{1,0:T(8,128)(2,1)S(1)} %fusion), channel_id=1, source_target_pairs={{0,6},{1,7},{2,4},{3,5},{4,2},{5,3},{6,0},{7,1},{8,14},{9,15},{10,... | collective-permute-start | bytes 98312 | tf_op jit(solution)/shard_map/ppermute | solution.py:31
  36.9 3.9 %collective-permute-start.8 = (bf16[128,128]{1,0:T(8,128)(2,1)S(1)}, bf16[128,128]{1,0:T(8,128)(2,1)S(1)}, u32[]{:S(2)}, u32[]{:S(2)}) collective-permute-start(bf16[128,128]{1,0:T(8,128)(2,1)S(1)} %fusion), channel_id=1, source_target_pairs={{0,2},{1,3},{2,0},{3,1},{4,6},{5,7},{6,4},{7,5},{8,10},{9,11},{10,... | collective-permute-start | bytes 98312 | tf_op jit(solution)/shard_map/ppermute | solution.py:31
  38.3 3.8 %collective-permute-start.9 = (bf16[128,128]{1,0:T(8,128)(2,1)S(1)}, bf16[128,128]{1,0:T(8,128)(2,1)S(1)}, u32[]{:S(2)}, u32[]{:S(2)}) collective-permute-start(bf16[128,128]{1,0:T(8,128)(2,1)S(1)} %fusion), channel_id=1, source_target_pairs={{0,4},{1,5},{2,6},{3,7},{4,0},{5,1},{6,2},{7,3},{8,12},{9,13},{10,... | collective-permute-start | bytes 98312 | tf_op jit(solution)/shard_map/ppermute | solution.py:31
  43.0 16.2 %all-to-all-start = ((bf16[16,128,128]{2,1,0:T(8,128)(2,1)}), bf16[16,128,128]{2,1,0:T(8,128)(2,1)S(1)}, u32[]{:S(2)}, u32[]{:S(2)}) async-start(bf16[16,128,128]{2,1,0:T(8,128)(2,1)} %broadcast_in_dim.7), calls=%async_computation | async-start | bytes 1048576 | tf_op jit(solution)/shard_map/all_to_all | solution.py:45
  50.3 13.1 %collective-permute-start.5 = (f32[17,1024]{1,0:T(8,128)S(1)}, f32[17,1024]{1,0:T(8,128)S(1)}, u32[]{:S(2)}, u32[]{:S(2)}) collective-permute-start(f32[17,1024]{1,0:T(8,128)S(1)} %get-tuple-element.52), channel_id=1, source_target_pairs={{4,0},{9,1},{6,2},{11,3},{12,4},{1,5},{14,6},{3,7},{0,8},{13,9},{2... | collective-permute-start | bytes 208904 | tf_op jit(solution)/shard_map/ppermute | solution.py:35
  51.0 12.3 %collective-permute-start.4 = (f32[17,1024]{1,0:T(8,128)S(1)}, f32[17,1024]{1,0:T(8,128)S(1)}, u32[]{:S(2)}, u32[]{:S(2)}) collective-permute-start(f32[17,1024]{1,0:T(8,128)S(1)} %get-tuple-element.51), channel_id=1, source_target_pairs={{1,0},{3,1},{0,2},{2,3},{5,4},{7,5},{4,6},{6,7},{9,8},{11,9},{8,10... | collective-permute-start | bytes 208904 | tf_op jit(solution)/shard_map/ppermute | solution.py:35
  59.4 4.9 %collective-permute-start.11 = (f32[128,128]{1,0:T(8,128)S(1)}, f32[128,128]{1,0:T(8,128)S(1)}, u32[]{:S(2)}, u32[]{:S(2)}) collective-permute-start(f32[128,128]{1,0:T(8,128)S(1)} %convert_reduce_fusion), channel_id=1, source_target_pairs={{0,1},{1,0},{2,3},{3,2},{4,5},{5,4},{6,7},{7,6},{8,9},{9,8},{10,11... | collective-permute-start | bytes 196616 | tf_op jit(solution)/shard_map/ppermute | solution.py:39

commit v6 on v5

--- a/solution.py
+++ b/solution.py
@@ -59,6 +59,10 @@
 
 def dot_nt(a, b):
     return lax.dot_general(a, b, (((1,), (1,)), ((), ())), preferred_element_type=F32)
+
+
+def tiles_up(rows):
+    return -(-rows // 16) * 16
 
 
 def transposed(x):
@@ -110,7 +114,7 @@
         here = pl.ds(r, CHUNK)
         kernel = kernel_rows(feats[here, :], row_sq[here, :], feats_t, col_sq, feat)
         weight = (dot(av_t[here, :], va[...]) * kernel).astype(BF16)
-        prod[:, here] = dot_nt(va[...], kernel.astype(BF16))
+        prod[:, here] = dot_nt(va[: prod.shape[0], :], kernel.astype(BF16))
         sums = dot_nt(feats1_t[...], weight)
         grad[:, here] = grad_of(sums, feats_t[:, r : r + CHUNK], feat)
 
@@ -126,7 +130,7 @@
         ).astype(BF16)
     for r in range(0, n, CHUNK):
         here = pl.ds(r, CHUNK)
-        prod_c[:, here] = dot(va[...], kernel[:, here])[: prod_c.shape[0]]
+        prod_c[:, here] = dot(va[: tiles_up(prod_c.shape[0]), :], kernel[:, here])[: prod_c.shape[0]]
 
 
 def pair_kernel(
@@ -143,7 +147,7 @@
         here = pl.ds(r, CHUNK)
         pairing = dot(av_t[here, :], va_c[...])
         weight[here, :] = (pairing * kernel[here, :].astype(F32)).astype(BF16)
-        prod_new[:, here] = prod[:, here] + dot_nt(va_c[...], kernel[here, :])
+        prod_new[:, here] = prod[:, here] + dot_nt(va_c[: prod.shape[0], :], kernel[here, :])
         sums = dot_nt(feats1_c[...], weight[here, :])
         total = grad[:, here] + grad_of(sums, feats1_t[:feat, here], feat)
         if last:
@@ -187,8 +191,10 @@
     va = jnp.concatenate([vectors, adjoint, blank], axis=0)
     av = jnp.concatenate([adjoint, vectors, blank], axis=0)
     k = va.shape[0]
-    far_points, far_va = send(points, far_target), send(va, far_target)
-    near_points, near_va = send(points, near_target), send(va, near_target)
+    near_points = send(points, near_target)
+    va, later_points = lax.optimization_barrier((va, points))
+    near_va = send(va, near_target)
+    far_points, far_va = send(later_points, far_target), send(va, far_target)
 
     w_in_t, w_out_t, feats, feats1_t, hid_t, av_t, row_sq, prod, grad = call(
         own_kernel,
@@ -201,7 +207,7 @@
             ((hid, n), BF16),
             ((n, k), BF16),
             ((n, 1), F32),
-            ((k, n), F32),
+            ((tiles_up(nvec), n), F32),
             ((feat, n), F32),
         ),
     )
@@ -218,7 +224,7 @@
     prod, grad, g_in, g_out = call(
         functools.partial(pair_kernel, False),
         (near_points, near_va, hid_c, feats1_c, kernel, w_output, feats1_t, av_t, prod, grad),
-        (((k, n), F32), ((feat, n), F32), ((hid, din), F32), ((hid, feat), F32)),
+        (((tiles_up(nvec), n), F32), ((feat, n), F32), ((hid, din), F32), ((hid, feat), F32)),
         scratch,
     )
     second = lax.axis_index("c").astype(jnp.int32).reshape(1)
@@ -229,7 +235,7 @@
         functools.partial(pair_kernel, True),
         (late_points, far_va, hid_c, feats1_c, kernel, w_output, feats1_t, av_t, prod, grad)
         + (hid_t, points, second, g_in, g_out),
-        (((k, n), F32), ((hid, feat), F32), ((hid, feat), F32)),
+        (((tiles_up(nvec), n), F32), ((hid, feat), F32), ((hid, feat), F32)),
         scratch,
         smem=12,
     )

time: 65.3 us -> 65.1 us (level)
    all_to_all x1, starting transfers between devices: 7.23 us -> 6.45 us  [sum_over(): got = lax.all_to_all(sent, axes, 0, 0)]
    ppermute x2, starting transfers between devices: 8.3 us -> 9.03 us  [send_back(): lax.ppermute(x, ALL, [(target(i), i) for i in range(lax.axis_size(ALL))])]
    all_to_all x1, waiting for transfers between devices: 0.71 us -> 0.01 us  [sum_over(): got = lax.all_to_all(sent, axes, 0, 0)]
where the time goes in v6:
time: 65.1 us; the launch traced here: 64.7 us
  starting transfers between devices  40.8 us (63%)
  Pallas kernels  11.5 us (18%)
  waiting for transfers between devices  5.79 us (9%)
  local copies, waits for them, and re-layouts  3.47 us (5%)
  other arithmetic  2.43 us (4%)
  between operations  0.73 us (1%)
    ppermute x8, starting transfers between devices, send(): lax.ppermute(x, ALL, [(i, target(i)) for i in range(lax.axis_size(ALL))])  20.9 us
    pallas_call x5, Pallas kernels, call(): pl.pallas_call(body, out_shape=[jax.ShapeDtypeStruct(s, d) for s, d in ou...  11.5 us
    ppermute x2, starting transfers between devices, send_back(): lax.ppermute(x, ALL, [(target(i), i) for i in range(lax.axis_size(ALL))])  9.03 us
    all_to_all x1, starting transfers between devices, sum_over(): got = lax.all_to_all(sent, axes, 0, 0)  6.45 us
    ppermute x2, starting transfers between devices, swap_cores(): return lax.ppermute(x, 'c', [(0, 1), (1, 0)])  4.42 us
    ppermute x8, waiting for transfers between devices, send(): lax.ppermute(x, ALL, [(i, target(i)) for i in range(lax.axis_size(ALL))])  4.31 us
    unnamed x8, local copies, waits for them, and re-layouts  2.48 us
    ppermute x2, waiting for transfers between devices, swap_cores(): return lax.ppermute(x, 'c', [(0, 1), (1, 0)])  1.48 us
  transfers between devices with their start and end apart: 13, of which 6 were waited for; matrix products, arithmetic and copies ran while one was open for 3% of the time, Pallas kernels for 14%

profile of v6, /device:TPU:1, one launch (start us, length us, event | category | flops | bytes accessed | tf_op | source)
XLA Modules:
  0.0 64.7 jit_solution(11688136909145528307)
XLA Ops:
  0.6 2.6 %collective-permute-start = (bf16[1024,128]{1,0:T(8,128)(2,1)}, bf16[1024,128]{1,0:T(8,128)(2,1)S(1)}, u32[]{:S(2)}, u32[]{:S(2)}) collective-permute-start(bf16[1024,128]{1,0:T(8,128)(2,1)} %refs_1_.1), channel_id=1, source_target_pairs={{0,1},{1,3},{2,0},{3,2},{4,5},{5,7},{6,4},{7,6},{8,9},{9,11},{10,8... | collective-permute-start | bytes 786440 | tf_op jit(solution)/shard_map/ppermute | solution.py:31
  3.2 0.1 pad.5.clone
  3.3 1.0 %maximum_maximum_fusion.1 = (bf16[40,1024]{1,0:T(8,128)(2,1)S(1)}, bf16[40,1024]{1,0:T(8,128)(2,1)S(1)}) fusion(bf16[17,1024]{1,0:T(8,128)(2,1)} %param.8, bf16[17,1024]{1,0:T(8,128)(2,1)} %param.9, bf16[40]{0:T(256)(128)(2,1)S(1)} %pad.5.clone), kind=kLoop, calls=%fused_computation.3 | loop fusion | flops 450560 | bytes 233552 | tf_op jit(solution)/shard_map/concatenate | solution.py:192
  4.2 6.1 %collective-permute-start.2 = (bf16[1024,128]{1,0:T(8,128)(2,1)}, bf16[1024,128]{1,0:T(8,128)(2,1)S(1)}, u32[]{:S(2)}, u32[]{:S(2)}) collective-permute-start(bf16[1024,128]{1,0:T(8,128)(2,1)} %refs_1_.1), channel_id=1, source_target_pairs={{0,4},{1,9},{2,6},{3,11},{4,12},{5,1},{6,14},{7,3},{8,0},{9,13},{1... | collective-permute-start | bytes 786440 | tf_op jit(solution)/shard_map/ppermute | solution.py:31
  10.3 0.7 %collective-permute-start.1 = (bf16[40,1024]{1,0:T(8,128)(2,1)S(1)}, bf16[40,1024]{1,0:T(8,128)(2,1)S(1)}, u32[]{:S(2)}, u32[]{:S(2)}) collective-permute-start(bf16[40,1024]{1,0:T(8,128)(2,1)S(1)} %get-tuple-element.31.va), channel_id=1, source_target_pairs={{0,1},{1,3},{2,0},{3,2},{4,5},{5,7},{6,4},{7,6},{8,9},{9,11},{10,8... | collective-permute-start | bytes 245768 | tf_op jit(solution)/shard_map/ppermute | solution.py:31
  11.0 1.2 %collective-permute-start.3 = (bf16[40,1024]{1,0:T(8,128)(2,1)S(1)}, bf16[40,1024]{1,0:T(8,128)(2,1)S(1)}, u32[]{:S(2)}, u32[]{:S(2)}) collective-permute-start(bf16[40,1024]{1,0:T(8,128)(2,1)S(1)} %get-tuple-element.31.va), channel_id=1, source_target_pairs={{0,4},{1,9},{2,6},{3,11},{4,12},{5,1},{6,14},{7,3},{8,0},{9,13},{1... | collective-permute-start | bytes 245768 | tf_op jit(solution)/shard_map/ppermute | solution.py:31
  12.2 0.9 %copy-done = bf16[1024,128]{1,0:T(8,128)(2,1)S(1)} copy-done((bf16[1024,128]{1,0:T(8,128)(2,1)S(1)}, bf16[1024,128]{1,0:T(8,128)(2,1)}, u32[]{:S(2)}) %copy-start) | copy-done | bytes 262168
  13.1 0.8 %copy-done.2 = bf16[128,128]{1,0:T(8,128)(2,1)S(1)} copy-done((bf16[128,128]{1,0:T(8,128)(2,1)S(1)}, bf16[128,128]{1,0:T(8,128)(2,1)}, u32[]{:S(2)}) %copy-start.2) | copy-done | bytes 32792
  13.9 0.8 %copy-done.3 = bf16[128,128]{1,0:T(8,128)(2,1)S(1)} copy-done((bf16[128,128]{1,0:T(8,128)(2,1)S(1)}, bf16[128,128]{1,0:T(8,128)(2,1)}, u32[]{:S(2)}) %copy-start.3) | copy-done | bytes 32792
  14.7 3.1 %shard_map.76 = (bf16[128,128]{1,0:T(8,128)(2,1)S(1)}, bf16[128,128]{1,0:T(8,128)(2,1)S(1)}, bf16[1024,128]{1,0:T(8,128)(2,1)S(1)}, bf16[144,1024]{1,0:T(8,128)(...) custom-call(bf16[1024,128]{1,0:T(8,128)(2,1)S(1)} %copy-done, ...), custom_call_target="tpu_custom_call" | custom-call | tf_op jit(solution)/shard_map/pallas_call | solution.py:177
  17.7 1.6 %shard_map.77 = (bf16[128,1024]{1,0:T(8,128)(2,1)S(1)}, bf16[144,1024]{1,0:T(8,128)(2,1)S(1)}, bf16[1024,1024]{1,0:T(8,128)(2,1)S(1)}, f32[17,1024]{1,0:T(8,128)S(1)}) custom-call(bf16[1024,128]{1,0:T(8,128)(2,1)S(1)} %collective-permute-done.pts_c, bf16[128,128]{1,0:T(8,128)(2,1)S(1)} %get-tuple-element.32.w_in_t, ...), custom_call_target="tpu_custom_call" | custom-call | tf_op jit(solution)/shard_map/pallas_call | solution.py:177
  19.4 2.5 %shard_map.78 = (f32[32,1024]{1,0:T(8,128)S(1)}, f32[128,1024]{1,0:T(8,128)S(1)}, f32[128,128]{1,0:T(8,128)S(1)}, f32[128,128]{1,0:T(8,128)S(1)}) custom-call(bf16[1024,128]{1,0:T(8,128)(2,1)S(1)} %collective-permute-done.pts_c, bf16[40,1024]{1,0:T(8,128)(2,1)S(1)} %collective-permute-done.1.va_c, bf16[128,1024]{1,0:T(8,128)(2,1)S(1)} %get-tuple-element.36.hid_c, ...), custom_call_target="tpu_custom_call" | custom-call | tf_op jit(solution)/shard_map/pallas_call | solution.py:177
  21.8 1.6 %shard_map.79 = (bf16[128,1024]{1,0:T(8,128)(2,1)S(1)}, bf16[144,1024]{1,0:T(8,128)(2,1)S(1)}, bf16[1024,1024]{1,0:T(8,128)(2,1)S(1)}, f32[17,1024]{1,0:T(8,128)S(1)}) custom-call(bf16[1024,128]{1,0:T(8,128)(2,1)S(1)} %collective-permute-done.2.pts_c, bf16[128,128]{1,0:T(8,128)(2,1)S(1)} %get-tuple-element.32.w_in_t, ...), custom_call_target="tpu_custom_call" | custom-call | tf_op jit(solution)/shard_map/pallas_call | solution.py:177
  23.5 2.7 %shard_map.80 = (f32[32,1024]{1,0:T(8,128)S(1)}, f32[128,128]{1,0:T(8,128)S(1)}, f32[128,128]{1,0:T(8,128)S(1)}) custom-call(bf16[1024,128]{1,0:T(8,128)(2,1)S(1)} %collective-permute-done.2.pts_c, bf16[40,1024]{1,0:T(8,128)(2,1)S(1)} %collective-permute-done.3.va_c, bf16[128,1024]{1,0:T(8,128)(2,1)S(1)} %get-tuple-element.46.hid_c, ...), custom_call_target="tpu_custom_call" | custom-call | tf_op jit(solution)/shard_map/pallas_call | solution.py:177
  26.2 0.1 collective-permute-start.6
  26.3 1.2 %collective-permute-done.6 = f32[128,128]{1,0:T(8,128)S(1)} collective-permute-done((f32[128,128]{1,0:T(8,128)S(1)}, f32[128,128]{1,0:T(8,128)S(1)}, u32[]{:S(2)}, u32[]{:S(2)}) %collective-permute-start.6) | collective-permute-done | bytes 65568 | tf_op jit(solution)/shard_map/ppermute | solution.py:39
  27.6 6.8 %collective-permute-start.7 = (bf16[128,128]{1,0:T(8,128)(2,1)S(1)}, bf16[128,128]{1,0:T(8,128)(2,1)S(1)}, u32[]{:S(2)}, u32[]{:S(2)}) collective-permute-start(bf16[128,128]{1,0:T(8,128)(2,1)S(1)} %fusion.1), channel_id=1, source_target_pairs={{0,8},{1,9},{2,10},{3,11},{4,12},{5,13},{6,14},{7,15},{8,0},{9,1},... | collective-permute-start | bytes 98312 | tf_op jit(solution)/shard_map/ppermute | solution.py:31
  34.3 1.3 %collective-permute-done.7 = bf16[128,128]{1,0:T(8,128)(2,1)S(1)} collective-permute-done((bf16[128,128]{1,0:T(8,128)(2,1)S(1)}, bf16[128,128]{1,0:T(8,128)(2,1)S(1)}, u32[]{:S(2)}, u32[]{:S(2)}) %collective-permute-start.7) | collective-permute-done | bytes 32800 | tf_op jit(solution)/shard_map/ppermute | solution.py:31
  35.7 2.4 %collective-permute-start.10 = (bf16[128,128]{1,0:T(8,128)(2,1)S(1)}, bf16[128,128]{1,0:T(8,128)(2,1)S(1)}, u32[]{:S(2)}, u32[]{:S(2)}) collective-permute-start(bf16[128,128]{1,0:T(8,128)(2,1)S(1)} %fusion), channel_id=1, source_target_pairs={{0,6},{1,7},{2,4},{3,5},{4,2},{5,3},{6,0},{7,1},{8,14},{9,15},{10,... | collective-permute-start | bytes 98312 | tf_op jit(solution)/shard_map/ppermute | solution.py:31
  38.1 1.2 %collective-permute-start.9 = (bf16[128,128]{1,0:T(8,128)(2,1)S(1)}, bf16[128,128]{1,0:T(8,128)(2,1)S(1)}, u32[]{:S(2)}, u32[]{:S(2)}) collective-permute-start(bf16[128,128]{1,0:T(8,128)(2,1)S(1)} %fusion), channel_id=1, source_target_pairs={{0,4},{1,5},{2,6},{3,7},{4,0},{5,1},{6,2},{7,3},{8,12},{9,13},{10,... | collective-permute-start | bytes 98312 | tf_op jit(solution)/shard_map/ppermute | solution.py:31
  39.3 1.0 %collective-permute-done.10 = bf16[128,128]{1,0:T(8,128)(2,1)S(1)} collective-permute-done((bf16[128,128]{1,0:T(8,128)(2,1)S(1)}, bf16[128,128]{1,0:T(8,128)(2,1)S(1)}, u32[]{:S(2)}, u32[]{:S(2)}) %collective-permute-start.10) | collective-permute-done | bytes 32800 | tf_op jit(solution)/shard_map/ppermute | solution.py:31
  40.3 0.5 collective-permute-done.8
  40.9 1.4 %collective-permute-done.9 = bf16[128,128]{1,0:T(8,128)(2,1)S(1)} collective-permute-done((bf16[128,128]{1,0:T(8,128)(2,1)S(1)}, bf16[128,128]{1,0:T(8,128)(2,1)S(1)}, u32[]{:S(2)}, u32[]{:S(2)}) %collective-permute-start.9) | collective-permute-done | bytes 32800 | tf_op jit(solution)/shard_map/ppermute | solution.py:31
  42.3 0.9 %broadcast_in_dim.7 = bf16[16,128,128]{2,1,0:T(8,128)(2,1)} broadcast(bf16[128,128]{1,0:T(8,128)(2,1)S(1)} %add_convert_fusion), dimensions={1,2} | broadcast | bytes 557056 | tf_op jit(solution)/shard_map/broadcast_in_dim | solution.py:44
  43.2 6.4 %all-to-all-start = ((bf16[16,128,128]{2,1,0:T(8,128)(2,1)}), bf16[16,128,128]{2,1,0:T(8,128)(2,1)S(1)}, u32[]{:S(2)}, u32[]{:S(2)}) async-start(bf16[16,128,128]{2,1,0:T(8,128)(2,1)} %broadcast_in_dim.7), calls=%async_computation | async-start | bytes 1048576 | tf_op jit(solution)/shard_map/all_to_all | solution.py:45
  49.7 1.1 %collective-permute-start.5 = (f32[17,1024]{1,0:T(8,128)S(1)}, f32[17,1024]{1,0:T(8,128)S(1)}, u32[]{:S(2)}, u32[]{:S(2)}) collective-permute-start(f32[17,1024]{1,0:T(8,128)S(1)} %get-tuple-element.56), channel_id=1, source_target_pairs={{4,0},{9,1},{6,2},{11,3},{12,4},{1,5},{14,6},{3,7},{0,8},{13,9},{2... | collective-permute-start | bytes 208904 | tf_op jit(solution)/shard_map/ppermute | solution.py:35
  50.8 7.9 %collective-permute-start.4 = (f32[17,1024]{1,0:T(8,128)S(1)}, f32[17,1024]{1,0:T(8,128)S(1)}, u32[]{:S(2)}, u32[]{:S(2)}) collective-permute-start(f32[17,1024]{1,0:T(8,128)S(1)} %get-tuple-element.55), channel_id=1, source_target_pairs={{1,0},{3,1},{0,2},{2,3},{5,4},{7,5},{4,6},{6,7},{9,8},{11,9},{8,10... | collective-permute-start | bytes 208904 | tf_op jit(solution)/shard_map/ppermute | solution.py:35
  58.7 0.1 convert_reduce_fusion
  58.8 4.3 %collective-permute-start.11 = (f32[128,128]{1,0:T(8,128)S(1)}, f32[128,128]{1,0:T(8,128)S(1)}, u32[]{:S(2)}, u32[]{:S(2)}) collective-permute-start(f32[128,128]{1,0:T(8,128)S(1)} %convert_reduce_fusion), channel_id=1, source_target_pairs={{0,1},{1,0},{2,3},{3,2},{4,5},{5,4},{6,7},{7,6},{8,9},{9,8},{10,11... | collective-permute-start | bytes 196616 | tf_op jit(solution)/shard_map/ppermute | solution.py:39
  63.1 0.7 %add_add_fusion = f32[17,1024]{1,0:T(8,128)} fusion(f32[17,1024]{1,0:T(8,128)S(1)} %collective-permute-done.5, f32[17,1024]{1,0:T(8,128)S(1)} %collective-permute-done.4, f32[32,1024]{1,0:T(8,128)S(1)} %get-tuple-element.54), kind=kLoop, calls=%fused_computation.1 | loop fusion | flops 34816 | bytes 278528 | tf_op jit(solution)/shard_map/add | solution.py:251
  63.8 0.2 collective-permute-done.11
  64.0 0.7 %broadcast_select_fusion = (f32[128,128]{1,0:T(8,128)}, f32[128,128]{1,0:T(8,128)}) fusion(f32[128,128]{1,0:T(8,128)S(1)} %convert_reduce_fusion, f32[128,128]{1,0:T(8,128)S(1)} %collective-permute-done.11, pred[]{:T(512)S(6)} %eq.3), kind=kLoop, calls=%fused_computation.8 | loop fusion | flops 32768 | bytes 262145 | tf_op jit(solution)/shard_map/jit(_where)/select_n | solution.py:250
  (17 shorter events, 0.1 us)
Async XLA Ops:
  0.6 17.1 %collective-permute-start = (bf16[1024,128]{1,0:T(8,128)(2,1)}, bf16[1024,128]{1,0:T(8,128)(2,1)S(1)}, u32[]{:S(2)}, u32[]{:S(2)}) collective-permute-start(bf16[1024,128]{1,0:T(8,128)(2,1)} %refs_1_.1), channel_id=1, source_target_pairs={{0,1},{1,3},{2,0},{3,2},{4,5},{5,7},{6,4},{7,6},{8,9},{9,11},{10,8... | collective-permute-start | bytes 786440 | tf_op jit(solution)/shard_map/ppermute | solution.py:31
  4.2 17.6 %collective-permute-start.2 = (bf16[1024,128]{1,0:T(8,128)(2,1)}, bf16[1024,128]{1,0:T(8,128)(2,1)S(1)}, u32[]{:S(2)}, u32[]{:S(2)}) collective-permute-start(bf16[1024,128]{1,0:T(8,128)(2,1)} %refs_1_.1), channel_id=1, source_target_pairs={{0,4},{1,9},{2,6},{3,11},{4,12},{5,1},{6,14},{7,3},{8,0},{9,13},{1... | collective-permute-start | bytes 786440 | tf_op jit(solution)/shard_map/ppermute | solution.py:31
  10.3 9.0 %collective-permute-start.1 = (bf16[40,1024]{1,0:T(8,128)(2,1)S(1)}, bf16[40,1024]{1,0:T(8,128)(2,1)S(1)}, u32[]{:S(2)}, u32[]{:S(2)}) collective-permute-start(bf16[40,1024]{1,0:T(8,128)(2,1)S(1)} %get-tuple-element.31.va), channel_id=1, source_target_pairs={{0,1},{1,3},{2,0},{3,2},{4,5},{5,7},{6,4},{7,6},{8,9},{9,11},{10,8... | collective-permute-start | bytes 245768 | tf_op jit(solution)/shard_map/ppermute | solution.py:31
  11.0 12.5 %collective-permute-start.3 = (bf16[40,1024]{1,0:T(8,128)(2,1)S(1)}, bf16[40,1024]{1,0:T(8,128)(2,1)S(1)}, u32[]{:S(2)}, u32[]{:S(2)}) collective-permute-start(bf16[40,1024]{1,0:T(8,128)(2,1)S(1)} %get-tuple-element.31.va), channel_id=1, source_target_pairs={{0,4},{1,9},{2,6},{3,11},{4,12},{5,1},{6,14},{7,3},{8,0},{9,13},{1... | collective-permute-start | bytes 245768 | tf_op jit(solution)/shard_map/ppermute | solution.py:31
  12.2 0.9 %copy-start = (bf16[1024,128]{1,0:T(8,128)(2,1)S(1)}, bf16[1024,128]{1,0:T(8,128)(2,1)}, u32[]{:S(2)}) copy-start(bf16[1024,128]{1,0:T(8,128)(2,1)} %refs_1_.1) | copy-start | bytes 786436
  13.1 0.8 %copy-start.2 = (bf16[128,128]{1,0:T(8,128)(2,1)S(1)}, bf16[128,128]{1,0:T(8,128)(2,1)}, u32[]{:S(2)}) copy-start(bf16[128,128]{1,0:T(8,128)(2,1)} %w_out.5) | copy-start | bytes 98308
  13.9 0.8 %copy-start.3 = (bf16[128,128]{1,0:T(8,128)(2,1)S(1)}, bf16[128,128]{1,0:T(8,128)(2,1)}, u32[]{:S(2)}) copy-start(bf16[128,128]{1,0:T(8,128)(2,1)} %w_in.1) | copy-start | bytes 98308
  19.3 4.1 %copy-start.1 = (bf16[1024,128]{1,0:T(8,128)(2,1)S(1)}, bf16[1024,128]{1,0:T(8,128)(2,1)}, u32[]{:S(2)}) copy-start(bf16[1024,128]{1,0:T(8,128)(2,1)} %refs_1_.1) | copy-start | bytes 786436
  26.2 1.3 %collective-permute-start.6 = (f32[128,128]{1,0:T(8,128)S(1)}, f32[128,128]{1,0:T(8,128)S(1)}, u32[]{:S(2)}, u32[]{:S(2)}) collective-permute-start(f32[128,128]{1,0:T(8,128)S(1)} %get-tuple-element.58), channel_id=1, source_target_pairs={{0,1},{1,0},{2,3},{3,2},{4,5},{5,4},{6,7},{7,6},{8,9},{9,8},{10,11... | collective-permute-start | bytes 196616 | tf_op jit(solution)/shard_map/ppermute | solution.py:39
  27.6 8.1 %collective-permute-start.7 = (bf16[128,128]{1,0:T(8,128)(2,1)S(1)}, bf16[128,128]{1,0:T(8,128)(2,1)S(1)}, u32[]{:S(2)}, u32[]{:S(2)}) collective-permute-start(bf16[128,128]{1,0:T(8,128)(2,1)S(1)} %fusion.1), channel_id=1, source_target_pairs={{0,8},{1,9},{2,10},{3,11},{4,12},{5,13},{6,14},{7,15},{8,0},{9,1},... | collective-permute-start | bytes 98312 | tf_op jit(solution)/shard_map/ppermute | solution.py:31
  35.7 4.7 %collective-permute-start.10 = (bf16[128,128]{1,0:T(8,128)(2,1)S(1)}, bf16[128,128]{1,0:T(8,128)(2,1)S(1)}, u32[]{:S(2)}, u32[]{:S(2)}) collective-permute-start(bf16[128,128]{1,0:T(8,128)(2,1)S(1)} %fusion), channel_id=1, source_target_pairs={{0,6},{1,7},{2,4},{3,5},{4,2},{5,3},{6,0},{7,1},{8,14},{9,15},{10,... | collective-permute-start | bytes 98312 | tf_op jit(solution)/shard_map/ppermute | solution.py:31
  38.1 2.8 %collective-permute-start.8 = (bf16[128,128]{1,0:T(8,128)(2,1)S(1)}, bf16[128,128]{1,0:T(8,128)(2,1)S(1)}, u32[]{:S(2)}, u32[]{:S(2)}) collective-permute-start(bf16[128,128]{1,0:T(8,128)(2,1)S(1)} %fusion), channel_id=1, source_target_pairs={{0,2},{1,3},{2,0},{3,1},{4,6},{5,7},{6,4},{7,5},{8,10},{9,11},{10,... | collective-permute-start | bytes 98312 | tf_op jit(solution)/shard_map/ppermute | solution.py:31
  38.1 4.2 %collective-permute-start.9 = (bf16[128,128]{1,0:T(8,128)(2,1)S(1)}, bf16[128,128]{1,0:T(8,128)(2,1)S(1)}, u32[]{:S(2)}, u32[]{:S(2)}) collective-permute-start(bf16[128,128]{1,0:T(8,128)(2,1)S(1)} %fusion), channel_id=1, source_target_pairs={{0,4},{1,5},{2,6},{3,7},{4,0},{5,1},{6,2},{7,3},{8,12},{9,13},{10,... | collective-permute-start | bytes 98312 | tf_op jit(solution)/shard_map/ppermute | solution.py:31
  43.2 15.5 %all-to-all-start = ((bf16[16,128,128]{2,1,0:T(8,128)(2,1)}), bf16[16,128,128]{2,1,0:T(8,128)(2,1)S(1)}, u32[]{:S(2)}, u32[]{:S(2)}) async-start(bf16[16,128,128]{2,1,0:T(8,128)(2,1)} %broadcast_in_dim.7), calls=%async_computation | async-start | bytes 1048576 | tf_op jit(solution)/shard_map/all_to_all | solution.py:45
  49.7 13.4 %collective-permute-start.5 = (f32[17,1024]{1,0:T(8,128)S(1)}, f32[17,1024]{1,0:T(8,128)S(1)}, u32[]{:S(2)}, u32[]{:S(2)}) collective-permute-start(f32[17,1024]{1,0:T(8,128)S(1)} %get-tuple-element.56), channel_id=1, source_target_pairs={{4,0},{9,1},{6,2},{11,3},{12,4},{1,5},{14,6},{3,7},{0,8},{13,9},{2... | collective-permute-start | bytes 208904 | tf_op jit(solution)/shard_map/ppermute | solution.py:35
  50.8 12.4 %collective-permute-start.4 = (f32[17,1024]{1,0:T(8,128)S(1)}, f32[17,1024]{1,0:T(8,128)S(1)}, u32[]{:S(2)}, u32[]{:S(2)}) collective-permute-start(f32[17,1024]{1,0:T(8,128)S(1)} %get-tuple-element.55), channel_id=1, source_target_pairs={{1,0},{3,1},{0,2},{2,3},{5,4},{7,5},{4,6},{6,7},{9,8},{11,9},{8,10... | collective-permute-start | bytes 208904 | tf_op jit(solution)/shard_map/ppermute | solution.py:35
  58.8 5.2 %collective-permute-start.11 = (f32[128,128]{1,0:T(8,128)S(1)}, f32[128,128]{1,0:T(8,128)S(1)}, u32[]{:S(2)}, u32[]{:S(2)}) collective-permute-start(f32[128,128]{1,0:T(8,128)S(1)} %convert_reduce_fusion), channel_id=1, source_target_pairs={{0,1},{1,0},{2,3},{3,2},{4,5},{5,4},{6,7},{7,6},{8,9},{9,8},{10,11... | collective-permute-start | bytes 196616 | tf_op jit(solution)/shard_map/ppermute | solution.py:39
